TPU v7x, 256 devices: a whole 4x4x8 slice. The times are simulated.
256 devices in a mesh: tm: 64 (over x, y, z_lo), rows: 4 (over z_hi, core).
Axes of the slice: x: 4, y: 4, z: 8 (z_hi: 2, z_lo: 4; z = z_hi * 4 + z_lo), core: 2. Of those that a mesh axis runs over, the one named last changes fastest.
Arguments:
- band_blocks: bfloat16 [64, 3, 2048, 256], P('tm', None, 'rows'), may hold values from -0.21875 to 0.21875
- site_mask: int32 [64, 2048], P('tm', 'rows'), may hold values 0 or 1
- observed: float32 [64, 2048], P('tm', 'rows'), may hold values from -6 to 6
- band_offsets: int32 [64, 3], P('tm'), may hold values from -2 to 2, as said below
- site_gain: float32 [2048], P('rows'), may hold values from 0.2 to 0.9
Outputs:
- composed_matrix: bfloat16 [64, 2048, 2048], P('tm', 'rows')
- composed_offset: bfloat16 [64, 2048], P('tm', 'rows')
Inputs may be any that keep to these rules, and one draw needn't show every extreme that they name: `band_offsets`: the 3 offsets of one step are distinct.
All inputs are finite; a program needn't handle non-finite values. No bound on the sum of `site_mask` on one device may be relied on, other than what follows from the above.
Results may differ from a plain program's by a relative error of at most 0.0062.
Values may be sent and summed in bfloat16 or wider, within the bound.
No kernel may reach another device: no remote copies, remote signals or barrier semaphores. Data moves between devices by JAX's collectives and lax.ppermute only.
A program may use at most 64 MiB of HBM per device.

v0:
```python
import jax
import jax.numpy as jnp
from jax import lax
from jax.sharding import PartitionSpec as P


def passed_along(block, axis, distance):
    devices = range(lax.axis_size(axis))
    route = [(i - distance, i) for i in devices if i - distance in devices]
    return lax.ppermute(block, axis, route)


def placement_table(offsets, block_count):
    starts = jnp.arange(block_count, dtype=jnp.int32)
    target = (starts[None, :] + offsets[:, None]) % block_count
    columns = jnp.arange(block_count, dtype=jnp.int32)
    return (columns[None, None, :] == target[:, :, None]).astype(jnp.float32)


def place_rows(scaled, table, first_block):
    band_count, row_count, block_size = scaled.shape
    row_blocks = row_count // block_size
    block_count = table.shape[2]
    chosen = lax.dynamic_slice_in_dim(table, first_block, row_blocks, 1)
    blocks = scaled.astype(jnp.float32).reshape(band_count, row_blocks, block_size, block_size)
    dense = jnp.einsum("jrc,jrib->ricb", chosen, blocks)
    return dense.reshape(row_count, block_count * block_size).astype(jnp.bfloat16)


def combine_whole(own_matrix, own_offset, earlier_matrix, earlier_offset, distance):
    product = jnp.dot(own_matrix, earlier_matrix, preferred_element_type=jnp.float32)
    vector = jnp.dot(
        own_matrix, earlier_offset, preferred_element_type=jnp.float32
    ) + own_offset.astype(jnp.float32)
    return finish(own_matrix, own_offset, product, vector, distance)


def finish(own_matrix, own_offset, product, vector, distance):
    keep = lax.axis_index("tm") >= distance
    new_matrix = jnp.where(keep, product, own_matrix.astype(jnp.float32)).astype(jnp.bfloat16)
    new_vector = jnp.where(keep, vector, own_offset.astype(jnp.float32)).astype(jnp.bfloat16)
    return (new_matrix, new_vector)


def advance(own_matrix, own_offset, distance):
    whole_matrix, whole_offset = (
        lax.all_gather(own_matrix, "rows", axis=0, tiled=True),
        lax.all_gather(own_offset, "rows", axis=0, tiled=True),
    )
    earlier_matrix, earlier_offset = passed_along((whole_matrix, whole_offset), "tm", distance)
    return combine_whole(own_matrix, own_offset, earlier_matrix, earlier_offset, distance)


def per_device(band_blocks, site_mask, observed, band_offsets, site_gain):
    local_rows = band_blocks.shape[2]
    block_size = band_blocks.shape[3]
    state_size = local_rows * lax.axis_size("rows")
    block_count = state_size // block_size
    first_block = lax.axis_index("rows") * (local_rows // block_size)
    observed_flag = site_mask[0].astype(jnp.float32)
    factor = 1.0 - site_gain * observed_flag
    scaled = (factor[None, :, None] * band_blocks[0].astype(jnp.float32)).astype(jnp.bfloat16)
    table = placement_table(band_offsets[0], block_count)
    own_matrix = place_rows(scaled, table, first_block)
    own_offset = (site_gain * observed_flag * observed[0]).astype(jnp.bfloat16)
    level_matrix, level_offset = advance(own_matrix, own_offset, 1)
    composed_matrix, composed_offset = advance(level_matrix, level_offset, 2)
    return (composed_matrix[None], composed_offset[None])


def solution(mesh):
    in_specs = (
        P("tm", None, "rows", None),
        P("tm", "rows"),
        P("tm", "rows"),
        P("tm", None),
        P("rows"),
    )
    out_specs = (P("tm", "rows", None), P("tm", "rows"))
    return jax.shard_map(
        per_device, mesh=mesh, in_specs=in_specs, out_specs=out_specs, check_vma=False
    )
```

profile of v0, /device:TPU:1, one launch (start us, length us, event | category | flops | bytes accessed | tf_op | source)
XLA Modules:
  0.0 833.7 jit_solution(15048005094043865752)
XLA Ops:
  7.2 0.0 all-gather.5.cloned.1.call-start
  7.2 0.7 add_select_fusion
  7.9 0.7 convert_element_type.57
  8.6 0.7 multiply_convert_fusion
  9.3 1.3 convert.1
  10.6 1.9 convolution_convert_fusion
  12.5 2.0 copy.11
  14.5 0.0 copy-start
  14.5 0.0 all-gather.5.cloned.1.call-update
  14.6 0.0 all-gather.7.cloned.1.call-start
  14.6 117.9 %all-gather.5.cloned.1.call-done = bf16[2048,2048]{1,0:T(8,128)(2,1)} async-done(((bf16[512,2048]{1,0:T(8,128)(2,1)}), bf16[2048,2048]{1,0:T(8,128)(2,1)}) %all-gather.5.cloned.1.call-update) | async-done | bytes 8388624 | tf_op jit(solution)/shard_map/all_gather | solution.py:47
  132.5 4.5 collective-permute-start
  137.0 176.7 %collective-permute-done = bf16[2048,2048]{1,0:T(8,128)(2,1)} collective-permute-done((bf16[2048,2048]{1,0:T(8,128)(2,1)}, bf16[2048,2048]{1,0:T(8,128)(2,1)}, u32[]{:S(2)}, u32[]{:S(2)}) %collective-permute-start) | collective-permute-done | bytes 8388640 | tf_op jit(solution)/shard_map/ppermute | solution.py:10
  313.7 0.0 copy-done
  313.7 9.1 %select_convert_fusion.1 = bf16[512,2048]{1,0:T(8,128)(2,1)} fusion(bf16[512,2048]{1,0:T(8,128)(2,1)S(1)} %bitcast.31, bf16[2048,2048]{1,0:T(8,128)(2,1)} %collective-permute-done, pred[]{:T(512)S(6)} %ge.7), kind=kOutput, calls=%fused_computation.1 | convolution fusion | flops 4298113024 | bytes 12582913 | tf_op jit(solution)/shard_map/dot_general | solution.py:31
  322.8 0.0 all-gather.7.cloned.1.call-update
  322.8 116.1 %all-gather.7.cloned.1.call-done = bf16[2048,2048]{1,0:T(8,128)(2,1)} async-done(((bf16[512,2048]{1,0:T(8,128)(2,1)}), bf16[2048,2048]{1,0:T(8,128)(2,1)}) %all-gather.7.cloned.1.call-update) | async-done | bytes 8388624 | tf_op jit(solution)/shard_map/all_gather | solution.py:47
  439.0 4.5 collective-permute-start.1
  443.5 181.1 %all-gather = bf16[4,1,512]{2,1,0:T(2,128)(2,1)S(1)} all-gather(bf16[1,1,512]{2,1,0:T(2,128)(2,1)S(1)} %reshape.50), channel_id=1, replica_groups=mesh['tm'=64,'rows'=4] {'rows'}, dimensions={0}, use_global_device_ids=true | all-gather | bytes 5120 | tf_op jit(solution)/shard_map/all_gather | solution.py:48
  624.6 1.3 collective-permute-start.2
  625.9 0.7 collective-permute-done.2
  626.7 0.6 fusion.13
  627.3 0.0 copy-start.1
  627.4 9.8 %all-gather.1 = bf16[4,1,512]{2,1,0:T(2,128)(2,1)S(1)} all-gather(bf16[1,1,512]{2,1,0:T(2,128)(2,1)S(1)} %reshape.52), channel_id=1, replica_groups=mesh['tm'=64,'rows'=4] {'rows'}, dimensions={0}, use_global_device_ids=true | all-gather | bytes 5120 | tf_op jit(solution)/shard_map/all_gather | solution.py:48
  637.2 176.9 %collective-permute-start.3 = (bf16[2048]{0:T(1024)(128)(2,1)S(1)}, bf16[2048]{0:T(1024)(128)(2,1)S(1)}, u32[]{:S(2)}, u32[]{:S(2)}) collective-permute-start(bf16[2048]{0:T(1024)(128)(2,1)S(1)} %bitcast.40), channel_id=1, source_target_pairs={{0,8},{4,12},{8,16},{12,20},{16,24},{20,28},{24,32},{28,36},{32,40... | collective-permute-start | bytes 12296 | tf_op jit(solution)/shard_map/ppermute | solution.py:10
  814.1 0.7 collective-permute-done.3
  814.8 2.2 fusion.14
  817.1 0.6 broadcast_in_dim.5
  817.7 0.0 collective-permute-done.1
  817.7 0.0 copy-done.1
  817.7 9.1 %fusion = bf16[1,512,2048]{2,1,0:T(8,128)(2,1)} fusion(bf16[512,2048]{1,0:T(8,128)(2,1)S(1)} %copy-done.1, bf16[2048,2048]{1,0:T(8,128)(2,1)} %collective-permute-done.1, pred[]{:T(512)S(6)} %ge.6), kind=kOutput, calls=%fused_computation.2 | convolution fusion | flops 4298113024 | bytes 12582913 | tf_op jit(solution)/shard_map/dot_general | solution.py:31
  (12 shorter events, 0.1 us)
Async XLA Ops:
  7.2 125.3 %all-gather.5.cloned.1.call-start = ((), (), s32[]{:S(2)}) async-start(), calls=%async_computation | async-start | bytes 10485760 | tf_op jit(solution)/shard_map/all_gather | solution.py:47
  14.5 299.2 %copy-start = (bf16[64,8,8,256]{3,1,2,0:T(8,128)(2,1)S(1)}, bf16[64,8,8,256]{3,1,2,0:T(8,128)(2,1)}, u32[]{:S(2)}) copy-start(bf16[64,8,8,256]{3,1,2,0:T(8,128)(2,1)} %copy.11) | copy-start | bytes 6291460
  14.6 424.4 %all-gather.7.cloned.1.call-start = ((), (), s32[]{:S(2)}) async-start(), calls=%async_computation.1 | async-start | bytes 10485760 | tf_op jit(solution)/shard_map/all_gather | solution.py:47
  132.5 181.2 %collective-permute-start = (bf16[2048,2048]{1,0:T(8,128)(2,1)}, bf16[2048,2048]{1,0:T(8,128)(2,1)}, u32[]{:S(2)}, u32[]{:S(2)}) collective-permute-start(bf16[2048,2048]{1,0:T(8,128)(2,1)} %all-gather.5.cloned.1.call-done), channel_id=1, source_target_pairs={{0,4},{4,8},{8,12},{12,16},{16,20},{20,24},{24,28},{28,32},{32,36}... | collective-permute-start | bytes 25165832 | tf_op jit(solution)/shard_map/ppermute | solution.py:10
  439.0 378.7 %collective-permute-start.1 = (bf16[2048,2048]{1,0:T(8,128)(2,1)}, bf16[2048,2048]{1,0:T(8,128)(2,1)}, u32[]{:S(2)}, u32[]{:S(2)}) collective-permute-start(bf16[2048,2048]{1,0:T(8,128)(2,1)} %all-gather.7.cloned.1.call-done), channel_id=1, source_target_pairs={{0,8},{4,12},{8,16},{12,20},{16,24},{20,28},{24,32},{28,36},{32,40... | collective-permute-start | bytes 25165832 | tf_op jit(solution)/shard_map/ppermute | solution.py:10
  624.6 2.0 collective-permute-start.2
  627.3 190.4 %copy-start.1 = (bf16[512,2048]{1,0:T(8,128)(2,1)S(1)}, bf16[512,2048]{1,0:T(8,128)(2,1)}, u32[]{:S(2)}) copy-start(bf16[512,2048]{1,0:T(8,128)(2,1)} %select_convert_fusion.1) | copy-start | bytes 6291460
  637.2 177.6 %collective-permute-start.3 = (bf16[2048]{0:T(1024)(128)(2,1)S(1)}, bf16[2048]{0:T(1024)(128)(2,1)S(1)}, u32[]{:S(2)}, u32[]{:S(2)}) collective-permute-start(bf16[2048]{0:T(1024)(128)(2,1)S(1)} %bitcast.40), channel_id=1, source_target_pairs={{0,8},{4,12},{8,16},{12,20},{16,24},{20,28},{24,32},{28,36},{32,40... | collective-permute-start | bytes 12296 | tf_op jit(solution)/shard_map/ppermute | solution.py:10
Sparse Core Ops, SparseCore 0:
  14.7 117.7 all-gather.4
  323.0 115.9 all-gather.6
where the time goes:
time: 837 us; the launch traced here: 834 us
  waiting for transfers between devices  412 us (49%)
  blocking collectives  191 us (23%)
  starting transfers between devices  187 us (22%)
  matrix products  23.1 us (3%)
  between operations  14.1 us (2%)
    all_gather x2, waiting for transfers between devices, advance(): lax.all_gather(own_matrix, 'rows', axis=0, tiled=True)  234 us
    all_gather x2, blocking collectives, advance(): lax.all_gather(own_offset, 'rows', axis=0, tiled=True)  191 us
    ppermute x4, starting transfers between devices, passed_along(): return lax.ppermute(block, axis, route)  187 us
    ppermute x4, waiting for transfers between devices, passed_along(): return lax.ppermute(block, axis, route)  178 us
    dot_general x2, matrix products, combine_whole(): jnp.dot(own_matrix, earlier_matrix, preferred_element_type=jnp.float32)  18.3 us
  transfers between devices with their start and end apart: 6, of which 5 were waited for; matrix products, arithmetic and copies ran while one was open for 0% of the time, Pallas kernels for 0%

commit v1 on v0

v1 whole, which is shorter than its diff:
```python
import functools

import jax
import jax.numpy as jnp
from jax import lax
from jax.experimental import pallas as pl
from jax.experimental.pallas import tpu as pltpu
from jax.sharding import PartitionSpec as P

BLK = 256
NBLK = 8
NBAND = 3
STEPS = 64
LOCAL = 512
BODY = NBAND * LOCAL
TOKEN = BODY + 16
CUTS = (0, 768, TOKEN)
AXES = ("tm", "rows")


def route(source, wanted=lambda step: True):
    pairs = []
    for step in range(STEPS):
        for half in range(2):
            if wanted(step):
                from_step, from_half = source(step, half)
                for core in range(2):
                    pairs.append(
                        ((from_step % STEPS) * 4 + from_half * 2 + core, step * 4 + half * 2 + core)
                    )
    return pairs


UP = route(lambda t, h: (t - 1, h if t % 4 > 0 else 1 - h))
DOWN = route(lambda t, h: (t + 1, h if t % 4 < 3 else 1 - h))
ACROSS = route(lambda t, h: (t - 4, h) if t % 4 > 0 else (t, h))
LEVEL_DOWN = route(lambda t, h: (t + 1, h) if t % 4 < 3 else (t - 3, 1 - h))
SIBLING = [(i, i ^ 1) for i in range(STEPS * 4)]


def prepare_kernel(offsets_ref, band_ref, mask_ref, observed_ref, gain_ref, *outs):
    flag = mask_ref[...].astype(jnp.float32)
    gain = gain_ref[...]
    factor = 1.0 - gain * flag
    vector = gain * flag * observed_ref[...]
    for i in range(LOCAL // 128):
        column = jnp.transpose(
            jnp.broadcast_to(factor[:, i * 128 : (i + 1) * 128], (128, 128))
        )
        for j in range(NBAND):
            top = j * LOCAL + i * 128
            piece = max(n for n in range(len(outs)) if CUTS[n] <= top)
            at = top - CUTS[piece]
            for side in range(2):
                lanes = slice(side * 128, side * 128 + 128)
                block = band_ref[0, j, i * 128 : (i + 1) * 128, lanes].astype(jnp.float32)
                outs[piece][at : at + 128, lanes] = (column * block).astype(jnp.bfloat16)
    row = lax.broadcasted_iota(jnp.int32, (16, BLK), 0)
    lane = lax.broadcasted_iota(jnp.int32, (16, BLK), 1)
    tile = jnp.where(row == 0, jnp.broadcast_to(vector[:, :BLK], (16, BLK)), 0.0)
    tile = jnp.where(row == 1, jnp.broadcast_to(vector[:, BLK:], (16, BLK)), tile)
    for j in range(NBAND):
        shift = offsets_ref[0, j].astype(jnp.float32)
        tile = jnp.where((row == 2) & (lane == j), shift, tile)
    at = BODY - CUTS[-2]
    outs[-1][at : at + 16, :] = tile.astype(jnp.bfloat16)


def prepare(band, mask, observed, offsets, gain):
    vmem = pl.BlockSpec(memory_space=pltpu.VMEM)
    return pl.pallas_call(
        prepare_kernel,
        out_shape=[
            jax.ShapeDtypeStruct((b - a, BLK), jnp.bfloat16) for a, b in zip(CUTS, CUTS[1:])
        ],
        in_specs=[pl.BlockSpec(memory_space=pltpu.SMEM)] + [vmem] * 4,
        out_specs=[vmem] * (len(CUTS) - 1),
    )(offsets, band, mask, observed, gain.reshape(1, LOCAL))


def tile_of(ref):
    return ref[BODY : BODY + 16, :].astype(jnp.float32)


def shifts_of(tile):
    row = lax.broadcasted_iota(jnp.int32, (16, BLK), 0)
    lane = lax.broadcasted_iota(jnp.int32, (16, BLK), 1)
    return [
        jnp.sum(jnp.where((row == 2) & (lane == j), tile, 0.0)).astype(jnp.int32)
        for j in range(NBAND)
    ]


def compose_kernel(*refs):
    pieces = len(CUTS) - 1
    arrived = refs[: 13 * pieces]
    matrix_ref, vector_ref = refs[13 * pieces : 13 * pieces + 2]
    own, earlier, factor_a, factor_b, total, own_sem, sems, out_sems = refs[13 * pieces + 2 :]
    step = lax.axis_index("tm")
    place = lax.axis_index("rows")
    half, core = place // 2, place % 2
    phase = step % 4

    own_copies = [
        pltpu.make_async_copy(arrived[n], own.at[CUTS[n] : CUTS[n + 1]], own_sem.at[n])
        for n in range(pieces)
    ]
    copies = [[], [], []]
    for level in range(3):
        side = jnp.where(phase >= level + 1, half, 1 - half)
        groups = [2 * side + core, 2 * side + 1 - core]
        groups += [2 * (1 - side) + core, 2 * (1 - side) + 1 - core]
        for source in range(4):
            for n in range(pieces):
                copies[level].append(
                    pltpu.make_async_copy(
                        arrived[(1 + level * 4 + source) * pieces + n],
                        earlier.at[level, groups[source], CUTS[n] : CUTS[n + 1]],
                        sems.at[level, source, n],
                    )
                )
    for copy in own_copies + copies[0] + copies[1] + copies[2]:
        copy.start()

    factor_a[...] = jnp.zeros_like(factor_a)
    total[...] = jnp.zeros_like(total)
    for copy in own_copies:
        copy.wait()
    own_tile = tile_of(own)
    own_shifts = shifts_of(own_tile)
    for j in range(NBAND):
        for r in range(2):
            target = lax.rem(2 * place + r + own_shifts[j] + NBLK, NBLK)
            factor_a[target, r * BLK : (r + 1) * BLK, :] = own[
                (2 * j + r) * BLK : (2 * j + r + 1) * BLK, :
            ]

    row = lax.broadcasted_iota(jnp.int32, (16, BLK), 0)
    buffers = [factor_a, factor_b]
    for level in range(3):
        source, target = buffers[level % 2], buffers[(level + 1) % 2]
        for copy in copies[level]:
            copy.wait()

        @pl.when(step > level)
        def _():
            shifts = shifts_of(tile_of(earlier.at[level, 0]))

            @pl.loop(0, NBLK)
            def _(c):
                product = None
                for j in range(NBAND):
                    k = lax.rem(c - shifts[j] + NBLK, NBLK)
                    at = pl.multiple_of((2 * j + k % 2) * BLK, BLK)
                    term = jnp.dot(
                        source[k],
                        earlier[level, k // 2, pl.ds(at, BLK), :],
                        preferred_element_type=jnp.float32,
                    )
                    product = term if product is None else product + term
                target[c] = product.astype(jnp.bfloat16)
                tile = tile_of(earlier.at[level, c // 2])
                vector = jnp.sum(jnp.where(row == c % 2, tile, 0.0), axis=0, keepdims=True)
                total[...] += source[c].astype(jnp.float32) * vector

        @pl.when(step <= level)
        def _():
            target[...] = source[...]

    result = buffers[1]
    writes = [
        pltpu.make_async_copy(
            result.at[c], matrix_ref.at[0, :, c * BLK : (c + 1) * BLK], out_sems.at[c]
        )
        for c in range(NBLK)
    ]
    for write in writes:
        write.start()
    value = total[...]
    high = value.astype(jnp.bfloat16)
    low = (value - high.astype(jnp.float32)).astype(jnp.bfloat16)
    ones = jnp.ones((16, BLK), jnp.bfloat16)
    sums = sum(
        lax.dot_general(
            ones, part, (((1,), (1,)), ((), ())), preferred_element_type=jnp.float32
        )
        for part in (high, low)
    )
    for r in range(2):
        vector_ref[:, r * BLK : (r + 1) * BLK] = (
            sums[0:1, r * BLK : (r + 1) * BLK] + own_tile[r : r + 1, :]
        ).astype(jnp.bfloat16)
    for write in writes:
        write.wait()


def compose(arrived):
    pieces = len(CUTS) - 1
    anywhere = pl.BlockSpec(memory_space=pl.ANY)
    return pl.pallas_call(
        compose_kernel,
        out_shape=[
            jax.ShapeDtypeStruct((1, LOCAL, NBLK * BLK), jnp.bfloat16),
            jax.ShapeDtypeStruct((1, LOCAL), jnp.bfloat16),
        ],
        in_specs=[anywhere] * len(arrived),
        out_specs=[anywhere, pl.BlockSpec(memory_space=pltpu.VMEM)],
        scratch_shapes=[
            pltpu.VMEM((TOKEN, BLK), jnp.bfloat16),
            pltpu.VMEM((3, 4, TOKEN, BLK), jnp.bfloat16),
            pltpu.VMEM((NBLK, LOCAL, BLK), jnp.bfloat16),
            pltpu.VMEM((NBLK, LOCAL, BLK), jnp.bfloat16),
            pltpu.VMEM((LOCAL, BLK), jnp.float32),
            pltpu.SemaphoreType.DMA((pieces,)),
            pltpu.SemaphoreType.DMA((3, 4, pieces)),
            pltpu.SemaphoreType.DMA((NBLK,)),
        ],
        compiler_params=pltpu.CompilerParams(vmem_limit_bytes=28 * 1024 * 1024),
    )(*arrived)


def per_device(band_blocks, site_mask, observed, band_offsets, site_gain):
    move = functools.partial(lax.ppermute, axis_name=AXES)
    own = prepare(band_blocks, site_mask, observed, band_offsets, site_gain)
    ups, downs = [], []
    for piece in own:
        across = move(piece, perm=ACROSS)
        up = [move(piece, perm=UP)]
        down = [move(across, perm=LEVEL_DOWN)]
        for _ in range(2):
            up.append(move(up[-1], perm=UP))
            down.append(move(down[-1], perm=DOWN))
        ups.append(up)
        downs.append(down)
    arrived = list(own)
    for level in range(3):
        for chain in ([up[level] for up in ups], [down[2 - level] for down in downs]):
            arrived += chain
            arrived += [move(piece, perm=SIBLING) for piece in chain]
    return tuple(compose(arrived))


def solution(mesh):
    in_specs = (
        P("tm", None, "rows", None),
        P("tm", "rows"),
        P("tm", "rows"),
        P("tm", None),
        P("rows"),
    )
    out_specs = (P("tm", "rows", None), P("tm", "rows"))
    return jax.shard_map(
        per_device, mesh=mesh, in_specs=in_specs, out_specs=out_specs, check_vma=False
    )
```

time: 837 us -> 111 us (0.13)
  the two profiles are of different devices: /device:TPU:1 before, /device:TPU:127 now
where the time goes in v1:
time: 111 us
  starting transfers between devices  44.1 us (40%)
  waiting for transfers between devices  42.8 us (39%)
  Pallas kernels  21.4 us (19%)
  local copies, waits for them, and re-layouts  1.99 us (2%)
    ppermute x4, starting transfers between devices, per_device(): up.append(move(up[-1], perm=UP))  24.5 us
    ppermute x4, waiting for transfers between devices, per_device(): down.append(move(down[-1], perm=DOWN))  24.3 us
    pallas_call x1, Pallas kernels, compose(): pl.pallas_call(compose_kernel, out_shape=[jax.ShapeDtypeStruct((1, LOCAL,...  19.1 us
    ppermute x12, starting transfers between devices, per_device(): arrived += [move(piece, perm=SIBLING) for piece in chain]  11.5 us
    ppermute x4, waiting for transfers between devices, per_device(): up.append(move(up[-1], perm=UP))  11.4 us
    ppermute x2, starting transfers between devices, per_device(): across = move(piece, perm=ACROSS)  5.1 us
    ppermute x2, waiting for transfers between devices, per_device(): across = move(piece, perm=ACROSS)  4.98 us
    ppermute x2, starting transfers between devices, per_device(): up = [move(piece, perm=UP)]  2.97 us
  transfers between devices with their start and end apart: 26, of which 11 were waited for; matrix products, arithmetic and copies ran while one was open for 0% of the time, Pallas kernels for 0%

profile of v1, /device:TPU:127, one launch (start us, length us, event | category | flops | bytes accessed | tf_op | source)
XLA Modules:
  0.0 111.2 jit_solution(18201838109707990876)
XLA Ops:
  0.6 2.3 %shard_map.68 = (bf16[768,256]{1,0:T(8,128)(2,1)}, bf16[784,256]{1,0:T(8,128)(2,1)}) custom-call(s32[1,3]{1,0:T(1,128)} %offsets_ref.1, bf16[1,3,512,256]{3,2,1,0:T(8,128)(2,1)} %band_ref.1, s32[1,512]{1,0:T(1,128)} %mask_ref.1, f32[1,512]{1,0:T(1,128)} %observed_ref.1, f32[1,512]{1,0:T(1,128)} %bitcast.1), custom_call_target="tpu_custom_call" | custom-call | tf_op jit(solution)/shard_map/pallas_call | solution.py:71
  2.9 1.9 %collective-permute-start.4 = (bf16[768,256]{1,0:T(8,128)(2,1)}, bf16[768,256]{1,0:T(8,128)(2,1)S(1)}, u32[]{:S(2)}, u32[]{:S(2)}) collective-permute-start(bf16[768,256]{1,0:T(8,128)(2,1)} %get-tuple-element.4.refs_0_), channel_id=1, source_target_pairs={{0,0},{1,1},{2,2},{3,3},{244,4},{245,5},{246,6},{247,7},{248,8},{2... | collective-permute-start | bytes 1179656 | tf_op jit(solution)/shard_map/ppermute | solution.py:227
  4.8 2.1 %collective-permute-start = (bf16[768,256]{1,0:T(8,128)(2,1)}, bf16[768,256]{1,0:T(8,128)(2,1)S(1)}, u32[]{:S(2)}, u32[]{:S(2)}) collective-permute-start(bf16[768,256]{1,0:T(8,128)(2,1)} %get-tuple-element.4.refs_0_), channel_id=1, source_target_pairs={{254,0},{255,1},{252,2},{253,3},{0,4},{1,5},{2,6},{3,7},{4,8},{5,9... | collective-permute-start | bytes 1179656 | tf_op jit(solution)/shard_map/ppermute | solution.py:228
  7.0 3.2 %collective-permute-start.8 = (bf16[784,256]{1,0:T(8,128)(2,1)}, bf16[784,256]{1,0:T(8,128)(2,1)S(1)}, u32[]{:S(2)}, u32[]{:S(2)}) collective-permute-start(bf16[784,256]{1,0:T(8,128)(2,1)} %get-tuple-element.5.refs_1_), channel_id=1, source_target_pairs={{0,0},{1,1},{2,2},{3,3},{244,4},{245,5},{246,6},{247,7},{248,8},{2... | collective-permute-start | bytes 1204232 | tf_op jit(solution)/shard_map/ppermute | solution.py:227
  10.2 0.8 collective-permute-start.1
  11.0 4.0 %collective-permute-done.4 = bf16[768,256]{1,0:T(8,128)(2,1)S(1)} collective-permute-done((bf16[768,256]{1,0:T(8,128)(2,1)}, bf16[768,256]{1,0:T(8,128)(2,1)S(1)}, u32[]{:S(2)}, u32[]{:S(2)}) %collective-permute-start.4) | collective-permute-done | bytes 393248 | tf_op jit(solution)/shard_map/ppermute | solution.py:227
  15.0 0.0 collective-permute-start.5
  15.0 0.1 collective-permute-done.refs_2_
  15.1 7.5 %collective-permute-start.14 = (bf16[768,256]{1,0:T(8,128)(2,1)S(1)}, bf16[768,256]{1,0:T(8,128)(2,1)S(1)}, u32[]{:S(2)}, u32[]{:S(2)}) collective-permute-start(bf16[768,256]{1,0:T(8,128)(2,1)S(1)} %collective-permute-done.refs_2_), channel_id=1, source_target_pairs={{254,0},{255,1},{252,2},{253,3},{0,4},{1,5},{2,6},{3,7},{4,8},{5,9... | collective-permute-start | bytes 1179656 | tf_op jit(solution)/shard_map/ppermute | solution.py:231
  22.6 1.0 collective-permute-done.8
  23.6 0.0 collective-permute-start.9
  23.6 0.1 collective-permute-done.1.refs_3_
  23.7 7.5 %collective-permute-start.15 = (bf16[784,256]{1,0:T(8,128)(2,1)S(1)}, bf16[784,256]{1,0:T(8,128)(2,1)S(1)}, u32[]{:S(2)}, u32[]{:S(2)}) collective-permute-start(bf16[784,256]{1,0:T(8,128)(2,1)S(1)} %collective-permute-done.1.refs_3_), channel_id=1, source_target_pairs={{254,0},{255,1},{252,2},{253,3},{0,4},{1,5},{2,6},{3,7},{4,8},{5,9... | collective-permute-start | bytes 1204232 | tf_op jit(solution)/shard_map/ppermute | solution.py:231
  31.2 3.0 %collective-permute-start.2 = (bf16[768,256]{1,0:T(8,128)(2,1)S(1)}, bf16[768,256]{1,0:T(8,128)(2,1)S(1)}, u32[]{:S(2)}, u32[]{:S(2)}) collective-permute-start(bf16[768,256]{1,0:T(8,128)(2,1)S(1)} %collective-permute-done.refs_2_), channel_id=1, source_target_pairs={{0,1},{1,0},{2,3},{3,2},{4,5},{5,4},{6,7},{7,6},{8,9},{9,8},{10,11... | collective-permute-start | bytes 1179656 | tf_op jit(solution)/shard_map/ppermute | solution.py:239
  34.2 0.0 collective-permute-done.5.refs_22_
  34.2 0.0 collective-permute-start.3
  34.2 0.0 collective-permute-done.14.refs_10_
  34.2 0.8 collective-permute-start.24
  34.9 0.0 collective-permute-done.9.refs_23_
  35.0 0.0 collective-permute-start.10
  35.0 0.6 collective-permute-done.2.refs_4_
  35.5 0.0 collective-permute-start.6
  35.5 5.1 %collective-permute-done.15.refs_11_ = bf16[784,256]{1,0:T(8,128)(2,1)S(1)} collective-permute-done((bf16[784,256]{1,0:T(8,128)(2,1)S(1)}, bf16[784,256]{1,0:T(8,128)(2,1)S(1)}, u32[]{:S(2)}, u32[]{:S(2)}) %collective-permute-start.15) | collective-permute-done | bytes 401440 | tf_op jit(solution)/shard_map/ppermute | solution.py:231
  40.6 7.0 %collective-permute-start.20 = (bf16[768,256]{1,0:T(8,128)(2,1)S(1)}, bf16[768,256]{1,0:T(8,128)(2,1)S(1)}, u32[]{:S(2)}, u32[]{:S(2)}) collective-permute-start(bf16[768,256]{1,0:T(8,128)(2,1)S(1)} %collective-permute-done.14.refs_10_), channel_id=1, source_target_pairs={{254,0},{255,1},{252,2},{253,3},{0,4},{1,5},{2,6},{3,7},{4,8},{5,9... | collective-permute-start | bytes 1179656 | tf_op jit(solution)/shard_map/ppermute | solution.py:231
  47.6 0.0 collective-permute-done.3.refs_5_
  47.6 2.5 %collective-permute-start.25 = (bf16[784,256]{1,0:T(8,128)(2,1)S(1)}, bf16[784,256]{1,0:T(8,128)(2,1)S(1)}, u32[]{:S(2)}, u32[]{:S(2)}) collective-permute-start(bf16[784,256]{1,0:T(8,128)(2,1)S(1)} %collective-permute-done.9.refs_23_), channel_id=1, source_target_pairs={{0,1},{1,0},{2,3},{3,2},{4,5},{5,4},{6,7},{7,6},{8,9},{9,8},{10,11... | collective-permute-start | bytes 1204232 | tf_op jit(solution)/shard_map/ppermute | solution.py:239
  50.0 0.0 collective-permute-done.24.refs_24_
  50.0 0.1 collective-permute-start.16
  50.1 9.3 %collective-permute-done.6.refs_14_ = bf16[768,256]{1,0:T(8,128)(2,1)S(1)} collective-permute-done((bf16[768,256]{1,0:T(8,128)(2,1)S(1)}, bf16[768,256]{1,0:T(8,128)(2,1)S(1)}, u32[]{:S(2)}, u32[]{:S(2)}) %collective-permute-start.6) | collective-permute-done | bytes 393248 | tf_op jit(solution)/shard_map/ppermute | solution.py:232
  59.5 2.4 %collective-permute-start.21 = (bf16[784,256]{1,0:T(8,128)(2,1)S(1)}, bf16[784,256]{1,0:T(8,128)(2,1)S(1)}, u32[]{:S(2)}, u32[]{:S(2)}) collective-permute-start(bf16[784,256]{1,0:T(8,128)(2,1)S(1)} %collective-permute-done.15.refs_11_), channel_id=1, source_target_pairs={{254,0},{255,1},{252,2},{253,3},{0,4},{1,5},{2,6},{3,7},{4,8},{5,9... | collective-permute-start | bytes 1204232 | tf_op jit(solution)/shard_map/ppermute | solution.py:231
  61.9 0.0 collective-permute-done.20.refs_18_
  61.9 1.1 collective-permute-start.17
  63.0 0.0 collective-permute-done.10.refs_15_
  63.0 0.0 collective-permute-start.11
  63.0 0.0 collective-permute-done.16.refs_12_
  63.0 0.4 collective-permute-start.18
  63.3 0.0 collective-permute-done.25.refs_25_
  63.3 0.0 collective-permute-start.7
  63.3 6.4 %collective-permute-done.21.refs_19_ = bf16[784,256]{1,0:T(8,128)(2,1)S(1)} collective-permute-done((bf16[784,256]{1,0:T(8,128)(2,1)S(1)}, bf16[784,256]{1,0:T(8,128)(2,1)S(1)}, u32[]{:S(2)}, u32[]{:S(2)}) %collective-permute-start.21) | collective-permute-done | bytes 401440 | tf_op jit(solution)/shard_map/ppermute | solution.py:231
  69.7 1.7 %collective-permute-start.19 = (bf16[784,256]{1,0:T(8,128)(2,1)S(1)}, bf16[784,256]{1,0:T(8,128)(2,1)S(1)}, u32[]{:S(2)}, u32[]{:S(2)}) collective-permute-start(bf16[784,256]{1,0:T(8,128)(2,1)S(1)} %collective-permute-done.10.refs_15_), channel_id=1, source_target_pairs={{0,1},{1,0},{2,3},{3,2},{4,5},{5,4},{6,7},{7,6},{8,9},{9,8},{10,11... | collective-permute-start | bytes 1204232 | tf_op jit(solution)/shard_map/ppermute | solution.py:239
  71.4 0.0 collective-permute-done.17.refs_13_
  71.4 0.0 collective-permute-start.23
  71.4 7.9 %collective-permute-done.11.refs_7_ = bf16[784,256]{1,0:T(8,128)(2,1)S(1)} collective-permute-done((bf16[784,256]{1,0:T(8,128)(2,1)S(1)}, bf16[784,256]{1,0:T(8,128)(2,1)S(1)}, u32[]{:S(2)}, u32[]{:S(2)}) %collective-permute-start.11) | collective-permute-done | bytes 401440 | tf_op jit(solution)/shard_map/ppermute | solution.py:232
  79.3 1.3 %collective-permute-start.13 = (bf16[784,256]{1,0:T(8,128)(2,1)S(1)}, bf16[784,256]{1,0:T(8,128)(2,1)S(1)}, u32[]{:S(2)}, u32[]{:S(2)}) collective-permute-start(bf16[784,256]{1,0:T(8,128)(2,1)S(1)} %collective-permute-done.11.refs_7_), channel_id=1, source_target_pairs={{0,1},{1,0},{2,3},{3,2},{4,5},{5,4},{6,7},{7,6},{8,9},{9,8},{10,11... | collective-permute-start | bytes 1204232 | tf_op jit(solution)/shard_map/ppermute | solution.py:239
  80.6 0.0 collective-permute-done.18.refs_16_
  80.6 0.0 collective-permute-start.22
  80.6 7.1 %collective-permute-done.7.refs_6_ = bf16[768,256]{1,0:T(8,128)(2,1)S(1)} collective-permute-done((bf16[768,256]{1,0:T(8,128)(2,1)S(1)}, bf16[768,256]{1,0:T(8,128)(2,1)S(1)}, u32[]{:S(2)}, u32[]{:S(2)}) %collective-permute-start.7) | collective-permute-done | bytes 393248 | tf_op jit(solution)/shard_map/ppermute | solution.py:232
  87.7 0.8 collective-permute-start.12
  88.5 0.0 collective-permute-done.22.refs_20_
  88.5 0.0 collective-permute-done.19.refs_17_
  88.5 0.0 collective-permute-done.23.refs_21_
  88.5 1.3 %collective-permute-done.12.refs_8_ = bf16[768,256]{1,0:T(8,128)(2,1)S(1)} collective-permute-done((bf16[768,256]{1,0:T(8,128)(2,1)S(1)}, bf16[768,256]{1,0:T(8,128)(2,1)S(1)}, u32[]{:S(2)}, u32[]{:S(2)}) %collective-permute-start.12) | collective-permute-done | bytes 393248 | tf_op jit(solution)/shard_map/ppermute | solution.py:239
  89.9 0.0 collective-permute-done.13.refs_9_
  89.9 0.0 copy-start
  89.9 1.0 copy-done
  90.9 0.0 copy-start.1
  90.9 1.0 copy-done.1
  91.9 19.1 %shard_map.69 = (bf16[1,512,2048]{2,1,0:T(8,128)(2,1)}, bf16[1,512]{1,0:T(2,128)(2,1)}) custom-call(bf16[768,256]{1,0:T(8,128)(2,1)S(1)} %copy-done.1, bf16[784,256]{1,0:T(8,128)(2,1)S(1)} %copy-done, bf16[768,256]{1,0:T(8,128)(2,1)S(1)} %collective-permute-done.refs_2_, bf16[784,256]{1,0:T(8,128)(2,1)S(1)} %collective-permute-done.1.refs_3_, ...), custom_call_target="tpu_custom_call" | custom-call | tf_op jit(solution)/shard_map/pallas_call | solution.py:200
Async XLA Ops:
  2.9 12.1 %collective-permute-start.4 = (bf16[768,256]{1,0:T(8,128)(2,1)}, bf16[768,256]{1,0:T(8,128)(2,1)S(1)}, u32[]{:S(2)}, u32[]{:S(2)}) collective-permute-start(bf16[768,256]{1,0:T(8,128)(2,1)} %get-tuple-element.4.refs_0_), channel_id=1, source_target_pairs={{0,0},{1,1},{2,2},{3,3},{244,4},{245,5},{246,6},{247,7},{248,8},{2... | collective-permute-start | bytes 1179656 | tf_op jit(solution)/shard_map/ppermute | solution.py:227
  4.8 10.2 %collective-permute-start = (bf16[768,256]{1,0:T(8,128)(2,1)}, bf16[768,256]{1,0:T(8,128)(2,1)S(1)}, u32[]{:S(2)}, u32[]{:S(2)}) collective-permute-start(bf16[768,256]{1,0:T(8,128)(2,1)} %get-tuple-element.4.refs_0_), channel_id=1, source_target_pairs={{254,0},{255,1},{252,2},{253,3},{0,4},{1,5},{2,6},{3,7},{4,8},{5,9... | collective-permute-start | bytes 1179656 | tf_op jit(solution)/shard_map/ppermute | solution.py:228
  7.0 16.6 %collective-permute-start.8 = (bf16[784,256]{1,0:T(8,128)(2,1)}, bf16[784,256]{1,0:T(8,128)(2,1)S(1)}, u32[]{:S(2)}, u32[]{:S(2)}) collective-permute-start(bf16[784,256]{1,0:T(8,128)(2,1)} %get-tuple-element.5.refs_1_), channel_id=1, source_target_pairs={{0,0},{1,1},{2,2},{3,3},{244,4},{245,5},{246,6},{247,7},{248,8},{2... | collective-permute-start | bytes 1204232 | tf_op jit(solution)/shard_map/ppermute | solution.py:227
  10.2 13.5 %collective-permute-start.1 = (bf16[784,256]{1,0:T(8,128)(2,1)}, bf16[784,256]{1,0:T(8,128)(2,1)S(1)}, u32[]{:S(2)}, u32[]{:S(2)}) collective-permute-start(bf16[784,256]{1,0:T(8,128)(2,1)} %get-tuple-element.5.refs_1_), channel_id=1, source_target_pairs={{254,0},{255,1},{252,2},{253,3},{0,4},{1,5},{2,6},{3,7},{4,8},{5,9... | collective-permute-start | bytes 1204232 | tf_op jit(solution)/shard_map/ppermute | solution.py:228
  15.0 19.2 %collective-permute-start.5 = (bf16[768,256]{1,0:T(8,128)(2,1)S(1)}, bf16[768,256]{1,0:T(8,128)(2,1)S(1)}, u32[]{:S(2)}, u32[]{:S(2)}) collective-permute-start(bf16[768,256]{1,0:T(8,128)(2,1)S(1)} %collective-permute-done.4), channel_id=1, source_target_pairs={{4,0},{5,1},{6,2},{7,3},{8,4},{9,5},{10,6},{11,7},{12,8},{13,9},{1... | collective-permute-start | bytes 1179656 | tf_op jit(solution)/shard_map/ppermute | solution.py:229
  15.1 19.1 %collective-permute-start.14 = (bf16[768,256]{1,0:T(8,128)(2,1)S(1)}, bf16[768,256]{1,0:T(8,128)(2,1)S(1)}, u32[]{:S(2)}, u32[]{:S(2)}) collective-permute-start(bf16[768,256]{1,0:T(8,128)(2,1)S(1)} %collective-permute-done.refs_2_), channel_id=1, source_target_pairs={{254,0},{255,1},{252,2},{253,3},{0,4},{1,5},{2,6},{3,7},{4,8},{5,9... | collective-permute-start | bytes 1179656 | tf_op jit(solution)/shard_map/ppermute | solution.py:231
  23.6 11.4 %collective-permute-start.9 = (bf16[784,256]{1,0:T(8,128)(2,1)S(1)}, bf16[784,256]{1,0:T(8,128)(2,1)S(1)}, u32[]{:S(2)}, u32[]{:S(2)}) collective-permute-start(bf16[784,256]{1,0:T(8,128)(2,1)S(1)} %collective-permute-done.8), channel_id=1, source_target_pairs={{4,0},{5,1},{6,2},{7,3},{8,4},{9,5},{10,6},{11,7},{12,8},{13,9},{1... | collective-permute-start | bytes 1204232 | tf_op jit(solution)/shard_map/ppermute | solution.py:229
  23.7 16.9 %collective-permute-start.15 = (bf16[784,256]{1,0:T(8,128)(2,1)S(1)}, bf16[784,256]{1,0:T(8,128)(2,1)S(1)}, u32[]{:S(2)}, u32[]{:S(2)}) collective-permute-start(bf16[784,256]{1,0:T(8,128)(2,1)S(1)} %collective-permute-done.1.refs_3_), channel_id=1, source_target_pairs={{254,0},{255,1},{252,2},{253,3},{0,4},{1,5},{2,6},{3,7},{4,8},{5,9... | collective-permute-start | bytes 1204232 | tf_op jit(solution)/shard_map/ppermute | solution.py:231
  31.2 4.3 %collective-permute-start.2 = (bf16[768,256]{1,0:T(8,128)(2,1)S(1)}, bf16[768,256]{1,0:T(8,128)(2,1)S(1)}, u32[]{:S(2)}, u32[]{:S(2)}) collective-permute-start(bf16[768,256]{1,0:T(8,128)(2,1)S(1)} %collective-permute-done.refs_2_), channel_id=1, source_target_pairs={{0,1},{1,0},{2,3},{3,2},{4,5},{5,4},{6,7},{7,6},{8,9},{9,8},{10,11... | collective-permute-start | bytes 1179656 | tf_op jit(solution)/shard_map/ppermute | solution.py:239
  34.2 13.4 %collective-permute-start.3 = (bf16[784,256]{1,0:T(8,128)(2,1)S(1)}, bf16[784,256]{1,0:T(8,128)(2,1)S(1)}, u32[]{:S(2)}, u32[]{:S(2)}) collective-permute-start(bf16[784,256]{1,0:T(8,128)(2,1)S(1)} %collective-permute-done.1.refs_3_), channel_id=1, source_target_pairs={{0,1},{1,0},{2,3},{3,2},{4,5},{5,4},{6,7},{7,6},{8,9},{9,8},{10,11... | collective-permute-start | bytes 1204232 | tf_op jit(solution)/shard_map/ppermute | solution.py:239
  34.2 15.9 %collective-permute-start.24 = (bf16[768,256]{1,0:T(8,128)(2,1)S(1)}, bf16[768,256]{1,0:T(8,128)(2,1)S(1)}, u32[]{:S(2)}, u32[]{:S(2)}) collective-permute-start(bf16[768,256]{1,0:T(8,128)(2,1)S(1)} %collective-permute-done.5.refs_22_), channel_id=1, source_target_pairs={{0,1},{1,0},{2,3},{3,2},{4,5},{5,4},{6,7},{7,6},{8,9},{9,8},{10,11... | collective-permute-start | bytes 1179656 | tf_op jit(solution)/shard_map/ppermute | solution.py:239
  35.0 28.0 %collective-permute-start.10 = (bf16[784,256]{1,0:T(8,128)(2,1)S(1)}, bf16[784,256]{1,0:T(8,128)(2,1)S(1)}, u32[]{:S(2)}, u32[]{:S(2)}) collective-permute-start(bf16[784,256]{1,0:T(8,128)(2,1)S(1)} %collective-permute-done.9.refs_23_), channel_id=1, source_target_pairs={{4,0},{5,1},{6,2},{7,3},{8,4},{9,5},{10,6},{11,7},{12,8},{13,9},{1... | collective-permute-start | bytes 1204232 | tf_op jit(solution)/shard_map/ppermute | solution.py:232
  35.5 23.9 %collective-permute-start.6 = (bf16[768,256]{1,0:T(8,128)(2,1)S(1)}, bf16[768,256]{1,0:T(8,128)(2,1)S(1)}, u32[]{:S(2)}, u32[]{:S(2)}) collective-permute-start(bf16[768,256]{1,0:T(8,128)(2,1)S(1)} %collective-permute-done.5.refs_22_), channel_id=1, source_target_pairs={{4,0},{5,1},{6,2},{7,3},{8,4},{9,5},{10,6},{11,7},{12,8},{13,9},{1... | collective-permute-start | bytes 1179656 | tf_op jit(solution)/shard_map/ppermute | solution.py:232
  40.6 21.3 %collective-permute-start.20 = (bf16[768,256]{1,0:T(8,128)(2,1)S(1)}, bf16[768,256]{1,0:T(8,128)(2,1)S(1)}, u32[]{:S(2)}, u32[]{:S(2)}) collective-permute-start(bf16[768,256]{1,0:T(8,128)(2,1)S(1)} %collective-permute-done.14.refs_10_), channel_id=1, source_target_pairs={{254,0},{255,1},{252,2},{253,3},{0,4},{1,5},{2,6},{3,7},{4,8},{5,9... | collective-permute-start | bytes 1179656 | tf_op jit(solution)/shard_map/ppermute | solution.py:231
  47.6 15.7 %collective-permute-start.25 = (bf16[784,256]{1,0:T(8,128)(2,1)S(1)}, bf16[784,256]{1,0:T(8,128)(2,1)S(1)}, u32[]{:S(2)}, u32[]{:S(2)}) collective-permute-start(bf16[784,256]{1,0:T(8,128)(2,1)S(1)} %collective-permute-done.9.refs_23_), channel_id=1, source_target_pairs={{0,1},{1,0},{2,3},{3,2},{4,5},{5,4},{6,7},{7,6},{8,9},{9,8},{10,11... | collective-permute-start | bytes 1204232 | tf_op jit(solution)/shard_map/ppermute | solution.py:239
  50.0 12.9 %collective-permute-start.16 = (bf16[768,256]{1,0:T(8,128)(2,1)S(1)}, bf16[768,256]{1,0:T(8,128)(2,1)S(1)}, u32[]{:S(2)}, u32[]{:S(2)}) collective-permute-start(bf16[768,256]{1,0:T(8,128)(2,1)S(1)} %collective-permute-done.14.refs_10_), channel_id=1, source_target_pairs={{0,1},{1,0},{2,3},{3,2},{4,5},{5,4},{6,7},{7,6},{8,9},{9,8},{10,11... | collective-permute-start | bytes 1179656 | tf_op jit(solution)/shard_map/ppermute | solution.py:239
  59.5 10.3 %collective-permute-start.21 = (bf16[784,256]{1,0:T(8,128)(2,1)S(1)}, bf16[784,256]{1,0:T(8,128)(2,1)S(1)}, u32[]{:S(2)}, u32[]{:S(2)}) collective-permute-start(bf16[784,256]{1,0:T(8,128)(2,1)S(1)} %collective-permute-done.15.refs_11_), channel_id=1, source_target_pairs={{254,0},{255,1},{252,2},{253,3},{0,4},{1,5},{2,6},{3,7},{4,8},{5,9... | collective-permute-start | bytes 1204232 | tf_op jit(solution)/shard_map/ppermute | solution.py:231
  61.9 9.5 %collective-permute-start.17 = (bf16[784,256]{1,0:T(8,128)(2,1)S(1)}, bf16[784,256]{1,0:T(8,128)(2,1)S(1)}, u32[]{:S(2)}, u32[]{:S(2)}) collective-permute-start(bf16[784,256]{1,0:T(8,128)(2,1)S(1)} %collective-permute-done.15.refs_11_), channel_id=1, source_target_pairs={{0,1},{1,0},{2,3},{3,2},{4,5},{5,4},{6,7},{7,6},{8,9},{9,8},{10,11... | collective-permute-start | bytes 1204232 | tf_op jit(solution)/shard_map/ppermute | solution.py:239
  63.0 16.3 %collective-permute-start.11 = (bf16[784,256]{1,0:T(8,128)(2,1)S(1)}, bf16[784,256]{1,0:T(8,128)(2,1)S(1)}, u32[]{:S(2)}, u32[]{:S(2)}) collective-permute-start(bf16[784,256]{1,0:T(8,128)(2,1)S(1)} %collective-permute-done.10.refs_15_), channel_id=1, source_target_pairs={{4,0},{5,1},{6,2},{7,3},{8,4},{9,5},{10,6},{11,7},{12,8},{13,9},{1... | collective-permute-start | bytes 1204232 | tf_op jit(solution)/shard_map/ppermute | solution.py:232
  63.0 17.6 %collective-permute-start.18 = (bf16[768,256]{1,0:T(8,128)(2,1)S(1)}, bf16[768,256]{1,0:T(8,128)(2,1)S(1)}, u32[]{:S(2)}, u32[]{:S(2)}) collective-permute-start(bf16[768,256]{1,0:T(8,128)(2,1)S(1)} %collective-permute-done.6.refs_14_), channel_id=1, source_target_pairs={{0,1},{1,0},{2,3},{3,2},{4,5},{5,4},{6,7},{7,6},{8,9},{9,8},{10,11... | collective-permute-start | bytes 1179656 | tf_op jit(solution)/shard_map/ppermute | solution.py:239
  63.3 24.4 %collective-permute-start.7 = (bf16[768,256]{1,0:T(8,128)(2,1)S(1)}, bf16[768,256]{1,0:T(8,128)(2,1)S(1)}, u32[]{:S(2)}, u32[]{:S(2)}) collective-permute-start(bf16[768,256]{1,0:T(8,128)(2,1)S(1)} %collective-permute-done.6.refs_14_), channel_id=1, source_target_pairs={{4,0},{5,1},{6,2},{7,3},{8,4},{9,5},{10,6},{11,7},{12,8},{13,9},{1... | collective-permute-start | bytes 1179656 | tf_op jit(solution)/shard_map/ppermute | solution.py:232
  69.7 18.8 %collective-permute-start.19 = (bf16[784,256]{1,0:T(8,128)(2,1)S(1)}, bf16[784,256]{1,0:T(8,128)(2,1)S(1)}, u32[]{:S(2)}, u32[]{:S(2)}) collective-permute-start(bf16[784,256]{1,0:T(8,128)(2,1)S(1)} %collective-permute-done.10.refs_15_), channel_id=1, source_target_pairs={{0,1},{1,0},{2,3},{3,2},{4,5},{5,4},{6,7},{7,6},{8,9},{9,8},{10,11... | collective-permute-start | bytes 1204232 | tf_op jit(solution)/shard_map/ppermute | solution.py:239
  71.4 17.1 %collective-permute-start.23 = (bf16[784,256]{1,0:T(8,128)(2,1)S(1)}, bf16[784,256]{1,0:T(8,128)(2,1)S(1)}, u32[]{:S(2)}, u32[]{:S(2)}) collective-permute-start(bf16[784,256]{1,0:T(8,128)(2,1)S(1)} %collective-permute-done.21.refs_19_), channel_id=1, source_target_pairs={{0,1},{1,0},{2,3},{3,2},{4,5},{5,4},{6,7},{7,6},{8,9},{9,8},{10,11... | collective-permute-start | bytes 1204232 | tf_op jit(solution)/shard_map/ppermute | solution.py:239
  79.3 10.6 %collective-permute-start.13 = (bf16[784,256]{1,0:T(8,128)(2,1)S(1)}, bf16[784,256]{1,0:T(8,128)(2,1)S(1)}, u32[]{:S(2)}, u32[]{:S(2)}) collective-permute-start(bf16[784,256]{1,0:T(8,128)(2,1)S(1)} %collective-permute-done.11.refs_7_), channel_id=1, source_target_pairs={{0,1},{1,0},{2,3},{3,2},{4,5},{5,4},{6,7},{7,6},{8,9},{9,8},{10,11... | collective-permute-start | bytes 1204232 | tf_op jit(solution)/shard_map/ppermute | solution.py:239
  80.6 8.0 %collective-permute-start.22 = (bf16[768,256]{1,0:T(8,128)(2,1)S(1)}, bf16[768,256]{1,0:T(8,128)(2,1)S(1)}, u32[]{:S(2)}, u32[]{:S(2)}) collective-permute-start(bf16[768,256]{1,0:T(8,128)(2,1)S(1)} %collective-permute-done.20.refs_18_), channel_id=1, source_target_pairs={{0,1},{1,0},{2,3},{3,2},{4,5},{5,4},{6,7},{7,6},{8,9},{9,8},{10,11... | collective-permute-start | bytes 1179656 | tf_op jit(solution)/shard_map/ppermute | solution.py:239
  87.7 2.2 %collective-permute-start.12 = (bf16[768,256]{1,0:T(8,128)(2,1)S(1)}, bf16[768,256]{1,0:T(8,128)(2,1)S(1)}, u32[]{:S(2)}, u32[]{:S(2)}) collective-permute-start(bf16[768,256]{1,0:T(8,128)(2,1)S(1)} %collective-permute-done.7.refs_6_), channel_id=1, source_target_pairs={{0,1},{1,0},{2,3},{3,2},{4,5},{5,4},{6,7},{7,6},{8,9},{9,8},{10,11... | collective-permute-start | bytes 1179656 | tf_op jit(solution)/shard_map/ppermute | solution.py:239
  89.9 1.0 copy-start
  90.9 1.0 copy-start.1

commit v2 on v0

v2 whole, which is shorter than its diff:
```python
import functools

import jax
import jax.numpy as jnp
from jax import lax
from jax.experimental import pallas as pl
from jax.experimental.pallas import tpu as pltpu
from jax.sharding import PartitionSpec as P

BLK = 256
NBLK = 8
NBAND = 3
STEPS = 64
LOCAL = 512
TILE = 16
TOKEN = TILE + NBAND * LOCAL
CUT = TILE + 384
AXES = ("tm", "rows")


def route(source):
    pairs = []
    for step in range(STEPS):
        for half in range(2):
            from_step, from_half = source(step, half)
            for core in range(2):
                pairs.append(
                    ((from_step % STEPS) * 4 + from_half * 2 + core, step * 4 + half * 2 + core)
                )
    return pairs


UP = route(lambda t, h: (t - 1, h if t % 4 > 0 else 1 - h))
DOWN = route(lambda t, h: (t + 1, h if t % 4 < 3 else 1 - h))
FIRST_DOWN = route(lambda t, h: (t - 3, h if t % 4 < 3 else 1 - h))
ACROSS = route(lambda t, h: (t - 4, h) if t % 4 == 3 else (t, h))
LEVEL_UP = route(lambda t, h: (t - 1, h) if t % 4 > 0 else (t + 3, 1 - h))
SIBLING = [(i, i ^ 1) for i in range(STEPS * 4)]


def store(outs, top, value, lanes=slice(0, BLK)):
    rows = value.shape[0]
    whole, low, high = outs
    whole[top : top + rows, lanes] = value
    if top + rows <= CUT:
        low[top : top + rows, lanes] = value
    else:
        high[top - CUT : top - CUT + rows, lanes] = value


def prepare_kernel(offsets_ref, band_ref, mask_ref, observed_ref, gain_ref, *outs):
    flag = mask_ref[...].astype(jnp.float32)
    gain = gain_ref[...]
    factor = 1.0 - gain * flag
    vector = gain * flag * observed_ref[...]
    row = lax.broadcasted_iota(jnp.int32, (TILE, BLK), 0)
    lane = lax.broadcasted_iota(jnp.int32, (TILE, BLK), 1)
    tile = jnp.where(row == 0, jnp.broadcast_to(vector[:, :BLK], (TILE, BLK)), 0.0)
    tile = jnp.where(row == 1, jnp.broadcast_to(vector[:, BLK:], (TILE, BLK)), tile)
    for j in range(NBAND):
        shift = offsets_ref[0, j].astype(jnp.float32)
        tile = jnp.where((row == 2) & (lane == j), shift, tile)
    store(outs, 0, tile.astype(jnp.bfloat16))
    for i in range(LOCAL // 128):
        column = jnp.transpose(
            jnp.broadcast_to(factor[:, i * 128 : (i + 1) * 128], (128, 128))
        )
        for j in range(NBAND):
            for side in range(2):
                lanes = slice(side * 128, side * 128 + 128)
                block = band_ref[0, j, i * 128 : (i + 1) * 128, lanes].astype(jnp.float32)
                top = TILE + j * LOCAL + i * 128
                store(outs, top, (column * block).astype(jnp.bfloat16), lanes)


def prepare(band, mask, observed, offsets, gain):
    vmem = pl.BlockSpec(memory_space=pltpu.VMEM)
    return pl.pallas_call(
        prepare_kernel,
        out_shape=[
            jax.ShapeDtypeStruct((rows, BLK), jnp.bfloat16) for rows in (TOKEN, CUT, TOKEN - CUT)
        ],
        in_specs=[pl.BlockSpec(memory_space=pltpu.SMEM)] + [vmem] * 4,
        out_specs=[vmem] * 3,
    )(offsets, band, mask, observed, gain.reshape(1, LOCAL))


def tile_of(ref):
    return ref[:TILE, :].astype(jnp.float32)


def shifts_of(tile):
    row = lax.broadcasted_iota(jnp.int32, (TILE, BLK), 0)
    lane = lax.broadcasted_iota(jnp.int32, (TILE, BLK), 1)
    return [
        jnp.sum(jnp.where((row == 2) & (lane == j), tile, 0.0)).astype(jnp.int32)
        for j in range(NBAND)
    ]


def place_of(step, place, distance):
    half, core = place // 2, place % 2
    side = jnp.where(step % 4 >= distance, half, 1 - half)
    return [
        2 * side + core,
        2 * side + 1 - core,
        2 * (1 - side) + core,
        2 * (1 - side) + 1 - core,
    ]


def gather(refs, whole, groups, sems):
    low, high, sibling_low, sibling_high, down, sibling_down = refs
    parts = [
        (low, groups[0], 0, CUT),
        (high, groups[0], CUT, TOKEN),
        (sibling_low, groups[1], 0, CUT),
        (sibling_high, groups[1], CUT, TOKEN),
        (down, groups[2], 0, TOKEN),
        (sibling_down, groups[3], 0, TOKEN),
    ]
    return [
        pltpu.make_async_copy(ref, whole.at[group, a:b], sems.at[n])
        for n, (ref, group, a, b) in enumerate(parts)
    ]


def column_of(source, earlier, shifts, c):
    product = None
    for j in range(NBAND):
        k = lax.rem(c - shifts[j] + NBLK, NBLK)
        at = pl.multiple_of(TILE + (2 * j + k % 2) * BLK, TILE)
        term = jnp.dot(
            source[k], earlier[k // 2, pl.ds(at, BLK), :], preferred_element_type=jnp.float32
        )
        product = term if product is None else product + term
    return product


def vector_of(tiles, c):
    return tiles[c // 2][c % 2 : c % 2 + 1, :]


def pair_kernel(*refs):
    own, first, second, last = refs[0], refs[1:7], refs[7:13], refs[13:17]
    product_ref, vector_ref = refs[17:19]
    near, far, bare, level, total, tiles, near_sems, far_sems, tile_sems = refs[19:]
    step, place = lax.axis_index("tm"), lax.axis_index("rows")

    near_copies = gather(first, near, place_of(step, place, 1), near_sems)
    far_copies = gather(second, far, place_of(step, place, 2), far_sems)
    groups = place_of(step, place, 3)
    tile_copies = [
        pltpu.make_async_copy(ref.at[0:TILE], tiles.at[group], tile_sems.at[n])
        for n, (ref, group) in enumerate(zip(last, groups))
    ]
    for copy in near_copies + tile_copies + far_copies:
        copy.start()

    bare[...] = jnp.zeros_like(bare)
    own_tile = tile_of(own)
    own_shifts = shifts_of(own_tile)
    for j in range(NBAND):
        for r in range(2):
            target = lax.rem(2 * place + r + own_shifts[j] + NBLK, NBLK)
            at = TILE + (2 * j + r) * BLK
            bare[target, r * BLK : (r + 1) * BLK, :] = own[at : at + BLK, :]
    for copy in near_copies + tile_copies:
        copy.wait()

    near_tiles = [tile_of(near.at[g]) for g in range(4)]
    total[...] = jnp.zeros_like(total)

    @pl.when(step >= 1)
    def _():
        shifts = shifts_of(near_tiles[0])
        for c in range(NBLK):
            level[c] = column_of(bare, near, shifts, c).astype(jnp.bfloat16)
            total[...] += bare[c].astype(jnp.float32) * vector_of(near_tiles, c)

    @pl.when(step < 1)
    def _():
        level[...] = bare[...]

    for copy in far_copies:
        copy.wait()
    far_tiles = [tile_of(far.at[g]) for g in range(4)]

    @pl.when(step >= 2)
    def _():
        shifts = shifts_of(far_tiles[0])
        for c in range(NBLK):
            product_ref[c] = column_of(level, far, shifts, c).astype(jnp.bfloat16)
            total[...] += level[c].astype(jnp.float32) * vector_of(far_tiles, c)

    @pl.when(step < 2)
    def _():
        product_ref[...] = level[...]

    @pl.when(step >= 3)
    def _():
        last_tiles = [tile_of(tiles.at[g]) for g in range(4)]
        value = total[...]
        for c in range(NBLK):
            value = value + product_ref[c].astype(jnp.float32) * vector_of(last_tiles, c)
        total[...] = value

    value = total[...]
    high = value.astype(jnp.bfloat16)
    low = (value - high.astype(jnp.float32)).astype(jnp.bfloat16)
    ones = jnp.ones((TILE, BLK), jnp.bfloat16)
    sums = sum(
        lax.dot_general(ones, part, (((1,), (1,)), ((), ())), preferred_element_type=jnp.float32)
        for part in (high, low)
    )
    for r in range(2):
        vector_ref[:, r * BLK : (r + 1) * BLK] = (
            sums[0:1, r * BLK : (r + 1) * BLK] + own_tile[r : r + 1, :]
        ).astype(jnp.bfloat16)


def pair(own, first, second, last):
    anywhere, vmem = pl.BlockSpec(memory_space=pl.ANY), pl.BlockSpec(memory_space=pltpu.VMEM)
    arrived = [own, *first, *second, *last]
    return pl.pallas_call(
        pair_kernel,
        out_shape=[
            jax.ShapeDtypeStruct((NBLK, LOCAL, BLK), jnp.bfloat16),
            jax.ShapeDtypeStruct((1, LOCAL), jnp.bfloat16),
        ],
        in_specs=[vmem] + [anywhere] * (len(arrived) - 1),
        out_specs=[vmem, vmem],
        scratch_shapes=[
            pltpu.VMEM((4, TOKEN, BLK), jnp.bfloat16),
            pltpu.VMEM((4, TOKEN, BLK), jnp.bfloat16),
            pltpu.VMEM((NBLK, LOCAL, BLK), jnp.bfloat16),
            pltpu.VMEM((NBLK, LOCAL, BLK), jnp.bfloat16),
            pltpu.VMEM((LOCAL, BLK), jnp.float32),
            pltpu.VMEM((4, TILE, BLK), jnp.bfloat16),
            pltpu.SemaphoreType.DMA((6,)),
            pltpu.SemaphoreType.DMA((6,)),
            pltpu.SemaphoreType.DMA((4,)),
        ],
        compiler_params=pltpu.CompilerParams(vmem_limit_bytes=24 * 1024 * 1024),
        cost_estimate=pl.CostEstimate(
            flops=96 * 2 * BLK**3, bytes_accessed=10 * 2**20, transcendentals=0
        ),
    )(*arrived)


def last_kernel(*refs):
    before_ref, third, matrix_ref = refs[0], refs[1:7], refs[7]
    before, earlier, result, before_sem, sems, out_sems = refs[8:]
    step, place = lax.axis_index("tm"), lax.axis_index("rows")
    before_copy = pltpu.make_async_copy(before_ref, before, before_sem.at[0])
    copies = gather(third, earlier, place_of(step, place, 3), sems)
    for copy in [before_copy] + copies:
        copy.start()
    for copy in [before_copy] + copies:
        copy.wait()
    writes = [
        pltpu.make_async_copy(
            result.at[c], matrix_ref.at[0, :, c * BLK : (c + 1) * BLK], out_sems.at[c]
        )
        for c in range(NBLK)
    ]

    @pl.when(step >= 3)
    def _():
        shifts = shifts_of(tile_of(earlier.at[0]))
        for c in range(NBLK):
            result[c] = column_of(before, earlier, shifts, c).astype(jnp.bfloat16)
            writes[c].start()

    @pl.when(step < 3)
    def _():
        for c in range(NBLK):
            result[c] = before[c]
            writes[c].start()

    for write in writes:
        write.wait()


def last(before, third):
    anywhere = pl.BlockSpec(memory_space=pl.ANY)
    return pl.pallas_call(
        last_kernel,
        out_shape=jax.ShapeDtypeStruct((1, LOCAL, NBLK * BLK), jnp.bfloat16),
        in_specs=[anywhere] * 7,
        out_specs=anywhere,
        scratch_shapes=[
            pltpu.VMEM((NBLK, LOCAL, BLK), jnp.bfloat16),
            pltpu.VMEM((4, TOKEN, BLK), jnp.bfloat16),
            pltpu.VMEM((NBLK, LOCAL, BLK), jnp.bfloat16),
            pltpu.SemaphoreType.DMA((1,)),
            pltpu.SemaphoreType.DMA((6,)),
            pltpu.SemaphoreType.DMA((NBLK,)),
        ],
        compiler_params=pltpu.CompilerParams(vmem_limit_bytes=24 * 1024 * 1024),
        cost_estimate=pl.CostEstimate(
            flops=48 * 2 * BLK**3, bytes_accessed=7 * 2**20, transcendentals=0
        ),
    )(before, *third)


def after(values, *done):
    return list(lax.optimization_barrier((tuple(values), done))[0])


def per_device(band_blocks, site_mask, observed, band_offsets, site_gain):
    move = functools.partial(lax.ppermute, axis_name=AXES)
    swap = functools.partial(move, perm=SIBLING)
    own, low, high = prepare(band_blocks, site_mask, observed, band_offsets, site_gain)
    down1 = move(own, perm=FIRST_DOWN)
    low0, high0 = move(low, perm=ACROSS), move(high, perm=ACROSS)
    low1 = move(low0, perm=LEVEL_UP)
    low2 = move(low1, perm=UP)
    low3 = move(low2, perm=UP)
    (high0,) = after([high0], low3)
    high1 = move(high0, perm=LEVEL_UP)
    down1, low1, low2 = after([down1, low1, low2], high0)
    down2 = move(down1, perm=DOWN)
    down1, low1, low2, low3 = after([down1, low1, low2, low3], high1)
    swaps1 = [swap(x) for x in (down1, low1, low2, low3)]
    high2 = move(high1, perm=UP)
    (down2,) = after([down2], high1)
    down3 = move(down2, perm=DOWN)
    high1, down2 = after([high1, down2], down2)
    swaps2 = [swap(x) for x in (high1, down2)]
    high3 = move(high2, perm=UP)
    swaps3 = [swap(x) for x in (high2, down3)]
    low3, swaps1[3], down1, swaps1[0] = after([low3, swaps1[3], down1, swaps1[0]], high3)
    product, vector = pair(
        own,
        (low1, high1, swaps1[1], swaps2[0], down3, swaps3[1]),
        (low2, high2, swaps1[2], swaps3[0], down2, swaps2[1]),
        (low3, swaps1[3], down1, swaps1[0]),
    )
    matrix = last(product, (low3, high3, swaps1[3], swap(high3), down1, swaps1[0]))
    return matrix, vector


def solution(mesh):
    in_specs = (
        P("tm", None, "rows", None),
        P("tm", "rows"),
        P("tm", "rows"),
        P("tm", None),
        P("rows"),
    )
    out_specs = (P("tm", "rows", None), P("tm", "rows"))
    return jax.shard_map(
        per_device, mesh=mesh, in_specs=in_specs, out_specs=out_specs, check_vma=False
    )
```

time: 837 us -> 110 us (0.13)
  waiting for transfers between devices: 412 us -> 52.3 us
  blocking collectives: 191 us -> 0 us
  starting transfers between devices: 187 us -> 46.3 us
  matrix products: 23.1 us -> 0 us
  between operations: 14.1 us -> 0.85 us
  Pallas kernels: 0 us -> 8.71 us
    all_gather x2 -> x0, waiting for transfers between devices: 234 us -> none  [advance(): lax.all_gather(own_matrix, 'rows', axis=0, tiled=True)]
    all_gather x2 -> x0, blocking collectives: 191 us -> none  [advance(): lax.all_gather(own_offset, 'rows', axis=0, tiled=True)]
    ppermute x4 -> x20, starting transfers between devices: 187 us -> 46.3 us  [the longest x4 17 us: per_device(): swaps1 = [swap(x) for x in (down1, low1, low2, low3)]]
    ppermute x4 -> x20, waiting for transfers between devices: 178 us -> 52.3 us  [the longest x1 10.7 us: per_device(): low1 = move(low0, perm=LEVEL_UP)]
    dot_general x5 -> x0, matrix products: 23.1 us -> none  [the longest x2 18.3 us: combine_whole(): jnp.dot(own_matrix, earlier_matrix, preferred_element_type=jnp.float32)]
    pallas_call x0 -> x3, Pallas kernels: none -> 8.71 us  [the longest x1 3.59 us: pair(): pl.pallas_call(pair_kernel, out_shape=[jax.ShapeDtypeStruct((NBLK, LOCAL,...]
  transfers between devices with their start and end apart: 6 -> 20, of which waited for: 5 -> 8; matrix products, arithmetic and copies ran while one was open for 0% -> 0% of each run, Pallas kernels for 0% -> 3%
where the time goes in v2:
time: 110 us; the launch traced here: 109 us
  waiting for transfers between devices  52.3 us (48%)
  starting transfers between devices  46.3 us (42%)
  Pallas kernels  8.71 us (8%)
  local copies, waits for them, and re-layouts  1.13 us (1%)
    ppermute x4, starting transfers between devices, per_device(): swaps1 = [swap(x) for x in (down1, low1, low2, low3)]  17 us
    ppermute x1, waiting for transfers between devices, per_device(): low1 = move(low0, perm=LEVEL_UP)  10.7 us
    ppermute x1, waiting for transfers between devices, per_device(): low2 = move(low1, perm=UP)  10 us
    ppermute x1, waiting for transfers between devices, per_device(): low3 = move(low2, perm=UP)  10 us
    ppermute x1, starting transfers between devices, per_device(): swap(high3)  9.68 us
    ppermute x1, waiting for transfers between devices, per_device(): high1 = move(high0, perm=LEVEL_UP)  8.48 us
    ppermute x1, starting transfers between devices, per_device(): down1 = move(own, perm=FIRST_DOWN)  8.11 us
    ppermute x1, starting transfers between devices, per_device(): down3 = move(down2, perm=DOWN)  5.71 us
  transfers between devices with their start and end apart: 20, of which 8 were waited for; matrix products, arithmetic and copies ran while one was open for 0% of the time, Pallas kernels for 3%

profile of v2, /device:TPU:1, one launch (start us, length us, event | category | flops | bytes accessed | tf_op | source)
XLA Modules:
  0.0 109.3 jit_solution(1232369429910858631)
XLA Ops:
  0.6 2.6 %shard_map.68 = (bf16[1552,256]{1,0:T(8,128)(2,1)}, bf16[400,256]{1,0:T(8,128)(2,1)}, bf16[1152,256]{1,0:T(8,128)(2,1)}) custom-call(s32[1,3]{1,0:T(1,128)} %offsets_ref.1, bf16[1,3,512,256]{3,2,1,0:T(8,128)(2,1)} %band_ref.1, s32[1,512]{1,0:T(1,128)} %mask_ref.1, f32[1,512]{1,0:T(1,128)} %observed_ref.1, f32[1,512]{1,0:T(1,128)} %bitcast.1), custom_call_target="tpu_custom_call" | custom-call | tf_op jit(solution)/shard_map/pallas_call | solution.py:78
  3.2 1.6 %collective-permute-start.1 = (bf16[400,256]{1,0:T(8,128)(2,1)}, bf16[400,256]{1,0:T(8,128)(2,1)S(1)}, u32[]{:S(2)}, u32[]{:S(2)}) collective-permute-start(bf16[400,256]{1,0:T(8,128)(2,1)} %get-tuple-element.23), channel_id=1, source_target_pairs={{0,0},{1,1},{2,2},{3,3},{4,4},{5,5},{6,6},{7,7},{8,8},{9,9},{10,10... | collective-permute-start | bytes 614408 | tf_op jit(solution)/shard_map/ppermute | solution.py:316
  4.8 8.1 %collective-permute-start = (bf16[1552,256]{1,0:T(8,128)(2,1)}, bf16[1552,256]{1,0:T(8,128)(2,1)S(1)}, u32[]{:S(2)}, u32[]{:S(2)}) collective-permute-start(bf16[1552,256]{1,0:T(8,128)(2,1)} %get-tuple-element.22.refs_0_), channel_id=1, source_target_pairs={{244,0},{245,1},{246,2},{247,3},{248,4},{249,5},{250,6},{251,7},{2... | collective-permute-start | bytes 2383880 | tf_op jit(solution)/shard_map/ppermute | solution.py:315
  12.9 0.0 collective-permute-done.1
  12.9 0.0 collective-permute-start.2
  12.9 1.7 %collective-permute-start.4 = (bf16[1152,256]{1,0:T(8,128)(2,1)}, bf16[1152,256]{1,0:T(8,128)(2,1)S(1)}, u32[]{:S(2)}, u32[]{:S(2)}) collective-permute-start(bf16[1152,256]{1,0:T(8,128)(2,1)} %get-tuple-element.24), channel_id=1, source_target_pairs={{0,0},{1,1},{2,2},{3,3},{4,4},{5,5},{6,6},{7,7},{8,8},{9,9},{10,10... | collective-permute-start | bytes 1769480 | tf_op jit(solution)/shard_map/ppermute | solution.py:316
  14.6 10.7 %collective-permute-done.2.refs_1_ = bf16[400,256]{1,0:T(8,128)(2,1)S(1)} collective-permute-done((bf16[400,256]{1,0:T(8,128)(2,1)S(1)}, bf16[400,256]{1,0:T(8,128)(2,1)S(1)}, u32[]{:S(2)}, u32[]{:S(2)}) %collective-permute-start.2) | collective-permute-done | bytes 204832 | tf_op jit(solution)/shard_map/ppermute | solution.py:317
  25.3 0.0 collective-permute-start.3
  25.3 10.0 %collective-permute-done.3.refs_7_ = bf16[400,256]{1,0:T(8,128)(2,1)S(1)} collective-permute-done((bf16[400,256]{1,0:T(8,128)(2,1)S(1)}, bf16[400,256]{1,0:T(8,128)(2,1)S(1)}, u32[]{:S(2)}, u32[]{:S(2)}) %collective-permute-start.3) | collective-permute-done | bytes 204832 | tf_op jit(solution)/shard_map/ppermute | solution.py:318
  35.4 0.0 collective-permute-start.5
  35.4 0.0 collective-permute-done.4
  35.4 10.0 %collective-permute-done.5.refs_13_.refs_1_ = bf16[400,256]{1,0:T(8,128)(2,1)S(1)} collective-permute-done((bf16[400,256]{1,0:T(8,128)(2,1)S(1)}, bf16[400,256]{1,0:T(8,128)(2,1)S(1)}, u32[]{:S(2)}, u32[]{:S(2)}) %collective-permute-start.5) | collective-permute-done | bytes 204832 | tf_op jit(solution)/shard_map/ppermute | solution.py:319
  45.4 0.0 collective-permute-done.refs_15_.refs_5_
  45.4 0.0 collective-permute-start.7
  45.4 1.5 %collective-permute-start.6 = (bf16[1152,256]{1,0:T(8,128)(2,1)S(1)}, bf16[1152,256]{1,0:T(8,128)(2,1)S(1)}, u32[]{:S(2)}, u32[]{:S(2)}) collective-permute-start(bf16[1152,256]{1,0:T(8,128)(2,1)S(1)} %collective-permute-done.4), channel_id=1, source_target_pairs={{14,0},{15,1},{12,2},{13,3},{0,4},{1,5},{2,6},{3,7},{4,8},{5,9},{6... | collective-permute-start | bytes 1769480 | tf_op jit(solution)/shard_map/ppermute | solution.py:321
  46.9 8.5 %collective-permute-done.6.refs_2_ = bf16[1152,256]{1,0:T(8,128)(2,1)S(1)} collective-permute-done((bf16[1152,256]{1,0:T(8,128)(2,1)S(1)}, bf16[1152,256]{1,0:T(8,128)(2,1)S(1)}, u32[]{:S(2)}, u32[]{:S(2)}) %collective-permute-start.6) | collective-permute-done | bytes 589856 | tf_op jit(solution)/shard_map/ppermute | solution.py:321
  55.4 2.8 %collective-permute-done.7.refs_11_ = bf16[1552,256]{1,0:T(8,128)(2,1)S(1)} collective-permute-done((bf16[1552,256]{1,0:T(8,128)(2,1)S(1)}, bf16[1552,256]{1,0:T(8,128)(2,1)S(1)}, u32[]{:S(2)}, u32[]{:S(2)}) %collective-permute-start.7) | collective-permute-done | bytes 794656 | tf_op jit(solution)/shard_map/ppermute | solution.py:323
  58.1 5.7 %collective-permute-start.10 = (bf16[1552,256]{1,0:T(8,128)(2,1)S(1)}, bf16[1552,256]{1,0:T(8,128)(2,1)S(1)}, u32[]{:S(2)}, u32[]{:S(2)}) collective-permute-start(bf16[1552,256]{1,0:T(8,128)(2,1)S(1)} %collective-permute-done.7.refs_11_), channel_id=1, source_target_pairs={{4,0},{5,1},{6,2},{7,3},{8,4},{9,5},{10,6},{11,7},{12,8},{13,9},{1... | collective-permute-start | bytes 2383880 | tf_op jit(solution)/shard_map/ppermute | solution.py:328
  63.8 0.0 collective-permute-start.12
  63.8 8.0 %collective-permute-start.17 = (bf16[1552,256]{1,0:T(8,128)(2,1)S(1)}, bf16[1552,256]{1,0:T(8,128)(2,1)S(1)}, u32[]{:S(2)}, u32[]{:S(2)}) collective-permute-start(bf16[1552,256]{1,0:T(8,128)(2,1)S(1)} %collective-permute-done.refs_15_.refs_5_), channel_id=1, source_target_pairs={{0,1},{1,0},{2,3},{3,2},{4,5},{5,4},{6,7},{7,6},{8,9},{9,8},{10,11... | collective-permute-start | bytes 2383880 | tf_op jit(solution)/shard_map/ppermute | solution.py:325
  71.8 0.0 collective-permute-start.16
  71.8 0.5 collective-permute-start.13
  72.3 5.7 %collective-permute-done.12.refs_8_ = bf16[1152,256]{1,0:T(8,128)(2,1)S(1)} collective-permute-done((bf16[1152,256]{1,0:T(8,128)(2,1)S(1)}, bf16[1152,256]{1,0:T(8,128)(2,1)S(1)}, u32[]{:S(2)}, u32[]{:S(2)}) %collective-permute-start.12) | collective-permute-done | bytes 589856 | tf_op jit(solution)/shard_map/ppermute | solution.py:326
  78.0 0.0 collective-permute-start.18
  78.0 0.0 collective-permute-done.16.refs_14_.refs_3_
  78.0 8.6 %collective-permute-start.8 = (bf16[400,256]{1,0:T(8,128)(2,1)S(1)}, bf16[400,256]{1,0:T(8,128)(2,1)S(1)}, u32[]{:S(2)}, u32[]{:S(2)}) collective-permute-start(bf16[400,256]{1,0:T(8,128)(2,1)S(1)} %collective-permute-done.2.refs_1_), channel_id=1, source_target_pairs={{0,1},{1,0},{2,3},{3,2},{4,5},{5,4},{6,7},{7,6},{8,9},{9,8},{10,11... | collective-permute-start | bytes 614408 | tf_op jit(solution)/shard_map/ppermute | solution.py:325
  86.6 0.0 collective-permute-done.13.refs_9_
  86.6 0.1 collective-permute-start.15
  86.7 0.0 collective-permute-done.10.refs_5_
  86.7 0.4 collective-permute-start.11
  87.1 0.6 collective-permute-done.8.refs_3_
  87.7 0.4 collective-permute-start.9
  88.0 0.0 collective-permute-done.17.refs_16_.refs_6_
  88.0 0.1 collective-permute-start.14
  88.2 4.0 %collective-permute-done.18.refs_2_ = bf16[1152,256]{1,0:T(8,128)(2,1)S(1)} collective-permute-done((bf16[1152,256]{1,0:T(8,128)(2,1)S(1)}, bf16[1152,256]{1,0:T(8,128)(2,1)S(1)}, u32[]{:S(2)}, u32[]{:S(2)}) %collective-permute-start.18) | collective-permute-done | bytes 589856 | tf_op jit(solution)/shard_map/ppermute | solution.py:331
  92.2 9.7 %collective-permute-start.19 = (bf16[1152,256]{1,0:T(8,128)(2,1)S(1)}, bf16[1152,256]{1,0:T(8,128)(2,1)S(1)}, u32[]{:S(2)}, u32[]{:S(2)}) collective-permute-start(bf16[1152,256]{1,0:T(8,128)(2,1)S(1)} %collective-permute-done.18.refs_2_), channel_id=1, source_target_pairs={{0,1},{1,0},{2,3},{3,2},{4,5},{5,4},{6,7},{7,6},{8,9},{9,8},{10,11... | collective-permute-start | bytes 1769480 | tf_op jit(solution)/shard_map/ppermute | solution.py:340
  101.9 0.0 collective-permute-done.9.refs_4_
  101.9 0.0 collective-permute-done.15.refs_12_
  101.9 0.0 collective-permute-done.14.refs_10_
  101.9 0.0 collective-permute-done.11.refs_6_
  101.9 0.0 copy-start
  101.9 1.1 %copy-done = bf16[1552,256]{1,0:T(8,128)(2,1)S(1)} copy-done((bf16[1552,256]{1,0:T(8,128)(2,1)S(1)}, bf16[1552,256]{1,0:T(8,128)(2,1)}, u32[]{:S(2)}) %copy-start) | copy-done | bytes 794648
  103.0 3.6 %shard_map.69 = (bf16[8,512,256]{2,1,0:T(8,128)(2,1)S(1)}, bf16[1,512]{1,0:T(2,128)(2,1)}) custom-call(bf16[1552,256]{1,0:T(8,128)(2,1)S(1)} %copy-done, bf16[400,256]{1,0:T(8,128)(2,1)S(1)} %collective-permute-done.2.refs_1_, bf16[1152,256]{1,0:T(8,128)(2,1)S(1)} %collective-permute-done.6.refs_2_, bf16[400,256]{1,0:T(8,128)(2,1)S(1)} %collective-permute-done.8.refs_3_, ...), custom_call_target="tpu_custom_call" | custom-call | flops 3221225472 | bytes 10485760 | tf_op jit(solution)/shard_map/pallas_call | solution.py:225
  106.6 0.0 collective-permute-done.19.refs_4_
  106.7 2.5 %shard_map.70 = bf16[1,512,2048]{2,1,0:T(8,128)(2,1)} custom-call(bf16[8,512,256]{2,1,0:T(8,128)(2,1)S(1)} %get-tuple-element.40.refs_0_, bf16[400,256]{1,0:T(8,128)(2,1)S(1)} %collective-permute-done.5.refs_13_.refs_1_, bf16[1152,256]{1,0:T(8,128)(2,1)S(1)} %collective-permute-done.18.refs_2_, ...), custom_call_target="tpu_custom_call" | custom-call | flops 1610612736 | bytes 7340032 | tf_op jit(solution)/shard_map/pallas_call | solution.py:287
Async XLA Ops:
  3.2 9.7 %collective-permute-start.1 = (bf16[400,256]{1,0:T(8,128)(2,1)}, bf16[400,256]{1,0:T(8,128)(2,1)S(1)}, u32[]{:S(2)}, u32[]{:S(2)}) collective-permute-start(bf16[400,256]{1,0:T(8,128)(2,1)} %get-tuple-element.23), channel_id=1, source_target_pairs={{0,0},{1,1},{2,2},{3,3},{4,4},{5,5},{6,6},{7,7},{8,8},{9,9},{10,10... | collective-permute-start | bytes 614408 | tf_op jit(solution)/shard_map/ppermute | solution.py:316
  4.8 40.6 %collective-permute-start = (bf16[1552,256]{1,0:T(8,128)(2,1)}, bf16[1552,256]{1,0:T(8,128)(2,1)S(1)}, u32[]{:S(2)}, u32[]{:S(2)}) collective-permute-start(bf16[1552,256]{1,0:T(8,128)(2,1)} %get-tuple-element.22.refs_0_), channel_id=1, source_target_pairs={{244,0},{245,1},{246,2},{247,3},{248,4},{249,5},{250,6},{251,7},{2... | collective-permute-start | bytes 2383880 | tf_op jit(solution)/shard_map/ppermute | solution.py:315
  12.9 12.4 %collective-permute-start.2 = (bf16[400,256]{1,0:T(8,128)(2,1)S(1)}, bf16[400,256]{1,0:T(8,128)(2,1)S(1)}, u32[]{:S(2)}, u32[]{:S(2)}) collective-permute-start(bf16[400,256]{1,0:T(8,128)(2,1)S(1)} %collective-permute-done.1), channel_id=1, source_target_pairs={{14,0},{15,1},{12,2},{13,3},{0,4},{1,5},{2,6},{3,7},{4,8},{5,9},{6... | collective-permute-start | bytes 614408 | tf_op jit(solution)/shard_map/ppermute | solution.py:317
  12.9 22.5 %collective-permute-start.4 = (bf16[1152,256]{1,0:T(8,128)(2,1)}, bf16[1152,256]{1,0:T(8,128)(2,1)S(1)}, u32[]{:S(2)}, u32[]{:S(2)}) collective-permute-start(bf16[1152,256]{1,0:T(8,128)(2,1)} %get-tuple-element.24), channel_id=1, source_target_pairs={{0,0},{1,1},{2,2},{3,3},{4,4},{5,5},{6,6},{7,7},{8,8},{9,9},{10,10... | collective-permute-start | bytes 1769480 | tf_op jit(solution)/shard_map/ppermute | solution.py:316
  25.3 10.0 %collective-permute-start.3 = (bf16[400,256]{1,0:T(8,128)(2,1)S(1)}, bf16[400,256]{1,0:T(8,128)(2,1)S(1)}, u32[]{:S(2)}, u32[]{:S(2)}) collective-permute-start(bf16[400,256]{1,0:T(8,128)(2,1)S(1)} %collective-permute-done.2.refs_1_), channel_id=1, source_target_pairs={{254,0},{255,1},{252,2},{253,3},{0,4},{1,5},{2,6},{3,7},{4,8},{5,9... | collective-permute-start | bytes 614408 | tf_op jit(solution)/shard_map/ppermute | solution.py:318
  35.4 10.0 %collective-permute-start.5 = (bf16[400,256]{1,0:T(8,128)(2,1)S(1)}, bf16[400,256]{1,0:T(8,128)(2,1)S(1)}, u32[]{:S(2)}, u32[]{:S(2)}) collective-permute-start(bf16[400,256]{1,0:T(8,128)(2,1)S(1)} %collective-permute-done.3.refs_7_), channel_id=1, source_target_pairs={{254,0},{255,1},{252,2},{253,3},{0,4},{1,5},{2,6},{3,7},{4,8},{5,9... | collective-permute-start | bytes 614408 | tf_op jit(solution)/shard_map/ppermute | solution.py:319
  45.4 12.7 %collective-permute-start.7 = (bf16[1552,256]{1,0:T(8,128)(2,1)S(1)}, bf16[1552,256]{1,0:T(8,128)(2,1)S(1)}, u32[]{:S(2)}, u32[]{:S(2)}) collective-permute-start(bf16[1552,256]{1,0:T(8,128)(2,1)S(1)} %collective-permute-done.refs_15_.refs_5_), channel_id=1, source_target_pairs={{4,0},{5,1},{6,2},{7,3},{8,4},{9,5},{10,6},{11,7},{12,8},{13,9},{1... | collective-permute-start | bytes 2383880 | tf_op jit(solution)/shard_map/ppermute | solution.py:323
  45.4 9.9 %collective-permute-start.6 = (bf16[1152,256]{1,0:T(8,128)(2,1)S(1)}, bf16[1152,256]{1,0:T(8,128)(2,1)S(1)}, u32[]{:S(2)}, u32[]{:S(2)}) collective-permute-start(bf16[1152,256]{1,0:T(8,128)(2,1)S(1)} %collective-permute-done.4), channel_id=1, source_target_pairs={{14,0},{15,1},{12,2},{13,3},{0,4},{1,5},{2,6},{3,7},{4,8},{5,9},{6... | collective-permute-start | bytes 1769480 | tf_op jit(solution)/shard_map/ppermute | solution.py:321
  58.1 28.6 %collective-permute-start.10 = (bf16[1552,256]{1,0:T(8,128)(2,1)S(1)}, bf16[1552,256]{1,0:T(8,128)(2,1)S(1)}, u32[]{:S(2)}, u32[]{:S(2)}) collective-permute-start(bf16[1552,256]{1,0:T(8,128)(2,1)S(1)} %collective-permute-done.7.refs_11_), channel_id=1, source_target_pairs={{4,0},{5,1},{6,2},{7,3},{8,4},{9,5},{10,6},{11,7},{12,8},{13,9},{1... | collective-permute-start | bytes 2383880 | tf_op jit(solution)/shard_map/ppermute | solution.py:328
  63.8 14.2 %collective-permute-start.12 = (bf16[1152,256]{1,0:T(8,128)(2,1)S(1)}, bf16[1152,256]{1,0:T(8,128)(2,1)S(1)}, u32[]{:S(2)}, u32[]{:S(2)}) collective-permute-start(bf16[1152,256]{1,0:T(8,128)(2,1)S(1)} %collective-permute-done.6.refs_2_), channel_id=1, source_target_pairs={{254,0},{255,1},{252,2},{253,3},{0,4},{1,5},{2,6},{3,7},{4,8},{5,9... | collective-permute-start | bytes 1769480 | tf_op jit(solution)/shard_map/ppermute | solution.py:326
  63.8 24.2 %collective-permute-start.17 = (bf16[1552,256]{1,0:T(8,128)(2,1)S(1)}, bf16[1552,256]{1,0:T(8,128)(2,1)S(1)}, u32[]{:S(2)}, u32[]{:S(2)}) collective-permute-start(bf16[1552,256]{1,0:T(8,128)(2,1)S(1)} %collective-permute-done.refs_15_.refs_5_), channel_id=1, source_target_pairs={{0,1},{1,0},{2,3},{3,2},{4,5},{5,4},{6,7},{7,6},{8,9},{9,8},{10,11... | collective-permute-start | bytes 2383880 | tf_op jit(solution)/shard_map/ppermute | solution.py:325
  71.8 6.2 %collective-permute-start.16 = (bf16[400,256]{1,0:T(8,128)(2,1)S(1)}, bf16[400,256]{1,0:T(8,128)(2,1)S(1)}, u32[]{:S(2)}, u32[]{:S(2)}) collective-permute-start(bf16[400,256]{1,0:T(8,128)(2,1)S(1)} %collective-permute-done.5.refs_13_.refs_1_), channel_id=1, source_target_pairs={{0,1},{1,0},{2,3},{3,2},{4,5},{5,4},{6,7},{7,6},{8,9},{9,8},{10,11... | collective-permute-start | bytes 614408 | tf_op jit(solution)/shard_map/ppermute | solution.py:325
  71.8 14.8 %collective-permute-start.13 = (bf16[400,256]{1,0:T(8,128)(2,1)S(1)}, bf16[400,256]{1,0:T(8,128)(2,1)S(1)}, u32[]{:S(2)}, u32[]{:S(2)}) collective-permute-start(bf16[400,256]{1,0:T(8,128)(2,1)S(1)} %collective-permute-done.3.refs_7_), channel_id=1, source_target_pairs={{0,1},{1,0},{2,3},{3,2},{4,5},{5,4},{6,7},{7,6},{8,9},{9,8},{10,11... | collective-permute-start | bytes 614408 | tf_op jit(solution)/shard_map/ppermute | solution.py:325
  78.0 14.2 %collective-permute-start.18 = (bf16[1152,256]{1,0:T(8,128)(2,1)S(1)}, bf16[1152,256]{1,0:T(8,128)(2,1)S(1)}, u32[]{:S(2)}, u32[]{:S(2)}) collective-permute-start(bf16[1152,256]{1,0:T(8,128)(2,1)S(1)} %collective-permute-done.12.refs_8_), channel_id=1, source_target_pairs={{254,0},{255,1},{252,2},{253,3},{0,4},{1,5},{2,6},{3,7},{4,8},{5,9... | collective-permute-start | bytes 1769480 | tf_op jit(solution)/shard_map/ppermute | solution.py:331
  78.0 9.6 %collective-permute-start.8 = (bf16[400,256]{1,0:T(8,128)(2,1)S(1)}, bf16[400,256]{1,0:T(8,128)(2,1)S(1)}, u32[]{:S(2)}, u32[]{:S(2)}) collective-permute-start(bf16[400,256]{1,0:T(8,128)(2,1)S(1)} %collective-permute-done.2.refs_1_), channel_id=1, source_target_pairs={{0,1},{1,0},{2,3},{3,2},{4,5},{5,4},{6,7},{7,6},{8,9},{9,8},{10,11... | collective-permute-start | bytes 614408 | tf_op jit(solution)/shard_map/ppermute | solution.py:325
  86.6 15.3 %collective-permute-start.15 = (bf16[1552,256]{1,0:T(8,128)(2,1)S(1)}, bf16[1552,256]{1,0:T(8,128)(2,1)S(1)}, u32[]{:S(2)}, u32[]{:S(2)}) collective-permute-start(bf16[1552,256]{1,0:T(8,128)(2,1)S(1)} %collective-permute-done.7.refs_11_), channel_id=1, source_target_pairs={{0,1},{1,0},{2,3},{3,2},{4,5},{5,4},{6,7},{7,6},{8,9},{9,8},{10,11... | collective-permute-start | bytes 2383880 | tf_op jit(solution)/shard_map/ppermute | solution.py:330
  86.7 15.2 %collective-permute-start.11 = (bf16[1552,256]{1,0:T(8,128)(2,1)S(1)}, bf16[1552,256]{1,0:T(8,128)(2,1)S(1)}, u32[]{:S(2)}, u32[]{:S(2)}) collective-permute-start(bf16[1552,256]{1,0:T(8,128)(2,1)S(1)} %collective-permute-done.10.refs_5_), channel_id=1, source_target_pairs={{0,1},{1,0},{2,3},{3,2},{4,5},{5,4},{6,7},{7,6},{8,9},{9,8},{10,11... | collective-permute-start | bytes 2383880 | tf_op jit(solution)/shard_map/ppermute | solution.py:332
  87.7 14.2 %collective-permute-start.9 = (bf16[1152,256]{1,0:T(8,128)(2,1)S(1)}, bf16[1152,256]{1,0:T(8,128)(2,1)S(1)}, u32[]{:S(2)}, u32[]{:S(2)}) collective-permute-start(bf16[1152,256]{1,0:T(8,128)(2,1)S(1)} %collective-permute-done.6.refs_2_), channel_id=1, source_target_pairs={{0,1},{1,0},{2,3},{3,2},{4,5},{5,4},{6,7},{7,6},{8,9},{9,8},{10,11... | collective-permute-start | bytes 1769480 | tf_op jit(solution)/shard_map/ppermute | solution.py:330
  88.0 13.9 %collective-permute-start.14 = (bf16[1152,256]{1,0:T(8,128)(2,1)S(1)}, bf16[1152,256]{1,0:T(8,128)(2,1)S(1)}, u32[]{:S(2)}, u32[]{:S(2)}) collective-permute-start(bf16[1152,256]{1,0:T(8,128)(2,1)S(1)} %collective-permute-done.12.refs_8_), channel_id=1, source_target_pairs={{0,1},{1,0},{2,3},{3,2},{4,5},{5,4},{6,7},{7,6},{8,9},{9,8},{10,11... | collective-permute-start | bytes 1769480 | tf_op jit(solution)/shard_map/ppermute | solution.py:332
  92.2 14.4 %collective-permute-start.19 = (bf16[1152,256]{1,0:T(8,128)(2,1)S(1)}, bf16[1152,256]{1,0:T(8,128)(2,1)S(1)}, u32[]{:S(2)}, u32[]{:S(2)}) collective-permute-start(bf16[1152,256]{1,0:T(8,128)(2,1)S(1)} %collective-permute-done.18.refs_2_), channel_id=1, source_target_pairs={{0,1},{1,0},{2,3},{3,2},{4,5},{5,4},{6,7},{7,6},{8,9},{9,8},{10,11... | collective-permute-start | bytes 1769480 | tf_op jit(solution)/shard_map/ppermute | solution.py:340
  101.9 1.1 %copy-start = (bf16[1552,256]{1,0:T(8,128)(2,1)S(1)}, bf16[1552,256]{1,0:T(8,128)(2,1)}, u32[]{:S(2)}) copy-start(bf16[1552,256]{1,0:T(8,128)(2,1)} %get-tuple-element.22.refs_0_) | copy-start | bytes 2383876

commit v3 on v0

v3 whole, which is shorter than its diff:
```python
import functools

import jax
import jax.numpy as jnp
from jax import lax
from jax.experimental import pallas as pl
from jax.experimental.pallas import tpu as pltpu
from jax.sharding import PartitionSpec as P

BLK = 256
NBLK = 8
NBAND = 3
STEPS = 64
LOCAL = 512
TILE = 16
TOKEN = TILE + NBAND * LOCAL
AXES = ("tm", "rows")


def route(up, down):
    pairs = []
    for step in range(STEPS):
        for half in range(2):
            for core, source in enumerate((up, down)):
                from_step, from_half = source(step, half)
                pairs.append(
                    ((from_step % STEPS) * 4 + from_half * 2 + core, step * 4 + half * 2 + core)
                )
    return pairs


def above(t, h):
    return t + 1, h if t % 4 < 3 else 1 - h


def below(t, h):
    return t - 1, h if t % 4 > 0 else 1 - h


HOPS = (
    route(
        lambda t, h: (t - 4, h) if t % 4 == 3 else (t, h),
        lambda t, h: (t - 3, h if t % 4 < 3 else 1 - h),
    ),
    route(lambda t, h: (t - 1, h) if t % 4 > 0 else (t + 3, 1 - h), above),
    route(below, above),
    route(below, lambda t, h: (t, h)),
)
SIBLING = [(i, i ^ 1) for i in range(STEPS * 4)]


def prepare_kernel(offsets_ref, band_ref, mask_ref, observed_ref, gain_ref, token_ref):
    flag = mask_ref[...].astype(jnp.float32)
    gain = gain_ref[...]
    factor = 1.0 - gain * flag
    vector = gain * flag * observed_ref[...]
    row = lax.broadcasted_iota(jnp.int32, (TILE, BLK), 0)
    lane = lax.broadcasted_iota(jnp.int32, (TILE, BLK), 1)
    tile = jnp.where(row == 0, jnp.broadcast_to(vector[:, :BLK], (TILE, BLK)), 0.0)
    tile = jnp.where(row == 1, jnp.broadcast_to(vector[:, BLK:], (TILE, BLK)), tile)
    for j in range(NBAND):
        shift = offsets_ref[0, j].astype(jnp.float32)
        tile = jnp.where((row == 2) & (lane == j), shift, tile)
    token_ref[:TILE, :] = tile.astype(jnp.bfloat16)
    for i in range(LOCAL // 128):
        column = jnp.transpose(
            jnp.broadcast_to(factor[:, i * 128 : (i + 1) * 128], (128, 128))
        )
        for j in range(NBAND):
            for side in range(2):
                lanes = slice(side * 128, side * 128 + 128)
                block = band_ref[0, j, i * 128 : (i + 1) * 128, lanes].astype(jnp.float32)
                top = TILE + j * LOCAL + i * 128
                token_ref[top : top + 128, lanes] = (column * block).astype(jnp.bfloat16)


def prepare(band, mask, observed, offsets, gain):
    vmem = pl.BlockSpec(memory_space=pltpu.VMEM)
    return pl.pallas_call(
        prepare_kernel,
        out_shape=jax.ShapeDtypeStruct((TOKEN, BLK), jnp.bfloat16),
        in_specs=[pl.BlockSpec(memory_space=pltpu.SMEM)] + [vmem] * 4,
        out_specs=vmem,
    )(offsets, band, mask, observed, gain.reshape(1, LOCAL))


def tile_of(ref):
    return ref[:TILE, :].astype(jnp.float32)


def shifts_of(tile):
    row = lax.broadcasted_iota(jnp.int32, (TILE, BLK), 0)
    lane = lax.broadcasted_iota(jnp.int32, (TILE, BLK), 1)
    return [
        jnp.sum(jnp.where((row == 2) & (lane == j), tile, 0.0)).astype(jnp.int32)
        for j in range(NBAND)
    ]


def gather(refs, whole, distance, sems):
    step, place = lax.axis_index("tm"), lax.axis_index("rows")
    half = place // 2
    side = jnp.where(step % 4 >= distance, half, 1 - half)
    groups = [2 * side, 2 * side + 1, 2 * (1 - side) + 1, 2 * (1 - side)]
    rows = whole.shape[1]
    pairs = [
        [
            pltpu.make_async_copy(refs[4 * core + n].at[0:rows], whole.at[groups[n]], sems.at[n])
            for n in range(4)
        ]
        for core in range(2)
    ]

    def start():
        for core in range(2):

            @pl.when(place % 2 == core)
            def _():
                for copy in pairs[core]:
                    copy.start()

    def wait():
        for copy in pairs[0]:
            copy.wait()

    return start, wait


def column_of(source, earlier, shifts, c):
    product = None
    for j in range(NBAND):
        k = lax.rem(c - shifts[j] + NBLK, NBLK)
        at = pl.multiple_of(TILE + (2 * j + k % 2) * BLK, TILE)
        term = jnp.dot(
            source[k], earlier[k // 2, pl.ds(at, BLK), :], preferred_element_type=jnp.float32
        )
        product = term if product is None else product + term
    return product


def vector_of(tiles, c):
    return tiles[c // 2][c % 2 : c % 2 + 1, :]


def place_kernel(own_ref, bare_ref, vector_ref):
    place = lax.axis_index("rows")
    tile = tile_of(own_ref)
    shifts = shifts_of(tile)
    bare_ref[...] = jnp.zeros_like(bare_ref)
    for j in range(NBAND):
        for r in range(2):
            target = lax.rem(2 * place + r + shifts[j] + NBLK, NBLK)
            at = TILE + (2 * j + r) * BLK
            bare_ref[target, r * BLK : (r + 1) * BLK, :] = own_ref[at : at + BLK, :]
    for r in range(2):
        vector_ref[:, r * BLK : (r + 1) * BLK] = tile[r : r + 1, :]


def place_blocks(own):
    vmem = pl.BlockSpec(memory_space=pltpu.VMEM)
    return pl.pallas_call(
        place_kernel,
        out_shape=[
            jax.ShapeDtypeStruct((NBLK, LOCAL, BLK), jnp.bfloat16),
            jax.ShapeDtypeStruct((1, LOCAL), jnp.float32),
        ],
        in_specs=[vmem],
        out_specs=[vmem, vmem],
        cost_estimate=pl.CostEstimate(flops=0, bytes_accessed=3 * 2**20, transcendentals=0),
    )(own)


def pair_kernel(*refs):
    bare_ref, first, second = refs[0], refs[1:9], refs[9:17]
    product_ref, total = refs[17:19]
    near, far, bare, level, bare_sem, near_sems, far_sems = refs[19:]
    step, place = lax.axis_index("tm"), lax.axis_index("rows")
    near_start, near_wait = gather(first, near, 1, near_sems)
    far_start, far_wait = gather(second, far, 2, far_sems)
    bare_copy = pltpu.make_async_copy(bare_ref, bare, bare_sem.at[0])
    bare_copy.start()
    near_start()
    far_start()

    total[...] = jnp.zeros_like(total)
    bare_copy.wait()
    near_wait()

    @pl.when(step >= 1)
    def _():
        tiles = [tile_of(near.at[g]) for g in range(4)]
        shifts = shifts_of(tiles[0])
        for c in range(NBLK):
            level[c] = column_of(bare, near, shifts, c).astype(jnp.bfloat16)
            total[...] += bare[c].astype(jnp.float32) * vector_of(tiles, c)

    @pl.when(step < 1)
    def _():
        level[...] = bare[...]

    far_wait()

    @pl.when(step >= 2)
    def _():
        tiles = [tile_of(far.at[g]) for g in range(4)]
        shifts = shifts_of(tiles[0])
        for c in range(NBLK):
            product_ref[c] = column_of(level, far, shifts, c).astype(jnp.bfloat16)
            total[...] += level[c].astype(jnp.float32) * vector_of(tiles, c)

    @pl.when(step < 2)
    def _():
        product_ref[...] = level[...]


def pair(bare, first, second):
    anywhere, vmem = pl.BlockSpec(memory_space=pl.ANY), pl.BlockSpec(memory_space=pltpu.VMEM)
    return pl.pallas_call(
        pair_kernel,
        out_shape=[
            jax.ShapeDtypeStruct((NBLK, LOCAL, BLK), jnp.bfloat16),
            jax.ShapeDtypeStruct((LOCAL, BLK), jnp.float32),
        ],
        in_specs=[anywhere] * 17,
        out_specs=[vmem, vmem],
        scratch_shapes=[
            pltpu.VMEM((4, TOKEN, BLK), jnp.bfloat16),
            pltpu.VMEM((4, TOKEN, BLK), jnp.bfloat16),
            pltpu.VMEM((NBLK, LOCAL, BLK), jnp.bfloat16),
            pltpu.VMEM((NBLK, LOCAL, BLK), jnp.bfloat16),
            pltpu.SemaphoreType.DMA((1,)),
            pltpu.SemaphoreType.DMA((4,)),
            pltpu.SemaphoreType.DMA((4,)),
        ],
        compiler_params=pltpu.CompilerParams(vmem_limit_bytes=24 * 1024 * 1024),
        cost_estimate=pl.CostEstimate(
            flops=96 * 2 * BLK**3, bytes_accessed=10 * 2**20, transcendentals=0
        ),
    )(bare, *first, *second)


def last_kernel(*refs):
    before_ref, total_ref, own_ref, third = refs[0], refs[1], refs[2], refs[3:11]
    matrix_ref, vector_ref = refs[11:13]
    before, earlier, result, before_sem, sems, out_sems = refs[13:]
    step = lax.axis_index("tm")
    before_copy = pltpu.make_async_copy(before_ref, before, before_sem.at[0])
    start, wait = gather(third, earlier, 3, sems)
    before_copy.start()
    start()
    before_copy.wait()
    wait()
    writes = [
        pltpu.make_async_copy(
            result.at[c], matrix_ref.at[0, :, c * BLK : (c + 1) * BLK], out_sems.at[c]
        )
        for c in range(NBLK)
    ]

    @pl.when(step >= 3)
    def _():
        tiles = [tile_of(earlier.at[g]) for g in range(4)]
        shifts = shifts_of(tiles[0])
        for c in range(NBLK):
            result[c] = column_of(before, earlier, shifts, c).astype(jnp.bfloat16)
            total_ref[...] += before[c].astype(jnp.float32) * vector_of(tiles, c)
            writes[c].start()

    @pl.when(step < 3)
    def _():
        for c in range(NBLK):
            result[c] = before[c]
            writes[c].start()

    value = total_ref[...]
    high = value.astype(jnp.bfloat16)
    low = (value - high.astype(jnp.float32)).astype(jnp.bfloat16)
    ones = jnp.ones((TILE, BLK), jnp.bfloat16)
    sums = sum(
        lax.dot_general(ones, part, (((1,), (1,)), ((), ())), preferred_element_type=jnp.float32)
        for part in (high, low)
    )
    for r in range(2):
        vector_ref[:, r * BLK : (r + 1) * BLK] = (
            sums[0:1, r * BLK : (r + 1) * BLK] + own_ref[:, r * BLK : (r + 1) * BLK]
        ).astype(jnp.bfloat16)
    for write in writes:
        write.wait()


def last(before, total, own, third):
    anywhere, vmem = pl.BlockSpec(memory_space=pl.ANY), pl.BlockSpec(memory_space=pltpu.VMEM)
    return pl.pallas_call(
        last_kernel,
        out_shape=[
            jax.ShapeDtypeStruct((1, LOCAL, NBLK * BLK), jnp.bfloat16),
            jax.ShapeDtypeStruct((1, LOCAL), jnp.bfloat16),
        ],
        grid=(1,),
        in_specs=[
            anywhere,
            pl.BlockSpec((LOCAL, BLK), lambda i: (0, 0)),
            pl.BlockSpec((1, LOCAL), lambda i: (0, 0)),
        ]
        + [anywhere] * 8,
        out_specs=[anywhere, pl.BlockSpec((1, LOCAL), lambda i: (0, 0))],
        scratch_shapes=[
            pltpu.VMEM((NBLK, LOCAL, BLK), jnp.bfloat16),
            pltpu.VMEM((4, TOKEN, BLK), jnp.bfloat16),
            pltpu.VMEM((NBLK, LOCAL, BLK), jnp.bfloat16),
            pltpu.SemaphoreType.DMA((1,)),
            pltpu.SemaphoreType.DMA((4,)),
            pltpu.SemaphoreType.DMA((NBLK,)),
        ],
        compiler_params=pltpu.CompilerParams(vmem_limit_bytes=24 * 1024 * 1024),
        cost_estimate=pl.CostEstimate(
            flops=48 * 2 * BLK**3, bytes_accessed=7 * 2**20, transcendentals=0
        ),
    )(before, total, own, *third)


def after(values, *done):
    return list(lax.optimization_barrier((tuple(values), done))[0])


def per_device(band_blocks, site_mask, observed, band_offsets, site_gain):
    move = functools.partial(lax.ppermute, axis_name=AXES)
    own = prepare(band_blocks, site_mask, observed, band_offsets, site_gain)
    bare, vector = place_blocks(own)
    sibling = move(own, perm=SIBLING)
    held = [[own, sibling]]
    for n, hop in enumerate(HOPS):
        a, b = held[-1]
        if n == 1:
            (a,) = after([a], sibling)
        if n == 2:
            (a,) = after([a], bare)
        held.append([move(a, perm=hop), move(b, perm=hop)])
    held = held[1:]
    swapped = []
    for n in range(3):
        a, b = after(held[n], held[n + 1][0])
        swapped.append([move(a, perm=SIBLING), move(b, perm=SIBLING)])
    product, total = pair(
        bare,
        held[1] + swapped[2] + swapped[1] + held[2],
        held[2] + swapped[1] + swapped[2] + held[1],
    )
    a, b = held[3]
    (b,) = after([b], product)
    held[3] = [a, b]
    swapped.append([move(a, perm=SIBLING), move(b, perm=SIBLING)])
    third = held[3] + swapped[0] + swapped[3] + held[0]
    return tuple(last(product, total, vector, third))


def solution(mesh):
    in_specs = (
        P("tm", None, "rows", None),
        P("tm", "rows"),
        P("tm", "rows"),
        P("tm", None),
        P("rows"),
    )
    out_specs = (P("tm", "rows", None), P("tm", "rows"))
    return jax.shard_map(
        per_device, mesh=mesh, in_specs=in_specs, out_specs=out_specs, check_vma=False
    )
```

time: 837 us -> 108 us (0.13)
  waiting for transfers between devices: 412 us -> 39.4 us
  blocking collectives: 191 us -> 0 us
  starting transfers between devices: 187 us -> 57.2 us
  matrix products: 23.1 us -> 0 us
  between operations: 14.1 us -> 0.88 us
  Pallas kernels: 0 us -> 8.66 us
    all_gather x2 -> x0, waiting for transfers between devices: 234 us -> none  [advance(): lax.all_gather(own_matrix, 'rows', axis=0, tiled=True)]
    all_gather x2 -> x0, blocking collectives: 191 us -> none  [advance(): lax.all_gather(own_offset, 'rows', axis=0, tiled=True)]
    ppermute x4 -> x17, waiting for transfers between devices: 178 us -> 39.4 us  [the longest x8 37.4 us: per_device(): held.append([move(a, perm=hop), move(b, perm=hop)])]
    ppermute x4 -> x17, starting transfers between devices: 187 us -> 57.2 us  [the longest x8 36.2 us: per_device(): held.append([move(a, perm=hop), move(b, perm=hop)])]
    dot_general x5 -> x0, matrix products: 23.1 us -> none  [the longest x2 18.3 us: combine_whole(): jnp.dot(own_matrix, earlier_matrix, preferred_element_type=jnp.float32)]
    pallas_call x0 -> x4, Pallas kernels: none -> 8.66 us  [the longest x1 2.69 us: place_blocks(): pl.pallas_call(place_kernel, out_shape=[jax.ShapeDtypeStruct((NBLK, LOCAL...]
  transfers between devices with their start and end apart: 6 -> 17, of which waited for: 5 -> 7; matrix products, arithmetic and copies ran while one was open for 0% -> 0% of each run, Pallas kernels for 0% -> 4%
where the time goes in v3:
time: 108 us
  starting transfers between devices  57.2 us (53%)
  waiting for transfers between devices  39.4 us (36%)
  Pallas kernels  8.66 us (8%)
  local copies, waits for them, and re-layouts  1.59 us (1%)
    ppermute x8, waiting for transfers between devices, per_device(): held.append([move(a, perm=hop), move(b, perm=hop)])  37.4 us
    ppermute x8, starting transfers between devices, per_device(): held.append([move(a, perm=hop), move(b, perm=hop)])  36.2 us
    ppermute x8, starting transfers between devices, per_device(): swapped.append([move(a, perm=SIBLING), move(b, perm=SIBLING)])  20.9 us
    pallas_call x1, Pallas kernels, place_blocks(): pl.pallas_call(place_kernel, out_shape=[jax.ShapeDtypeStruct((NBLK, LOCAL...  2.69 us
    pallas_call x1, Pallas kernels, last(): pl.pallas_call(last_kernel, out_shape=[jax.ShapeDtypeStruct((1, LOCAL, NB...  2.43 us
    pallas_call x1, Pallas kernels, prepare(): pl.pallas_call(prepare_kernel, out_shape=jax.ShapeDtypeStruct((TOKEN, BLK...  2.27 us
  transfers between devices with their start and end apart: 17, of which 7 were waited for; matrix products, arithmetic and copies ran while one was open for 0% of the time, Pallas kernels for 4%

profile of v3, /device:TPU:1, one launch (start us, length us, event | category | flops | bytes accessed | tf_op | source)
XLA Modules:
  0.0 107.6 jit_solution(3589610656166259684)
XLA Ops:
  0.6 2.3 %shard_map.68.own_ref = bf16[1552,256]{1,0:T(8,128)(2,1)} custom-call(s32[1,3]{1,0:T(1,128)} %offsets_ref.1, bf16[1,3,512,256]{3,2,1,0:T(8,128)(2,1)} %band_ref.1, s32[1,512]{1,0:T(1,128)} %mask_ref.1, f32[1,512]{1,0:T(1,128)} %observed_ref.1, f32[1,512]{1,0:T(1,128)} %bitcast.1), custom_call_target="tpu_custom_call" | custom-call | tf_op jit(solution)/shard_map/pallas_call | solution.py:79
  2.9 8.3 %collective-permute-start = (bf16[1552,256]{1,0:T(8,128)(2,1)}, bf16[1552,256]{1,0:T(8,128)(2,1)S(1)}, u32[]{:S(2)}, u32[]{:S(2)}) collective-permute-start(bf16[1552,256]{1,0:T(8,128)(2,1)} %shard_map.68.own_ref), channel_id=1, source_target_pairs={{0,0},{245,1},{2,2},{247,3},{4,4},{249,5},{6,6},{251,7},{8,8},{253... | collective-permute-start | bytes 2383880 | tf_op jit(solution)/shard_map/ppermute | solution.py:338
  11.2 0.1 collective-permute-start.1
  11.3 10.3 %collective-permute-done.refs_9_ = bf16[1552,256]{1,0:T(8,128)(2,1)S(1)} collective-permute-done((bf16[1552,256]{1,0:T(8,128)(2,1)}, bf16[1552,256]{1,0:T(8,128)(2,1)S(1)}, u32[]{:S(2)}, u32[]{:S(2)}) %collective-permute-start) | collective-permute-done | bytes 794656 | tf_op jit(solution)/shard_map/ppermute | solution.py:338
  21.6 0.0 collective-permute-done.1
  21.6 6.6 %collective-permute-start.2 = (bf16[1552,256]{1,0:T(8,128)(2,1)S(1)}, bf16[1552,256]{1,0:T(8,128)(2,1)S(1)}, u32[]{:S(2)}, u32[]{:S(2)}) collective-permute-start(bf16[1552,256]{1,0:T(8,128)(2,1)S(1)} %collective-permute-done.refs_9_), channel_id=1, source_target_pairs={{14,0},{5,1},{12,2},{7,3},{0,4},{9,5},{2,6},{11,7},{4,8},{13,9},{6... | collective-permute-start | bytes 2383880 | tf_op jit(solution)/shard_map/ppermute | solution.py:338
  28.2 1.9 %collective-permute-start.3 = (bf16[1552,256]{1,0:T(8,128)(2,1)S(1)}, bf16[1552,256]{1,0:T(8,128)(2,1)S(1)}, u32[]{:S(2)}, u32[]{:S(2)}) collective-permute-start(bf16[1552,256]{1,0:T(8,128)(2,1)S(1)} %collective-permute-done.1), channel_id=1, source_target_pairs={{0,0},{245,1},{2,2},{247,3},{4,4},{249,5},{6,6},{251,7},{8,8},{253... | collective-permute-start | bytes 2383880 | tf_op jit(solution)/shard_map/ppermute | solution.py:338
  30.1 2.7 %shard_map.69 = (bf16[8,512,256]{2,1,0:T(8,128)(2,1)}, f32[1,512]{1,0:T(1,128)}) custom-call(bf16[1552,256]{1,0:T(8,128)(2,1)} %shard_map.68.own_ref), custom_call_target="tpu_custom_call" | custom-call | bytes 3145728 | tf_op jit(solution)/shard_map/pallas_call | solution.py:161
  32.8 4.4 %collective-permute-done.2.refs_1_.refs_15_ = bf16[1552,256]{1,0:T(8,128)(2,1)S(1)} collective-permute-done((bf16[1552,256]{1,0:T(8,128)(2,1)S(1)}, bf16[1552,256]{1,0:T(8,128)(2,1)S(1)}, u32[]{:S(2)}, u32[]{:S(2)}) %collective-permute-start.2) | collective-permute-done | bytes 794656 | tf_op jit(solution)/shard_map/ppermute | solution.py:338
  37.2 7.3 %collective-permute-start.5 = (bf16[1552,256]{1,0:T(8,128)(2,1)S(1)}, bf16[1552,256]{1,0:T(8,128)(2,1)S(1)}, u32[]{:S(2)}, u32[]{:S(2)}) collective-permute-start(bf16[1552,256]{1,0:T(8,128)(2,1)S(1)} %collective-permute-done.2.refs_1_.refs_15_), channel_id=1, source_target_pairs={{254,0},{5,1},{252,2},{7,3},{0,4},{9,5},{2,6},{11,7},{4,8},{13,9},... | collective-permute-start | bytes 2383880 | tf_op jit(solution)/shard_map/ppermute | solution.py:338
  44.5 1.2 %collective-permute-done.3.refs_10_ = bf16[1552,256]{1,0:T(8,128)(2,1)S(1)} collective-permute-done((bf16[1552,256]{1,0:T(8,128)(2,1)S(1)}, bf16[1552,256]{1,0:T(8,128)(2,1)S(1)}, u32[]{:S(2)}, u32[]{:S(2)}) %collective-permute-start.3) | collective-permute-done | bytes 794656 | tf_op jit(solution)/shard_map/ppermute | solution.py:338
  45.7 3.3 %collective-permute-start.4 = (bf16[1552,256]{1,0:T(8,128)(2,1)S(1)}, bf16[1552,256]{1,0:T(8,128)(2,1)S(1)}, u32[]{:S(2)}, u32[]{:S(2)}) collective-permute-start(bf16[1552,256]{1,0:T(8,128)(2,1)S(1)} %collective-permute-done.3.refs_10_), channel_id=1, source_target_pairs={{14,0},{5,1},{12,2},{7,3},{0,4},{9,5},{2,6},{11,7},{4,8},{13,9},{6... | collective-permute-start | bytes 2383880 | tf_op jit(solution)/shard_map/ppermute | solution.py:338
  49.0 5.2 %collective-permute-done.5.refs_7_.refs_9_ = bf16[1552,256]{1,0:T(8,128)(2,1)S(1)} collective-permute-done((bf16[1552,256]{1,0:T(8,128)(2,1)S(1)}, bf16[1552,256]{1,0:T(8,128)(2,1)S(1)}, u32[]{:S(2)}, u32[]{:S(2)}) %collective-permute-start.5) | collective-permute-done | bytes 794656 | tf_op jit(solution)/shard_map/ppermute | solution.py:338
  54.2 0.7 collective-permute-start.7
  54.9 7.8 %collective-permute-done.4.refs_2_.refs_16_ = bf16[1552,256]{1,0:T(8,128)(2,1)S(1)} collective-permute-done((bf16[1552,256]{1,0:T(8,128)(2,1)S(1)}, bf16[1552,256]{1,0:T(8,128)(2,1)S(1)}, u32[]{:S(2)}, u32[]{:S(2)}) %collective-permute-start.4) | collective-permute-done | bytes 794656 | tf_op jit(solution)/shard_map/ppermute | solution.py:338
  62.8 7.3 %collective-permute-start.6 = (bf16[1552,256]{1,0:T(8,128)(2,1)S(1)}, bf16[1552,256]{1,0:T(8,128)(2,1)S(1)}, u32[]{:S(2)}, u32[]{:S(2)}) collective-permute-start(bf16[1552,256]{1,0:T(8,128)(2,1)S(1)} %collective-permute-done.4.refs_2_.refs_16_), channel_id=1, source_target_pairs={{254,0},{5,1},{252,2},{7,3},{0,4},{9,5},{2,6},{11,7},{4,8},{13,9},... | collective-permute-start | bytes 2383880 | tf_op jit(solution)/shard_map/ppermute | solution.py:338
  70.1 0.0 collective-permute-start.10
  70.1 0.5 collective-permute-start.11
  70.6 0.0 collective-permute-done.7.refs_3_
  70.6 8.5 %collective-permute-done.6.refs_8_.refs_10_ = bf16[1552,256]{1,0:T(8,128)(2,1)S(1)} collective-permute-done((bf16[1552,256]{1,0:T(8,128)(2,1)S(1)}, bf16[1552,256]{1,0:T(8,128)(2,1)S(1)}, u32[]{:S(2)}, u32[]{:S(2)}) %collective-permute-start.6) | collective-permute-done | bytes 794656 | tf_op jit(solution)/shard_map/ppermute | solution.py:338
  79.1 4.1 %collective-permute-start.8 = (bf16[1552,256]{1,0:T(8,128)(2,1)S(1)}, bf16[1552,256]{1,0:T(8,128)(2,1)S(1)}, u32[]{:S(2)}, u32[]{:S(2)}) collective-permute-start(bf16[1552,256]{1,0:T(8,128)(2,1)S(1)} %collective-permute-done.5.refs_7_.refs_9_), channel_id=1, source_target_pairs={{0,1},{1,0},{2,3},{3,2},{4,5},{5,4},{6,7},{7,6},{8,9},{9,8},{10,11... | collective-permute-start | bytes 2383880 | tf_op jit(solution)/shard_map/ppermute | solution.py:343
  83.2 0.0 collective-permute-start.9
  83.2 0.7 collective-permute-start.12
  83.9 0.0 collective-permute-done.10.refs_5_.refs_11_
  83.9 1.8 %collective-permute-start.13 = (bf16[1552,256]{1,0:T(8,128)(2,1)S(1)}, bf16[1552,256]{1,0:T(8,128)(2,1)S(1)}, u32[]{:S(2)}, u32[]{:S(2)}) collective-permute-start(bf16[1552,256]{1,0:T(8,128)(2,1)S(1)} %collective-permute-done.refs_9_), channel_id=1, source_target_pairs={{0,1},{1,0},{2,3},{3,2},{4,5},{5,4},{6,7},{7,6},{8,9},{9,8},{10,11... | collective-permute-start | bytes 2383880 | tf_op jit(solution)/shard_map/ppermute | solution.py:343
  85.8 0.0 collective-permute-done.11.refs_6_.refs_12_
  85.8 0.1 collective-permute-start.14
  85.9 0.0 collective-permute-done.8.refs_3_.refs_13_
  85.9 0.4 collective-permute-start.15
  86.3 0.0 collective-permute-done.9.refs_4_.refs_14_
  86.3 0.0 copy-start
  86.3 1.6 %copy-done = bf16[8,512,256]{2,1,0:T(8,128)(2,1)S(1)} copy-done((bf16[8,512,256]{2,1,0:T(8,128)(2,1)S(1)}, bf16[8,512,256]{2,1,0:T(8,128)(2,1)}, u32[]{:S(2)}) %copy-start) | copy-done | bytes 2097176
  87.9 0.0 copy-start.1
  87.9 1.3 %shard_map.70 = (bf16[8,512,256]{2,1,0:T(8,128)(2,1)S(1)}, f32[512,256]{1,0:T(8,128)S(1)}) custom-call(bf16[8,512,256]{2,1,0:T(8,128)(2,1)S(1)} %copy-done, bf16[1552,256]{1,0:T(8,128)(2,1)S(1)} %collective-permute-done.2.refs_1_.refs_15_, bf16[1552,256]{1,0:T(8,128)(2,1)S(1)} %collective-permute-done.4.refs_2_.refs_16_, ...), custom_call_target="tpu_custom_call" | custom-call | flops 3221225472 | bytes 10485760 | tf_op jit(solution)/shard_map/pallas_call | solution.py:218
  89.2 0.0 collective-permute-done.12.refs_4_
  89.2 14.0 %collective-permute-start.16 = (bf16[1552,256]{1,0:T(8,128)(2,1)S(1)}, bf16[1552,256]{1,0:T(8,128)(2,1)S(1)}, u32[]{:S(2)}, u32[]{:S(2)}) collective-permute-start(bf16[1552,256]{1,0:T(8,128)(2,1)S(1)} %collective-permute-done.12.refs_4_), channel_id=1, source_target_pairs={{0,1},{1,0},{2,3},{3,2},{4,5},{5,4},{6,7},{7,6},{8,9},{9,8},{10,11... | collective-permute-start | bytes 2383880 | tf_op jit(solution)/shard_map/ppermute | solution.py:352
  103.1 0.0 collective-permute-done.13.refs_5_
  103.1 0.0 collective-permute-done.14.refs_6_
  103.1 0.0 collective-permute-done.15.refs_7_
  103.1 1.9 %collective-permute-done.16.refs_8_ = bf16[1552,256]{1,0:T(8,128)(2,1)S(1)} collective-permute-done((bf16[1552,256]{1,0:T(8,128)(2,1)S(1)}, bf16[1552,256]{1,0:T(8,128)(2,1)S(1)}, u32[]{:S(2)}, u32[]{:S(2)}) %collective-permute-start.16) | collective-permute-done | bytes 794656 | tf_op jit(solution)/shard_map/ppermute | solution.py:352
  105.1 0.0 copy-done.1
  105.1 2.4 %shard_map.71 = (bf16[1,512,2048]{2,1,0:T(8,128)(2,1)}, bf16[1,512]{1,0:T(2,128)(2,1)}) custom-call(bf16[8,512,256]{2,1,0:T(8,128)(2,1)S(1)} %get-tuple-element.22.refs_0_, f32[512,256]{1,0:T(8,128)S(1)} %get-tuple-element.23.refs_1_, f32[1,512]{1,0:T(1,128)S(1)} %copy-done.1, bf16[1552,256]{1,0:T(8,128)(2,1)S(1)} %collective-permute-done.7.refs_3_, ...), custom_call_target="tpu_custom_call" | custom-call | flops 1610612736 | bytes 7340032 | tf_op jit(solution)/shard_map/pallas_call | solution.py:293
Async XLA Ops:
  2.9 18.7 %collective-permute-start = (bf16[1552,256]{1,0:T(8,128)(2,1)}, bf16[1552,256]{1,0:T(8,128)(2,1)S(1)}, u32[]{:S(2)}, u32[]{:S(2)}) collective-permute-start(bf16[1552,256]{1,0:T(8,128)(2,1)} %shard_map.68.own_ref), channel_id=1, source_target_pairs={{0,0},{245,1},{2,2},{247,3},{4,4},{249,5},{6,6},{251,7},{8,8},{253... | collective-permute-start | bytes 2383880 | tf_op jit(solution)/shard_map/ppermute | solution.py:338
  11.2 10.4 %collective-permute-start.1 = (bf16[1552,256]{1,0:T(8,128)(2,1)}, bf16[1552,256]{1,0:T(8,128)(2,1)S(1)}, u32[]{:S(2)}, u32[]{:S(2)}) collective-permute-start(bf16[1552,256]{1,0:T(8,128)(2,1)} %shard_map.68.own_ref), channel_id=1, source_target_pairs={{0,1},{1,0},{2,3},{3,2},{4,5},{5,4},{6,7},{7,6},{8,9},{9,8},{10,11... | collective-permute-start | bytes 2383880 | tf_op jit(solution)/shard_map/ppermute | solution.py:330
  21.6 15.6 %collective-permute-start.2 = (bf16[1552,256]{1,0:T(8,128)(2,1)S(1)}, bf16[1552,256]{1,0:T(8,128)(2,1)S(1)}, u32[]{:S(2)}, u32[]{:S(2)}) collective-permute-start(bf16[1552,256]{1,0:T(8,128)(2,1)S(1)} %collective-permute-done.refs_9_), channel_id=1, source_target_pairs={{14,0},{5,1},{12,2},{7,3},{0,4},{9,5},{2,6},{11,7},{4,8},{13,9},{6... | collective-permute-start | bytes 2383880 | tf_op jit(solution)/shard_map/ppermute | solution.py:338
  28.2 17.5 %collective-permute-start.3 = (bf16[1552,256]{1,0:T(8,128)(2,1)S(1)}, bf16[1552,256]{1,0:T(8,128)(2,1)S(1)}, u32[]{:S(2)}, u32[]{:S(2)}) collective-permute-start(bf16[1552,256]{1,0:T(8,128)(2,1)S(1)} %collective-permute-done.1), channel_id=1, source_target_pairs={{0,0},{245,1},{2,2},{247,3},{4,4},{249,5},{6,6},{251,7},{8,8},{253... | collective-permute-start | bytes 2383880 | tf_op jit(solution)/shard_map/ppermute | solution.py:338
  37.2 17.0 %collective-permute-start.5 = (bf16[1552,256]{1,0:T(8,128)(2,1)S(1)}, bf16[1552,256]{1,0:T(8,128)(2,1)S(1)}, u32[]{:S(2)}, u32[]{:S(2)}) collective-permute-start(bf16[1552,256]{1,0:T(8,128)(2,1)S(1)} %collective-permute-done.2.refs_1_.refs_15_), channel_id=1, source_target_pairs={{254,0},{5,1},{252,2},{7,3},{0,4},{9,5},{2,6},{11,7},{4,8},{13,9},... | collective-permute-start | bytes 2383880 | tf_op jit(solution)/shard_map/ppermute | solution.py:338
  45.7 17.0 %collective-permute-start.4 = (bf16[1552,256]{1,0:T(8,128)(2,1)S(1)}, bf16[1552,256]{1,0:T(8,128)(2,1)S(1)}, u32[]{:S(2)}, u32[]{:S(2)}) collective-permute-start(bf16[1552,256]{1,0:T(8,128)(2,1)S(1)} %collective-permute-done.3.refs_10_), channel_id=1, source_target_pairs={{14,0},{5,1},{12,2},{7,3},{0,4},{9,5},{2,6},{11,7},{4,8},{13,9},{6... | collective-permute-start | bytes 2383880 | tf_op jit(solution)/shard_map/ppermute | solution.py:338
  54.2 16.4 %collective-permute-start.7 = (bf16[1552,256]{1,0:T(8,128)(2,1)S(1)}, bf16[1552,256]{1,0:T(8,128)(2,1)S(1)}, u32[]{:S(2)}, u32[]{:S(2)}) collective-permute-start(bf16[1552,256]{1,0:T(8,128)(2,1)S(1)} %collective-permute-done.5.refs_7_.refs_9_), channel_id=1, source_target_pairs={{254,0},{1,1},{252,2},{3,3},{0,4},{5,5},{2,6},{7,7},{4,8},{9,9},{6... | collective-permute-start | bytes 2383880 | tf_op jit(solution)/shard_map/ppermute | solution.py:338
  62.8 16.4 %collective-permute-start.6 = (bf16[1552,256]{1,0:T(8,128)(2,1)S(1)}, bf16[1552,256]{1,0:T(8,128)(2,1)S(1)}, u32[]{:S(2)}, u32[]{:S(2)}) collective-permute-start(bf16[1552,256]{1,0:T(8,128)(2,1)S(1)} %collective-permute-done.4.refs_2_.refs_16_), channel_id=1, source_target_pairs={{254,0},{5,1},{252,2},{7,3},{0,4},{9,5},{2,6},{11,7},{4,8},{13,9},... | collective-permute-start | bytes 2383880 | tf_op jit(solution)/shard_map/ppermute | solution.py:338
  70.1 13.8 %collective-permute-start.10 = (bf16[1552,256]{1,0:T(8,128)(2,1)S(1)}, bf16[1552,256]{1,0:T(8,128)(2,1)S(1)}, u32[]{:S(2)}, u32[]{:S(2)}) collective-permute-start(bf16[1552,256]{1,0:T(8,128)(2,1)S(1)} %collective-permute-done.2.refs_1_.refs_15_), channel_id=1, source_target_pairs={{0,1},{1,0},{2,3},{3,2},{4,5},{5,4},{6,7},{7,6},{8,9},{9,8},{10,11... | collective-permute-start | bytes 2383880 | tf_op jit(solution)/shard_map/ppermute | solution.py:343
  70.1 15.7 %collective-permute-start.11 = (bf16[1552,256]{1,0:T(8,128)(2,1)S(1)}, bf16[1552,256]{1,0:T(8,128)(2,1)S(1)}, u32[]{:S(2)}, u32[]{:S(2)}) collective-permute-start(bf16[1552,256]{1,0:T(8,128)(2,1)S(1)} %collective-permute-done.4.refs_2_.refs_16_), channel_id=1, source_target_pairs={{0,1},{1,0},{2,3},{3,2},{4,5},{5,4},{6,7},{7,6},{8,9},{9,8},{10,11... | collective-permute-start | bytes 2383880 | tf_op jit(solution)/shard_map/ppermute | solution.py:343
  79.1 6.8 %collective-permute-start.8 = (bf16[1552,256]{1,0:T(8,128)(2,1)S(1)}, bf16[1552,256]{1,0:T(8,128)(2,1)S(1)}, u32[]{:S(2)}, u32[]{:S(2)}) collective-permute-start(bf16[1552,256]{1,0:T(8,128)(2,1)S(1)} %collective-permute-done.5.refs_7_.refs_9_), channel_id=1, source_target_pairs={{0,1},{1,0},{2,3},{3,2},{4,5},{5,4},{6,7},{7,6},{8,9},{9,8},{10,11... | collective-permute-start | bytes 2383880 | tf_op jit(solution)/shard_map/ppermute | solution.py:343
  83.2 3.1 %collective-permute-start.9 = (bf16[1552,256]{1,0:T(8,128)(2,1)S(1)}, bf16[1552,256]{1,0:T(8,128)(2,1)S(1)}, u32[]{:S(2)}, u32[]{:S(2)}) collective-permute-start(bf16[1552,256]{1,0:T(8,128)(2,1)S(1)} %collective-permute-done.6.refs_8_.refs_10_), channel_id=1, source_target_pairs={{0,1},{1,0},{2,3},{3,2},{4,5},{5,4},{6,7},{7,6},{8,9},{9,8},{10,11... | collective-permute-start | bytes 2383880 | tf_op jit(solution)/shard_map/ppermute | solution.py:343
  83.2 5.9 %collective-permute-start.12 = (bf16[1552,256]{1,0:T(8,128)(2,1)S(1)}, bf16[1552,256]{1,0:T(8,128)(2,1)S(1)}, u32[]{:S(2)}, u32[]{:S(2)}) collective-permute-start(bf16[1552,256]{1,0:T(8,128)(2,1)S(1)} %collective-permute-done.6.refs_8_.refs_10_), channel_id=1, source_target_pairs={{254,0},{1,1},{252,2},{3,3},{0,4},{5,5},{2,6},{7,7},{4,8},{9,9},{6... | collective-permute-start | bytes 2383880 | tf_op jit(solution)/shard_map/ppermute | solution.py:338
  83.9 19.2 %collective-permute-start.13 = (bf16[1552,256]{1,0:T(8,128)(2,1)S(1)}, bf16[1552,256]{1,0:T(8,128)(2,1)S(1)}, u32[]{:S(2)}, u32[]{:S(2)}) collective-permute-start(bf16[1552,256]{1,0:T(8,128)(2,1)S(1)} %collective-permute-done.refs_9_), channel_id=1, source_target_pairs={{0,1},{1,0},{2,3},{3,2},{4,5},{5,4},{6,7},{7,6},{8,9},{9,8},{10,11... | collective-permute-start | bytes 2383880 | tf_op jit(solution)/shard_map/ppermute | solution.py:343
  85.8 17.4 %collective-permute-start.14 = (bf16[1552,256]{1,0:T(8,128)(2,1)S(1)}, bf16[1552,256]{1,0:T(8,128)(2,1)S(1)}, u32[]{:S(2)}, u32[]{:S(2)}) collective-permute-start(bf16[1552,256]{1,0:T(8,128)(2,1)S(1)} %collective-permute-done.3.refs_10_), channel_id=1, source_target_pairs={{0,1},{1,0},{2,3},{3,2},{4,5},{5,4},{6,7},{7,6},{8,9},{9,8},{10,11... | collective-permute-start | bytes 2383880 | tf_op jit(solution)/shard_map/ppermute | solution.py:343
  85.9 17.3 %collective-permute-start.15 = (bf16[1552,256]{1,0:T(8,128)(2,1)S(1)}, bf16[1552,256]{1,0:T(8,128)(2,1)S(1)}, u32[]{:S(2)}, u32[]{:S(2)}) collective-permute-start(bf16[1552,256]{1,0:T(8,128)(2,1)S(1)} %collective-permute-done.7.refs_3_), channel_id=1, source_target_pairs={{0,1},{1,0},{2,3},{3,2},{4,5},{5,4},{6,7},{7,6},{8,9},{9,8},{10,11... | collective-permute-start | bytes 2383880 | tf_op jit(solution)/shard_map/ppermute | solution.py:352
  86.3 1.6 %copy-start = (bf16[8,512,256]{2,1,0:T(8,128)(2,1)S(1)}, bf16[8,512,256]{2,1,0:T(8,128)(2,1)}, u32[]{:S(2)}) copy-start(bf16[8,512,256]{2,1,0:T(8,128)(2,1)} %get-tuple-element.15.refs_0_) | copy-start | bytes 6291460
  87.9 17.2 %copy-start.1 = (f32[1,512]{1,0:T(1,128)S(1)}, f32[1,512]{1,0:T(1,128)}, u32[]{:S(2)}) copy-start(f32[1,512]{1,0:T(1,128)} %get-tuple-element.24.refs_2_) | copy-start | bytes 6148
  89.2 15.9 %collective-permute-start.16 = (bf16[1552,256]{1,0:T(8,128)(2,1)S(1)}, bf16[1552,256]{1,0:T(8,128)(2,1)S(1)}, u32[]{:S(2)}, u32[]{:S(2)}) collective-permute-start(bf16[1552,256]{1,0:T(8,128)(2,1)S(1)} %collective-permute-done.12.refs_4_), channel_id=1, source_target_pairs={{0,1},{1,0},{2,3},{3,2},{4,5},{5,4},{6,7},{7,6},{8,9},{9,8},{10,11... | collective-permute-start | bytes 2383880 | tf_op jit(solution)/shard_map/ppermute | solution.py:352

commit v4 on v3

v4 whole, which is shorter than its diff:
```python
import functools

import jax
import jax.numpy as jnp
from jax import lax
from jax.experimental import pallas as pl
from jax.experimental.pallas import tpu as pltpu
from jax.sharding import PartitionSpec as P

BLK = 256
NBLK = 8
NBAND = 3
STEPS = 64
LOCAL = 512
TILE = 16
TOKEN = TILE + NBAND * LOCAL
AXES = ("tm", "rows")


def route(up, down):
    pairs = []
    for step in range(STEPS):
        for half in range(2):
            for core, source in enumerate((up, down)):
                from_step, from_half = source(step, half)
                pairs.append(
                    ((from_step % STEPS) * 4 + from_half * 2 + core, step * 4 + half * 2 + core)
                )
    return pairs


def above(t, h):
    return t + 1, h if t % 4 < 3 else 1 - h


def below(t, h):
    return t - 1, h if t % 4 > 0 else 1 - h


HOPS = (
    route(
        lambda t, h: (t - 4, h) if t % 4 == 3 else (t, h),
        lambda t, h: (t - 3, h if t % 4 < 3 else 1 - h),
    ),
    route(lambda t, h: (t - 1, h) if t % 4 > 0 else (t + 3, 1 - h), above),
    route(below, above),
    route(below, lambda t, h: (t, h)),
)
SIBLING = [(i, i ^ 1) for i in range(STEPS * 4)]


def prepare_kernel(*refs):
    sources, token_ref, held, sems = refs[:5], refs[5], refs[6:11], refs[11]
    copies = [
        pltpu.make_async_copy(source, target, sems.at[n])
        for n, (source, target) in enumerate(zip(sources, held))
    ]
    for copy in copies:
        copy.start()
    for copy in copies:
        copy.wait()
    offsets_ref, band_ref, mask_ref, observed_ref, gain_ref = held
    flag = mask_ref[...].astype(jnp.float32)
    gain = gain_ref[...]
    factor = 1.0 - gain * flag
    vector = gain * flag * observed_ref[...]
    row = lax.broadcasted_iota(jnp.int32, (TILE, BLK), 0)
    lane = lax.broadcasted_iota(jnp.int32, (TILE, BLK), 1)
    tile = jnp.where(row == 0, jnp.broadcast_to(vector[:, :BLK], (TILE, BLK)), 0.0)
    tile = jnp.where(row == 1, jnp.broadcast_to(vector[:, BLK:], (TILE, BLK)), tile)
    for j in range(NBAND):
        shift = offsets_ref[0, j].astype(jnp.float32)
        tile = jnp.where((row == 2) & (lane == j), shift, tile)
    token_ref[:TILE, :] = tile.astype(jnp.bfloat16)
    for i in range(LOCAL // 128):
        column = jnp.transpose(
            jnp.broadcast_to(factor[:, i * 128 : (i + 1) * 128], (128, 128))
        )
        for j in range(NBAND):
            for side in range(2):
                lanes = slice(side * 128, side * 128 + 128)
                block = band_ref[0, j, i * 128 : (i + 1) * 128, lanes].astype(jnp.float32)
                top = TILE + j * LOCAL + i * 128
                token_ref[top : top + 128, lanes] = (column * block).astype(jnp.bfloat16)


def prepare(band, mask, observed, offsets, gain):
    return pl.pallas_call(
        prepare_kernel,
        out_shape=jax.ShapeDtypeStruct((TOKEN, BLK), jnp.bfloat16),
        in_specs=[pl.BlockSpec(memory_space=pltpu.HBM)] * 5,
        out_specs=pl.BlockSpec(memory_space=pltpu.VMEM),
        scratch_shapes=[
            pltpu.SMEM((1, NBAND), jnp.int32),
            pltpu.VMEM((1, NBAND, LOCAL, BLK), jnp.bfloat16),
            pltpu.VMEM((1, LOCAL), jnp.int32),
            pltpu.VMEM((1, LOCAL), jnp.float32),
            pltpu.VMEM((1, LOCAL), jnp.float32),
            pltpu.SemaphoreType.DMA((5,)),
        ],
    )(offsets, band, mask, observed, gain.reshape(1, LOCAL))


def tile_of(ref):
    return ref[:TILE, :].astype(jnp.float32)


def shifts_of(tile):
    row = lax.broadcasted_iota(jnp.int32, (TILE, BLK), 0)
    lane = lax.broadcasted_iota(jnp.int32, (TILE, BLK), 1)
    return [
        jnp.sum(jnp.where((row == 2) & (lane == j), tile, 0.0)).astype(jnp.int32)
        for j in range(NBAND)
    ]


def gather(refs, whole, distance, sems):
    step, place = lax.axis_index("tm"), lax.axis_index("rows")
    half = place // 2
    side = jnp.where(step % 4 >= distance, half, 1 - half)
    groups = [2 * side, 2 * side + 1, 2 * (1 - side) + 1, 2 * (1 - side)]
    rows = whole.shape[1]
    pairs = [
        [
            pltpu.make_async_copy(refs[4 * core + n].at[0:rows], whole.at[groups[n]], sems.at[n])
            for n in range(4)
        ]
        for core in range(2)
    ]

    def start():
        for core in range(2):

            @pl.when(place % 2 == core)
            def _():
                for copy in pairs[core]:
                    copy.start()

    def wait():
        for copy in pairs[0]:
            copy.wait()

    return start, wait


def column_of(source, earlier, shifts, c):
    product = None
    for j in range(NBAND):
        k = lax.rem(c - shifts[j] + NBLK, NBLK)
        at = pl.multiple_of(TILE + (2 * j + k % 2) * BLK, TILE)
        term = jnp.dot(
            source[k], earlier[k // 2, pl.ds(at, BLK), :], preferred_element_type=jnp.float32
        )
        product = term if product is None else product + term
    return product


def vector_of(tiles, c):
    return tiles[c // 2][c % 2 : c % 2 + 1, :]


def place_kernel(own_ref, bare_ref, vector_ref):
    place = lax.axis_index("rows")
    tile = tile_of(own_ref)
    shifts = shifts_of(tile)
    bare_ref[...] = jnp.zeros_like(bare_ref)
    for j in range(NBAND):
        for r in range(2):
            target = lax.rem(2 * place + r + shifts[j] + NBLK, NBLK)
            at = TILE + (2 * j + r) * BLK
            bare_ref[target, r * BLK : (r + 1) * BLK, :] = own_ref[at : at + BLK, :]
    for r in range(2):
        vector_ref[:, r * BLK : (r + 1) * BLK] = tile[r : r + 1, :]


def place_blocks(own):
    vmem = pl.BlockSpec(memory_space=pltpu.VMEM)
    return pl.pallas_call(
        place_kernel,
        out_shape=[
            jax.ShapeDtypeStruct((NBLK, LOCAL, BLK), jnp.bfloat16),
            jax.ShapeDtypeStruct((1, LOCAL), jnp.float32),
        ],
        in_specs=[vmem],
        out_specs=[vmem, vmem],
        compiler_params=pltpu.CompilerParams(vmem_limit_bytes=8 * 1018 * 1024),
        cost_estimate=pl.CostEstimate(flops=1, bytes_accessed=1, transcendentals=0),
    )(own)


def weigh(matrix, tiles, start):
    parts = []
    for top in range(0, LOCAL, 64):
        rows = slice(top, top + 64)
        value = None if start is None else start[rows, :]
        for c in range(NBLK):
            term = matrix[c, rows, :].astype(jnp.float32) * vector_of(tiles, c)
            term = term[:, :128] + term[:, 128:]
            value = term if value is None else value + term
        parts.append(value)
    return jnp.concatenate(parts, axis=0)


def multiply(source, earlier, shifts, target):
    for c in range(NBLK):
        target[c] = column_of(source, earlier, shifts, c).astype(jnp.bfloat16)


def pair_kernel(*refs):
    bare, first, second, third = refs[0], refs[1:9], refs[9:17], refs[17:19]
    product_ref, total_ref, tile = refs[19:22]
    near, far, level, near_sems, far_sems, tile_sem = refs[22:]
    step = lax.axis_index("tm")
    near_start, near_wait = gather(first, near, 1, near_sems)
    far_start, far_wait = gather(second, far, 2, far_sems)
    tile_copies = [pltpu.make_async_copy(ref.at[0:TILE], tile, tile_sem.at[0]) for ref in third]
    for core in range(2):

        @pl.when(lax.axis_index("rows") % 2 == core)
        def _():
            tile_copies[core].start()

    near_start()
    far_start()
    tile_copies[0].wait()
    near_wait()
    far_wait()
    near_tiles = [tile_of(near.at[g]) for g in range(4)]
    far_tiles = [tile_of(far.at[g]) for g in range(4)]
    near_shifts, far_shifts = shifts_of(near_tiles[0]), shifts_of(far_tiles[0])

    @pl.when(step >= 2)
    def _():
        multiply(bare, near, near_shifts, level)
        total = weigh(bare, near_tiles, None)
        multiply(level, far, far_shifts, product_ref)
        total_ref[...] = weigh(level, far_tiles, total)

    @pl.when(step == 1)
    def _():
        multiply(bare, near, near_shifts, product_ref)
        total_ref[...] = weigh(bare, near_tiles, None)

    @pl.when(step == 0)
    def _():
        product_ref[...] = bare[...]
        total_ref[...] = jnp.zeros_like(total_ref)


def pair(bare, first, second, third):
    anywhere, vmem = pl.BlockSpec(memory_space=pl.ANY), pl.BlockSpec(memory_space=pltpu.VMEM)
    return pl.pallas_call(
        pair_kernel,
        out_shape=[
            jax.ShapeDtypeStruct((NBLK, LOCAL, BLK), jnp.bfloat16),
            jax.ShapeDtypeStruct((LOCAL, 128), jnp.float32),
            jax.ShapeDtypeStruct((TILE, BLK), jnp.bfloat16),
        ],
        in_specs=[vmem] + [anywhere] * 18,
        out_specs=[vmem, vmem, vmem],
        scratch_shapes=[
            pltpu.VMEM((4, TOKEN, BLK), jnp.bfloat16),
            pltpu.VMEM((4, TOKEN, BLK), jnp.bfloat16),
            pltpu.VMEM((NBLK, LOCAL, BLK), jnp.bfloat16),
            pltpu.SemaphoreType.DMA((4,)),
            pltpu.SemaphoreType.DMA((4,)),
            pltpu.SemaphoreType.DMA((1,)),
        ],
        compiler_params=pltpu.CompilerParams(vmem_limit_bytes=18 * 1024 * 1024),
        cost_estimate=pl.CostEstimate(flops=1, bytes_accessed=1, transcendentals=0),
    )(bare, *first, *second, *third)


def last_kernel(*refs):
    before, total_ref, own_ref, tile, third = refs[0], refs[1], refs[2], refs[3], refs[4:12]
    matrix_ref, vector_ref = refs[12:14]
    earlier, result, vector, sems, out_sems = refs[14:]
    step = lax.axis_index("tm")
    start, wait = gather(third, earlier, 3, sems)
    start()
    shifts = shifts_of(tile_of(tile))
    writes = [
        pltpu.make_async_copy(
            result.at[c], matrix_ref.at[0, :, c * BLK : (c + 1) * BLK], out_sems.at[c]
        )
        for c in range(NBLK)
    ]
    writes.append(pltpu.make_async_copy(vector, vector_ref, out_sems.at[NBLK]))

    def finish(total):
        high = total.astype(jnp.bfloat16)
        low = (total - high.astype(jnp.float32)).astype(jnp.bfloat16)
        ones = jnp.ones((TILE, 128), jnp.bfloat16)
        sums = sum(
            lax.dot_general(
                ones, part, (((1,), (1,)), ((), ())), preferred_element_type=jnp.float32
            )
            for part in (high, low)
        )
        vector[...] = (sums[0:1, :] + own_ref[...]).astype(jnp.bfloat16)
        writes[NBLK].start()

    wait()

    @pl.when(step >= 3)
    def _():
        tiles = [tile_of(earlier.at[g]) for g in range(4)]
        for c in range(NBLK):
            result[c] = column_of(before, earlier, shifts, c).astype(jnp.bfloat16)
            term = before[c].astype(jnp.float32) * vector_of(tiles, c)
            total_ref[...] += term[:, :128] + term[:, 128:]
            if c == NBLK - 1:
                finish(total_ref[...])
            writes[c].start()

    @pl.when(step < 3)
    def _():
        for c in range(NBLK):
            result[c] = before[c]
            writes[c].start()
        finish(total_ref[...])

    for write in writes:
        write.wait()


def last(before, total, own, tile, third):
    anywhere, vmem = pl.BlockSpec(memory_space=pl.ANY), pl.BlockSpec(memory_space=pltpu.VMEM)
    return pl.pallas_call(
        last_kernel,
        out_shape=[
            jax.ShapeDtypeStruct((1, LOCAL, NBLK * BLK), jnp.bfloat16),
            jax.ShapeDtypeStruct((1, LOCAL), jnp.bfloat16),
        ],
        in_specs=[vmem] * 4 + [anywhere] * 8,
        out_specs=[anywhere, anywhere],
        scratch_shapes=[
            pltpu.VMEM((4, TOKEN, BLK), jnp.bfloat16),
            pltpu.VMEM((NBLK, LOCAL, BLK), jnp.bfloat16),
            pltpu.VMEM((1, LOCAL), jnp.bfloat16),
            pltpu.SemaphoreType.DMA((4,)),
            pltpu.SemaphoreType.DMA((NBLK + 1,)),
        ],
        compiler_params=pltpu.CompilerParams(vmem_limit_bytes=14 * 1024 * 1024),
        cost_estimate=pl.CostEstimate(
            flops=48 * 2 * BLK**3, bytes_accessed=7 * 2**20, transcendentals=0
        ),
    )(before, total, own, tile, *third)


def after(arrays, later, earlier):
    names = list(later) + list(earlier)
    tied = lax.optimization_barrier(tuple(arrays[n] for n in names))
    arrays.update(zip(names, tied))


def per_device(band_blocks, site_mask, observed, band_offsets, site_gain):
    x = {}

    def move(name, source, hop):
        x[name] = lax.ppermute(x[source], AXES, hop)

    x["0a"] = prepare(band_blocks, site_mask, observed, band_offsets, site_gain)
    move("0b", "0a", SIBLING)
    after(x, ["0a"], ["0b"])
    for n in range(3):
        for part in "ab":
            move(f"{n + 1}{part}", f"{n}{part}", HOPS[n])
    after(x, ["0a"], ["1b"])
    x["bare"], x["vector"] = place_blocks(x["0a"])
    move("s2a", "2a", SIBLING)
    move("s2b", "2b", SIBLING)
    after(x, ["3a"], ["bare", "s2a"])
    move("4a", "3a", HOPS[3])
    after(x, ["3b"], ["s2b"])
    move("s3a", "3a", SIBLING)
    move("s3b", "3b", SIBLING)
    move("4b", "3b", HOPS[3])
    after(x, ["1a", "1b"], ["2a"])
    move("s1a", "1a", SIBLING)
    move("s1b", "1b", SIBLING)
    after(x, ["bare"], ["4a"])
    x["product"], x["total"], tile = pair(
        x["bare"],
        [x[n] for n in ("2a", "2b", "s3a", "s3b", "s2a", "s2b", "3a", "3b")],
        [x[n] for n in ("3a", "3b", "s2a", "s2b", "s3a", "s3b", "2a", "2b")],
        [x["4a"], x["1a"]],
    )
    after(x, ["4b"], ["product"])
    for part in "ab":
        move(f"s4{part}", f"4{part}", SIBLING)
    third = [x[n] for n in ("4a", "4b", "s1a", "s1b", "s4a", "s4b", "1a", "1b")]
    return tuple(last(x["product"], x["total"], x["vector"], tile, third))


def solution(mesh):
    in_specs = (
        P("tm", None, "rows", None),
        P("tm", "rows"),
        P("tm", "rows"),
        P("tm", None),
        P("rows"),
    )
    out_specs = (P("tm", "rows", None), P("tm", "rows"))
    return jax.shard_map(
        per_device, mesh=mesh, in_specs=in_specs, out_specs=out_specs, check_vma=False
    )
```

time: 108 us -> 92.1 us (0.85)
  waiting for transfers between devices: 39.4 us -> 23.1 us
  starting transfers between devices: 57.2 us -> 61.1 us
  Pallas kernels: 8.66 us -> 5.51 us
    ppermute x17, waiting for transfers between devices: 39.4 us -> 23.1 us  [move(): x[name] = lax.ppermute(x[source], AXES, hop)]
    ppermute x17, starting transfers between devices: 57.2 us -> 61.1 us  [move(): x[name] = lax.ppermute(x[source], AXES, hop)]
    pallas_call x1, Pallas kernels: 2.69 us -> 0.23 us  [place_blocks(): pl.pallas_call(place_kernel, out_shape=[jax.ShapeDtypeStruct((NBLK, LOCAL...]
  transfers between devices with their start and end apart: 17 -> 17, of which waited for: 7 -> 8; matrix products, arithmetic and copies ran while one was open for 0% -> 0% of each run, Pallas kernels for 4% -> 1%
where the time goes in v4:
time: 92.1 us; the launch traced here: 91.8 us
  starting transfers between devices  61.1 us (66%)
  waiting for transfers between devices  23.1 us (25%)
  Pallas kernels  5.51 us (6%)
  local copies, waits for them, and re-layouts  1.14 us (1%)
    ppermute x17, starting transfers between devices, move(): x[name] = lax.ppermute(x[source], AXES, hop)  61.1 us
    ppermute x17, waiting for transfers between devices, move(): x[name] = lax.ppermute(x[source], AXES, hop)  23.1 us
    pallas_call x1, Pallas kernels, prepare(): pl.pallas_call(prepare_kernel, out_shape=jax.ShapeDtypeStruct((TOKEN, BLK...  2.29 us
    pallas_call x1, Pallas kernels, last(): pl.pallas_call(last_kernel, out_shape=[jax.ShapeDtypeStruct((1, LOCAL, NB...  1.88 us
  transfers between devices with their start and end apart: 17, of which 8 were waited for; matrix products, arithmetic and copies ran while one was open for 0% of the time, Pallas kernels for 1%

profile of v4, /device:TPU:1, one launch (start us, length us, event | category | flops | bytes accessed | tf_op | source)
XLA Modules:
  0.0 91.8 jit_solution(17173120919816487822)
XLA Ops:
  0.6 2.3 %shard_map.68.own_ref = bf16[1552,256]{1,0:T(8,128)(2,1)} custom-call(s32[1,3]{1,0:T(1,128)} %refs_0_.1, bf16[1,3,512,256]{3,2,1,0:T(8,128)(2,1)} %refs_1_.1, s32[1,512]{1,0:T(1,128)} %refs_2_.1, f32[1,512]{1,0:T(1,128)} %refs_3_.1, f32[1,512]{1,0:T(1,128)} %bitcast.1), custom_call_target="tpu_custom_call" | custom-call | tf_op jit(solution)/shard_map/pallas_call | solution.py:88
  2.9 3.3 %collective-permute-start = (bf16[1552,256]{1,0:T(8,128)(2,1)}, bf16[1552,256]{1,0:T(8,128)(2,1)S(1)}, u32[]{:S(2)}, u32[]{:S(2)}) collective-permute-start(bf16[1552,256]{1,0:T(8,128)(2,1)} %shard_map.68.own_ref), channel_id=1, source_target_pairs={{0,1},{1,0},{2,3},{3,2},{4,5},{5,4},{6,7},{7,6},{8,9},{9,8},{10,11... | collective-permute-start | bytes 2383880 | tf_op jit(solution)/shard_map/ppermute | solution.py:361
  6.3 2.1 %collective-permute-done = bf16[1552,256]{1,0:T(8,128)(2,1)S(1)} collective-permute-done((bf16[1552,256]{1,0:T(8,128)(2,1)}, bf16[1552,256]{1,0:T(8,128)(2,1)S(1)}, u32[]{:S(2)}, u32[]{:S(2)}) %collective-permute-start) | collective-permute-done | bytes 794656 | tf_op jit(solution)/shard_map/ppermute | solution.py:361
  8.4 5.7 %collective-permute-start.6 = (bf16[1552,256]{1,0:T(8,128)(2,1)}, bf16[1552,256]{1,0:T(8,128)(2,1)S(1)}, u32[]{:S(2)}, u32[]{:S(2)}) collective-permute-start(bf16[1552,256]{1,0:T(8,128)(2,1)} %shard_map.68.own_ref), channel_id=1, source_target_pairs={{0,0},{245,1},{2,2},{247,3},{4,4},{249,5},{6,6},{251,7},{8,8},{253... | collective-permute-start | bytes 2383880 | tf_op jit(solution)/shard_map/ppermute | solution.py:361
  14.1 3.6 %collective-permute-start.1 = (bf16[1552,256]{1,0:T(8,128)(2,1)S(1)}, bf16[1552,256]{1,0:T(8,128)(2,1)S(1)}, u32[]{:S(2)}, u32[]{:S(2)}) collective-permute-start(bf16[1552,256]{1,0:T(8,128)(2,1)S(1)} %collective-permute-done), channel_id=1, source_target_pairs={{0,0},{245,1},{2,2},{247,3},{4,4},{249,5},{6,6},{251,7},{8,8},{253... | collective-permute-start | bytes 2383880 | tf_op jit(solution)/shard_map/ppermute | solution.py:361
  17.8 7.8 %collective-permute-done.6.refs_18_.refs_10_ = bf16[1552,256]{1,0:T(8,128)(2,1)S(1)} collective-permute-done((bf16[1552,256]{1,0:T(8,128)(2,1)}, bf16[1552,256]{1,0:T(8,128)(2,1)S(1)}, u32[]{:S(2)}, u32[]{:S(2)}) %collective-permute-start.6) | collective-permute-done | bytes 794656 | tf_op jit(solution)/shard_map/ppermute | solution.py:361
  25.6 5.5 %collective-permute-start.7 = (bf16[1552,256]{1,0:T(8,128)(2,1)S(1)}, bf16[1552,256]{1,0:T(8,128)(2,1)S(1)}, u32[]{:S(2)}, u32[]{:S(2)}) collective-permute-start(bf16[1552,256]{1,0:T(8,128)(2,1)S(1)} %collective-permute-done.6.refs_18_.refs_10_), channel_id=1, source_target_pairs={{14,0},{5,1},{12,2},{7,3},{0,4},{9,5},{2,6},{11,7},{4,8},{13,9},{6... | collective-permute-start | bytes 2383880 | tf_op jit(solution)/shard_map/ppermute | solution.py:361
  31.1 3.0 %collective-permute-done.1.refs_11_ = bf16[1552,256]{1,0:T(8,128)(2,1)S(1)} collective-permute-done((bf16[1552,256]{1,0:T(8,128)(2,1)S(1)}, bf16[1552,256]{1,0:T(8,128)(2,1)S(1)}, u32[]{:S(2)}, u32[]{:S(2)}) %collective-permute-start.1) | collective-permute-done | bytes 794656 | tf_op jit(solution)/shard_map/ppermute | solution.py:361
  34.1 5.5 %collective-permute-start.2 = (bf16[1552,256]{1,0:T(8,128)(2,1)S(1)}, bf16[1552,256]{1,0:T(8,128)(2,1)S(1)}, u32[]{:S(2)}, u32[]{:S(2)}) collective-permute-start(bf16[1552,256]{1,0:T(8,128)(2,1)S(1)} %collective-permute-done.1.refs_11_), channel_id=1, source_target_pairs={{14,0},{5,1},{12,2},{7,3},{0,4},{9,5},{2,6},{11,7},{4,8},{13,9},{6... | collective-permute-start | bytes 2383880 | tf_op jit(solution)/shard_map/ppermute | solution.py:361
  39.6 0.8 collective-permute-done.7.refs_1_.refs_15_
  40.4 7.3 %collective-permute-start.8 = (bf16[1552,256]{1,0:T(8,128)(2,1)S(1)}, bf16[1552,256]{1,0:T(8,128)(2,1)S(1)}, u32[]{:S(2)}, u32[]{:S(2)}) collective-permute-start(bf16[1552,256]{1,0:T(8,128)(2,1)S(1)} %collective-permute-done.7.refs_1_.refs_15_), channel_id=1, source_target_pairs={{254,0},{5,1},{252,2},{7,3},{0,4},{9,5},{2,6},{11,7},{4,8},{13,9},... | collective-permute-start | bytes 2383880 | tf_op jit(solution)/shard_map/ppermute | solution.py:361
  47.7 0.0 collective-permute-start.9
  47.7 1.2 %collective-permute-done.2.refs_2_.refs_16_ = bf16[1552,256]{1,0:T(8,128)(2,1)S(1)} collective-permute-done((bf16[1552,256]{1,0:T(8,128)(2,1)S(1)}, bf16[1552,256]{1,0:T(8,128)(2,1)S(1)}, u32[]{:S(2)}, u32[]{:S(2)}) %collective-permute-start.2) | collective-permute-done | bytes 794656 | tf_op jit(solution)/shard_map/ppermute | solution.py:361
  48.9 7.3 %collective-permute-start.3 = (bf16[1552,256]{1,0:T(8,128)(2,1)S(1)}, bf16[1552,256]{1,0:T(8,128)(2,1)S(1)}, u32[]{:S(2)}, u32[]{:S(2)}) collective-permute-start(bf16[1552,256]{1,0:T(8,128)(2,1)S(1)} %collective-permute-done.2.refs_2_.refs_16_), channel_id=1, source_target_pairs={{254,0},{5,1},{252,2},{7,3},{0,4},{9,5},{2,6},{11,7},{4,8},{13,9},... | collective-permute-start | bytes 2383880 | tf_op jit(solution)/shard_map/ppermute | solution.py:361
  56.2 0.0 collective-permute-start.4
  56.2 0.0 copy-start
  56.2 1.1 %copy-done = bf16[1552,256]{1,0:T(8,128)(2,1)S(1)} copy-done((bf16[1552,256]{1,0:T(8,128)(2,1)S(1)}, bf16[1552,256]{1,0:T(8,128)(2,1)}, u32[]{:S(2)}) %copy-start) | copy-done | bytes 794648
  57.4 0.2 shard_map.69
  57.6 0.0 collective-permute-done.8.refs_7_.refs_9_
  57.6 0.0 collective-permute-done.9.refs_5_.refs_11_
  57.6 0.7 collective-permute-start.10
  58.3 2.5 %collective-permute-start.11 = (bf16[1552,256]{1,0:T(8,128)(2,1)S(1)}, bf16[1552,256]{1,0:T(8,128)(2,1)S(1)}, u32[]{:S(2)}, u32[]{:S(2)}) collective-permute-start(bf16[1552,256]{1,0:T(8,128)(2,1)S(1)} %collective-permute-done.8.refs_7_.refs_9_), channel_id=1, source_target_pairs={{0,1},{1,0},{2,3},{3,2},{4,5},{5,4},{6,7},{7,6},{8,9},{9,8},{10,11... | collective-permute-start | bytes 2383880 | tf_op jit(solution)/shard_map/ppermute | solution.py:361
  60.8 5.1 %collective-permute-done.3.refs_8_.refs_10_ = bf16[1552,256]{1,0:T(8,128)(2,1)S(1)} collective-permute-done((bf16[1552,256]{1,0:T(8,128)(2,1)S(1)}, bf16[1552,256]{1,0:T(8,128)(2,1)S(1)}, u32[]{:S(2)}, u32[]{:S(2)}) %collective-permute-start.3) | collective-permute-done | bytes 794656 | tf_op jit(solution)/shard_map/ppermute | solution.py:361
  65.9 0.0 collective-permute-done.4.refs_6_.refs_12_
  65.9 1.4 %collective-permute-start.12 = (bf16[1552,256]{1,0:T(8,128)(2,1)S(1)}, bf16[1552,256]{1,0:T(8,128)(2,1)S(1)}, u32[]{:S(2)}, u32[]{:S(2)}) collective-permute-start(bf16[1552,256]{1,0:T(8,128)(2,1)S(1)} %collective-permute-done.3.refs_8_.refs_10_), channel_id=1, source_target_pairs={{0,1},{1,0},{2,3},{3,2},{4,5},{5,4},{6,7},{7,6},{8,9},{9,8},{10,11... | collective-permute-start | bytes 2383880 | tf_op jit(solution)/shard_map/ppermute | solution.py:361
  67.3 0.7 collective-permute-start.5
  68.0 1.3 %collective-permute-start.13 = (bf16[1552,256]{1,0:T(8,128)(2,1)S(1)}, bf16[1552,256]{1,0:T(8,128)(2,1)S(1)}, u32[]{:S(2)}, u32[]{:S(2)}) collective-permute-start(bf16[1552,256]{1,0:T(8,128)(2,1)S(1)} %collective-permute-done.6.refs_18_.refs_10_), channel_id=1, source_target_pairs={{0,1},{1,0},{2,3},{3,2},{4,5},{5,4},{6,7},{7,6},{8,9},{9,8},{10,11... | collective-permute-start | bytes 2383880 | tf_op jit(solution)/shard_map/ppermute | solution.py:361
  69.3 0.0 collective-permute-done.10.refs_17_.refs_4_
  69.3 8.9 %collective-permute-start.14 = (bf16[1552,256]{1,0:T(8,128)(2,1)S(1)}, bf16[1552,256]{1,0:T(8,128)(2,1)S(1)}, u32[]{:S(2)}, u32[]{:S(2)}) collective-permute-start(bf16[1552,256]{1,0:T(8,128)(2,1)S(1)} %collective-permute-done.1.refs_11_), channel_id=1, source_target_pairs={{0,1},{1,0},{2,3},{3,2},{4,5},{5,4},{6,7},{7,6},{8,9},{9,8},{10,11... | collective-permute-start | bytes 2383880 | tf_op jit(solution)/shard_map/ppermute | solution.py:361
  78.2 0.0 collective-permute-done.11.refs_3_.refs_13_
  78.2 0.0 collective-permute-done.12.refs_4_.refs_14_
  78.2 1.1 %shard_map.70 = (bf16[8,512,256]{2,1,0:T(8,128)(2,1)S(1)}, f32[512,128]{1,0:T(8,128)S(1)}, bf16[16,256]{1,0:T(8,128)(2,1)S(1)}) custom-call(bf16[8,512,256]{2,1,0:T(8,128)(2,1)S(1)} %get-tuple-element.30.refs_0_, bf16[1552,256]{1,0:T(8,128)(2,1)S(1)} %collective-permute-done.7.refs_1_.refs_15_, ...), custom_call_target="tpu_custom_call" | custom-call | flops 1 | bytes 1 | tf_op jit(solution)/shard_map/pallas_call | solution.py:252
  79.3 0.0 collective-permute-done.5.refs_5_
  79.3 7.4 %collective-permute-start.16 = (bf16[1552,256]{1,0:T(8,128)(2,1)S(1)}, bf16[1552,256]{1,0:T(8,128)(2,1)S(1)}, u32[]{:S(2)}, u32[]{:S(2)}) collective-permute-start(bf16[1552,256]{1,0:T(8,128)(2,1)S(1)} %collective-permute-done.5.refs_5_), channel_id=1, source_target_pairs={{0,1},{1,0},{2,3},{3,2},{4,5},{5,4},{6,7},{7,6},{8,9},{9,8},{10,11... | collective-permute-start | bytes 2383880 | tf_op jit(solution)/shard_map/ppermute | solution.py:361
  86.7 0.0 collective-permute-start.15
  86.7 0.0 collective-permute-done.13.refs_6_
  86.7 0.0 collective-permute-done.14.refs_7_
  86.7 1.9 %collective-permute-done.16.refs_9_ = bf16[1552,256]{1,0:T(8,128)(2,1)S(1)} collective-permute-done((bf16[1552,256]{1,0:T(8,128)(2,1)S(1)}, bf16[1552,256]{1,0:T(8,128)(2,1)S(1)}, u32[]{:S(2)}, u32[]{:S(2)}) %collective-permute-start.16) | collective-permute-done | bytes 794656 | tf_op jit(solution)/shard_map/ppermute | solution.py:361
  88.6 1.1 %collective-permute-done.15.refs_8_ = bf16[1552,256]{1,0:T(8,128)(2,1)S(1)} collective-permute-done((bf16[1552,256]{1,0:T(8,128)(2,1)S(1)}, bf16[1552,256]{1,0:T(8,128)(2,1)S(1)}, u32[]{:S(2)}, u32[]{:S(2)}) %collective-permute-start.15) | collective-permute-done | bytes 794656 | tf_op jit(solution)/shard_map/ppermute | solution.py:361
  89.8 1.9 %shard_map.71 = (bf16[1,512,2048]{2,1,0:T(8,128)(2,1)}, bf16[1,512]{1,0:T(2,128)(2,1)}) custom-call(bf16[8,512,256]{2,1,0:T(8,128)(2,1)S(1)} %get-tuple-element.38.refs_0_, f32[512,128]{1,0:T(8,128)S(1)} %get-tuple-element.39.refs_1_, f32[1,512]{1,0:T(1,128)S(1)} %get-tuple-element.40.refs_2_, bf16[16,256]{1,0:T(8,128)(2,1)S(1)} %get-tuple-element.41.refs_3_, ...), custom_call_target="tpu_custom_call" | custom-call | flops 1610612736 | bytes 7340032 | tf_op jit(solution)/shard_map/pallas_call | solution.py:329
Async XLA Ops:
  2.9 5.5 %collective-permute-start = (bf16[1552,256]{1,0:T(8,128)(2,1)}, bf16[1552,256]{1,0:T(8,128)(2,1)S(1)}, u32[]{:S(2)}, u32[]{:S(2)}) collective-permute-start(bf16[1552,256]{1,0:T(8,128)(2,1)} %shard_map.68.own_ref), channel_id=1, source_target_pairs={{0,1},{1,0},{2,3},{3,2},{4,5},{5,4},{6,7},{7,6},{8,9},{9,8},{10,11... | collective-permute-start | bytes 2383880 | tf_op jit(solution)/shard_map/ppermute | solution.py:361
  8.4 17.2 %collective-permute-start.6 = (bf16[1552,256]{1,0:T(8,128)(2,1)}, bf16[1552,256]{1,0:T(8,128)(2,1)S(1)}, u32[]{:S(2)}, u32[]{:S(2)}) collective-permute-start(bf16[1552,256]{1,0:T(8,128)(2,1)} %shard_map.68.own_ref), channel_id=1, source_target_pairs={{0,0},{245,1},{2,2},{247,3},{4,4},{249,5},{6,6},{251,7},{8,8},{253... | collective-permute-start | bytes 2383880 | tf_op jit(solution)/shard_map/ppermute | solution.py:361
  14.1 20.0 %collective-permute-start.1 = (bf16[1552,256]{1,0:T(8,128)(2,1)S(1)}, bf16[1552,256]{1,0:T(8,128)(2,1)S(1)}, u32[]{:S(2)}, u32[]{:S(2)}) collective-permute-start(bf16[1552,256]{1,0:T(8,128)(2,1)S(1)} %collective-permute-done), channel_id=1, source_target_pairs={{0,0},{245,1},{2,2},{247,3},{4,4},{249,5},{6,6},{251,7},{8,8},{253... | collective-permute-start | bytes 2383880 | tf_op jit(solution)/shard_map/ppermute | solution.py:361
  25.6 14.7 %collective-permute-start.7 = (bf16[1552,256]{1,0:T(8,128)(2,1)S(1)}, bf16[1552,256]{1,0:T(8,128)(2,1)S(1)}, u32[]{:S(2)}, u32[]{:S(2)}) collective-permute-start(bf16[1552,256]{1,0:T(8,128)(2,1)S(1)} %collective-permute-done.6.refs_18_.refs_10_), channel_id=1, source_target_pairs={{14,0},{5,1},{12,2},{7,3},{0,4},{9,5},{2,6},{11,7},{4,8},{13,9},{6... | collective-permute-start | bytes 2383880 | tf_op jit(solution)/shard_map/ppermute | solution.py:361
  34.1 14.7 %collective-permute-start.2 = (bf16[1552,256]{1,0:T(8,128)(2,1)S(1)}, bf16[1552,256]{1,0:T(8,128)(2,1)S(1)}, u32[]{:S(2)}, u32[]{:S(2)}) collective-permute-start(bf16[1552,256]{1,0:T(8,128)(2,1)S(1)} %collective-permute-done.1.refs_11_), channel_id=1, source_target_pairs={{14,0},{5,1},{12,2},{7,3},{0,4},{9,5},{2,6},{11,7},{4,8},{13,9},{6... | collective-permute-start | bytes 2383880 | tf_op jit(solution)/shard_map/ppermute | solution.py:361
  40.4 17.2 %collective-permute-start.8 = (bf16[1552,256]{1,0:T(8,128)(2,1)S(1)}, bf16[1552,256]{1,0:T(8,128)(2,1)S(1)}, u32[]{:S(2)}, u32[]{:S(2)}) collective-permute-start(bf16[1552,256]{1,0:T(8,128)(2,1)S(1)} %collective-permute-done.7.refs_1_.refs_15_), channel_id=1, source_target_pairs={{254,0},{5,1},{252,2},{7,3},{0,4},{9,5},{2,6},{11,7},{4,8},{13,9},... | collective-permute-start | bytes 2383880 | tf_op jit(solution)/shard_map/ppermute | solution.py:361
  47.7 9.9 %collective-permute-start.9 = (bf16[1552,256]{1,0:T(8,128)(2,1)S(1)}, bf16[1552,256]{1,0:T(8,128)(2,1)S(1)}, u32[]{:S(2)}, u32[]{:S(2)}) collective-permute-start(bf16[1552,256]{1,0:T(8,128)(2,1)S(1)} %collective-permute-done.7.refs_1_.refs_15_), channel_id=1, source_target_pairs={{0,1},{1,0},{2,3},{3,2},{4,5},{5,4},{6,7},{7,6},{8,9},{9,8},{10,11... | collective-permute-start | bytes 2383880 | tf_op jit(solution)/shard_map/ppermute | solution.py:361
  48.9 17.0 %collective-permute-start.3 = (bf16[1552,256]{1,0:T(8,128)(2,1)S(1)}, bf16[1552,256]{1,0:T(8,128)(2,1)S(1)}, u32[]{:S(2)}, u32[]{:S(2)}) collective-permute-start(bf16[1552,256]{1,0:T(8,128)(2,1)S(1)} %collective-permute-done.2.refs_2_.refs_16_), channel_id=1, source_target_pairs={{254,0},{5,1},{252,2},{7,3},{0,4},{9,5},{2,6},{11,7},{4,8},{13,9},... | collective-permute-start | bytes 2383880 | tf_op jit(solution)/shard_map/ppermute | solution.py:361
  56.2 9.7 %collective-permute-start.4 = (bf16[1552,256]{1,0:T(8,128)(2,1)S(1)}, bf16[1552,256]{1,0:T(8,128)(2,1)S(1)}, u32[]{:S(2)}, u32[]{:S(2)}) collective-permute-start(bf16[1552,256]{1,0:T(8,128)(2,1)S(1)} %collective-permute-done.2.refs_2_.refs_16_), channel_id=1, source_target_pairs={{0,1},{1,0},{2,3},{3,2},{4,5},{5,4},{6,7},{7,6},{8,9},{9,8},{10,11... | collective-permute-start | bytes 2383880 | tf_op jit(solution)/shard_map/ppermute | solution.py:361
  56.2 1.1 %copy-start = (bf16[1552,256]{1,0:T(8,128)(2,1)S(1)}, bf16[1552,256]{1,0:T(8,128)(2,1)}, u32[]{:S(2)}) copy-start(bf16[1552,256]{1,0:T(8,128)(2,1)} %shard_map.68.own_ref) | copy-start | bytes 2383876
  57.6 11.7 %collective-permute-start.10 = (bf16[1552,256]{1,0:T(8,128)(2,1)S(1)}, bf16[1552,256]{1,0:T(8,128)(2,1)S(1)}, u32[]{:S(2)}, u32[]{:S(2)}) collective-permute-start(bf16[1552,256]{1,0:T(8,128)(2,1)S(1)} %collective-permute-done.8.refs_7_.refs_9_), channel_id=1, source_target_pairs={{254,0},{1,1},{252,2},{3,3},{0,4},{5,5},{2,6},{7,7},{4,8},{9,9},{6... | collective-permute-start | bytes 2383880 | tf_op jit(solution)/shard_map/ppermute | solution.py:361
  58.3 19.8 %collective-permute-start.11 = (bf16[1552,256]{1,0:T(8,128)(2,1)S(1)}, bf16[1552,256]{1,0:T(8,128)(2,1)S(1)}, u32[]{:S(2)}, u32[]{:S(2)}) collective-permute-start(bf16[1552,256]{1,0:T(8,128)(2,1)S(1)} %collective-permute-done.8.refs_7_.refs_9_), channel_id=1, source_target_pairs={{0,1},{1,0},{2,3},{3,2},{4,5},{5,4},{6,7},{7,6},{8,9},{9,8},{10,11... | collective-permute-start | bytes 2383880 | tf_op jit(solution)/shard_map/ppermute | solution.py:361
  65.9 12.3 %collective-permute-start.12 = (bf16[1552,256]{1,0:T(8,128)(2,1)S(1)}, bf16[1552,256]{1,0:T(8,128)(2,1)S(1)}, u32[]{:S(2)}, u32[]{:S(2)}) collective-permute-start(bf16[1552,256]{1,0:T(8,128)(2,1)S(1)} %collective-permute-done.3.refs_8_.refs_10_), channel_id=1, source_target_pairs={{0,1},{1,0},{2,3},{3,2},{4,5},{5,4},{6,7},{7,6},{8,9},{9,8},{10,11... | collective-permute-start | bytes 2383880 | tf_op jit(solution)/shard_map/ppermute | solution.py:361
  67.3 12.0 %collective-permute-start.5 = (bf16[1552,256]{1,0:T(8,128)(2,1)S(1)}, bf16[1552,256]{1,0:T(8,128)(2,1)S(1)}, u32[]{:S(2)}, u32[]{:S(2)}) collective-permute-start(bf16[1552,256]{1,0:T(8,128)(2,1)S(1)} %collective-permute-done.3.refs_8_.refs_10_), channel_id=1, source_target_pairs={{254,0},{1,1},{252,2},{3,3},{0,4},{5,5},{2,6},{7,7},{4,8},{9,9},{6... | collective-permute-start | bytes 2383880 | tf_op jit(solution)/shard_map/ppermute | solution.py:361
  68.0 18.7 %collective-permute-start.13 = (bf16[1552,256]{1,0:T(8,128)(2,1)S(1)}, bf16[1552,256]{1,0:T(8,128)(2,1)S(1)}, u32[]{:S(2)}, u32[]{:S(2)}) collective-permute-start(bf16[1552,256]{1,0:T(8,128)(2,1)S(1)} %collective-permute-done.6.refs_18_.refs_10_), channel_id=1, source_target_pairs={{0,1},{1,0},{2,3},{3,2},{4,5},{5,4},{6,7},{7,6},{8,9},{9,8},{10,11... | collective-permute-start | bytes 2383880 | tf_op jit(solution)/shard_map/ppermute | solution.py:361
  69.3 17.4 %collective-permute-start.14 = (bf16[1552,256]{1,0:T(8,128)(2,1)S(1)}, bf16[1552,256]{1,0:T(8,128)(2,1)S(1)}, u32[]{:S(2)}, u32[]{:S(2)}) collective-permute-start(bf16[1552,256]{1,0:T(8,128)(2,1)S(1)} %collective-permute-done.1.refs_11_), channel_id=1, source_target_pairs={{0,1},{1,0},{2,3},{3,2},{4,5},{5,4},{6,7},{7,6},{8,9},{9,8},{10,11... | collective-permute-start | bytes 2383880 | tf_op jit(solution)/shard_map/ppermute | solution.py:361
  79.3 9.3 %collective-permute-start.16 = (bf16[1552,256]{1,0:T(8,128)(2,1)S(1)}, bf16[1552,256]{1,0:T(8,128)(2,1)S(1)}, u32[]{:S(2)}, u32[]{:S(2)}) collective-permute-start(bf16[1552,256]{1,0:T(8,128)(2,1)S(1)} %collective-permute-done.5.refs_5_), channel_id=1, source_target_pairs={{0,1},{1,0},{2,3},{3,2},{4,5},{5,4},{6,7},{7,6},{8,9},{9,8},{10,11... | collective-permute-start | bytes 2383880 | tf_op jit(solution)/shard_map/ppermute | solution.py:361
  86.7 3.1 %collective-permute-start.15 = (bf16[1552,256]{1,0:T(8,128)(2,1)S(1)}, bf16[1552,256]{1,0:T(8,128)(2,1)S(1)}, u32[]{:S(2)}, u32[]{:S(2)}) collective-permute-start(bf16[1552,256]{1,0:T(8,128)(2,1)S(1)} %collective-permute-done.10.refs_17_.refs_4_), channel_id=1, source_target_pairs={{0,1},{1,0},{2,3},{3,2},{4,5},{5,4},{6,7},{7,6},{8,9},{9,8},{10,11... | collective-permute-start | bytes 2383880 | tf_op jit(solution)/shard_map/ppermute | solution.py:361

commit v5 on v4

--- a/solution.py
+++ b/solution.py
@@ -159,6 +159,21 @@
     return tiles[c // 2][c % 2 : c % 2 + 1, :]
 
 
+def mark_kernel(value_ref, mark_ref):
+    mark_ref[...] = jnp.zeros_like(mark_ref)
+
+
+def mark(value):
+    return pl.pallas_call(
+        mark_kernel,
+        out_shape=jax.ShapeDtypeStruct((8, 128), jnp.float32),
+        in_specs=[pl.BlockSpec(memory_space=pl.ANY)],
+        out_specs=pl.BlockSpec(memory_space=pltpu.VMEM),
+        compiler_params=pltpu.CompilerParams(vmem_limit_bytes=1024 * 1024),
+        cost_estimate=pl.CostEstimate(flops=0, bytes_accessed=4 * 2**20, transcendentals=0),
+    )(value)
+
+
 def place_kernel(own_ref, bare_ref, vector_ref):
     place = lax.axis_index("rows")
     tile = tile_of(own_ref)
@@ -273,8 +288,8 @@
 
 def last_kernel(*refs):
     before, total_ref, own_ref, tile, third = refs[0], refs[1], refs[2], refs[3], refs[4:12]
-    matrix_ref, vector_ref = refs[12:14]
-    earlier, result, vector, sems, out_sems = refs[14:]
+    matrix_ref, vector_ref = refs[13:15]
+    earlier, result, vector, sems, out_sems = refs[15:]
     step = lax.axis_index("tm")
     start, wait = gather(third, earlier, 3, sems)
     start()
@@ -324,7 +339,7 @@
         write.wait()
 
 
-def last(before, total, own, tile, third):
+def last(before, total, own, tile, third, mark):
     anywhere, vmem = pl.BlockSpec(memory_space=pl.ANY), pl.BlockSpec(memory_space=pltpu.VMEM)
     return pl.pallas_call(
         last_kernel,
@@ -332,7 +347,7 @@
             jax.ShapeDtypeStruct((1, LOCAL, NBLK * BLK), jnp.bfloat16),
             jax.ShapeDtypeStruct((1, LOCAL), jnp.bfloat16),
         ],
-        in_specs=[vmem] * 4 + [anywhere] * 8,
+        in_specs=[vmem] * 4 + [anywhere] * 9,
         out_specs=[anywhere, anywhere],
         scratch_shapes=[
             pltpu.VMEM((4, TOKEN, BLK), jnp.bfloat16),
@@ -345,7 +360,7 @@
         cost_estimate=pl.CostEstimate(
             flops=48 * 2 * BLK**3, bytes_accessed=7 * 2**20, transcendentals=0
         ),
-    )(before, total, own, tile, *third)
+    )(before, total, own, tile, *third, mark)
 
 
 def after(arrays, later, earlier):
@@ -362,8 +377,10 @@
 
     x["0a"] = prepare(band_blocks, site_mask, observed, band_offsets, site_gain)
     move("0b", "0a", SIBLING)
-    after(x, ["0a"], ["0b"])
-    for n in range(3):
+    move("1a", "0a", HOPS[0])
+    move("1b", "0b", HOPS[0])
+    after(x, ["1a"], ["0b"])
+    for n in (1, 2):
         for part in "ab":
             move(f"{n + 1}{part}", f"{n}{part}", HOPS[n])
     after(x, ["0a"], ["1b"])
@@ -386,11 +403,13 @@
         [x[n] for n in ("3a", "3b", "s2a", "s2b", "s3a", "s3b", "2a", "2b")],
         [x["4a"], x["1a"]],
     )
-    after(x, ["4b"], ["product"])
-    for part in "ab":
-        move(f"s4{part}", f"4{part}", SIBLING)
+    x["mark"] = mark(x["4a"])
+    after(x, ["4a"], ["mark"])
+    move("s4a", "4a", SIBLING)
+    after(x, ["4b"], ["product", "s4a"])
+    move("s4b", "4b", SIBLING)
     third = [x[n] for n in ("4a", "4b", "s1a", "s1b", "s4a", "s4b", "1a", "1b")]
-    return tuple(last(x["product"], x["total"], x["vector"], tile, third))
+    return tuple(last(x["product"], x["total"], x["vector"], tile, third, x["mark"]))
 
 
 def solution(mesh):

time: 92.1 us -> 88.7 us (0.963)
  waiting for transfers between devices: 23.1 us -> 20.5 us
    ppermute x17, waiting for transfers between devices: 23.1 us -> 20.5 us  [move(): x[name] = lax.ppermute(x[source], AXES, hop)]
  transfers between devices with their start and end apart: 17 -> 17, of which waited for: 8 -> 7; matrix products, arithmetic and copies ran while one was open for 0% -> 0% of each run, Pallas kernels for 1% -> 2%
where the time goes in v5:
time: 88.7 us; the launch traced here: 88.4 us
  starting transfers between devices  60.4 us (68%)
  waiting for transfers between devices  20.5 us (23%)
  Pallas kernels  5.5 us (6%)
  local copies, waits for them, and re-layouts  1.14 us (1%)
  between operations  0.89 us (1%)
    ppermute x17, starting transfers between devices, move(): x[name] = lax.ppermute(x[source], AXES, hop)  60.4 us
    ppermute x17, waiting for transfers between devices, move(): x[name] = lax.ppermute(x[source], AXES, hop)  20.5 us
    pallas_call x1, Pallas kernels, prepare(): pl.pallas_call(prepare_kernel, out_shape=jax.ShapeDtypeStruct((TOKEN, BLK...  2.29 us
    pallas_call x1, Pallas kernels, last(): pl.pallas_call(last_kernel, out_shape=[jax.ShapeDtypeStruct((1, LOCAL, NB...  1.88 us
  transfers between devices with their start and end apart: 17, of which 7 were waited for; matrix products, arithmetic and copies ran while one was open for 0% of the time, Pallas kernels for 2%

profile of v5, /device:TPU:1, one launch (start us, length us, event | category | flops | bytes accessed | tf_op | source)
XLA Modules:
  0.0 88.4 jit_solution(5090112773351104997)
XLA Ops:
  0.6 2.3 %shard_map.68.own_ref = bf16[1552,256]{1,0:T(8,128)(2,1)} custom-call(s32[1,3]{1,0:T(1,128)} %refs_0_.1, bf16[1,3,512,256]{3,2,1,0:T(8,128)(2,1)} %refs_1_.1, s32[1,512]{1,0:T(1,128)} %refs_2_.1, f32[1,512]{1,0:T(1,128)} %refs_3_.1, f32[1,512]{1,0:T(1,128)} %bitcast.1), custom_call_target="tpu_custom_call" | custom-call | tf_op jit(solution)/shard_map/pallas_call | solution.py:88
  2.9 3.3 %collective-permute-start = (bf16[1552,256]{1,0:T(8,128)(2,1)}, bf16[1552,256]{1,0:T(8,128)(2,1)S(1)}, u32[]{:S(2)}, u32[]{:S(2)}) collective-permute-start(bf16[1552,256]{1,0:T(8,128)(2,1)} %shard_map.68.own_ref), channel_id=1, source_target_pairs={{0,1},{1,0},{2,3},{3,2},{4,5},{5,4},{6,7},{7,6},{8,9},{9,8},{10,11... | collective-permute-start | bytes 2383880 | tf_op jit(solution)/shard_map/ppermute | solution.py:376
  6.3 5.7 %collective-permute-start.6 = (bf16[1552,256]{1,0:T(8,128)(2,1)}, bf16[1552,256]{1,0:T(8,128)(2,1)S(1)}, u32[]{:S(2)}, u32[]{:S(2)}) collective-permute-start(bf16[1552,256]{1,0:T(8,128)(2,1)} %shard_map.68.own_ref), channel_id=1, source_target_pairs={{0,0},{245,1},{2,2},{247,3},{4,4},{249,5},{6,6},{251,7},{8,8},{253... | collective-permute-start | bytes 2383880 | tf_op jit(solution)/shard_map/ppermute | solution.py:376
  12.0 0.0 collective-permute-done
  12.0 3.6 %collective-permute-start.1 = (bf16[1552,256]{1,0:T(8,128)(2,1)S(1)}, bf16[1552,256]{1,0:T(8,128)(2,1)S(1)}, u32[]{:S(2)}, u32[]{:S(2)}) collective-permute-start(bf16[1552,256]{1,0:T(8,128)(2,1)S(1)} %collective-permute-done), channel_id=1, source_target_pairs={{0,0},{245,1},{2,2},{247,3},{4,4},{249,5},{6,6},{251,7},{8,8},{253... | collective-permute-start | bytes 2383880 | tf_op jit(solution)/shard_map/ppermute | solution.py:376
  15.7 7.8 %collective-permute-done.6.refs_18_.refs_10_ = bf16[1552,256]{1,0:T(8,128)(2,1)S(1)} collective-permute-done((bf16[1552,256]{1,0:T(8,128)(2,1)}, bf16[1552,256]{1,0:T(8,128)(2,1)S(1)}, u32[]{:S(2)}, u32[]{:S(2)}) %collective-permute-start.6) | collective-permute-done | bytes 794656 | tf_op jit(solution)/shard_map/ppermute | solution.py:376
  23.5 5.5 %collective-permute-start.7 = (bf16[1552,256]{1,0:T(8,128)(2,1)S(1)}, bf16[1552,256]{1,0:T(8,128)(2,1)S(1)}, u32[]{:S(2)}, u32[]{:S(2)}) collective-permute-start(bf16[1552,256]{1,0:T(8,128)(2,1)S(1)} %collective-permute-done.6.refs_18_.refs_10_), channel_id=1, source_target_pairs={{14,0},{5,1},{12,2},{7,3},{0,4},{9,5},{2,6},{11,7},{4,8},{13,9},{6... | collective-permute-start | bytes 2383880 | tf_op jit(solution)/shard_map/ppermute | solution.py:376
  29.0 3.0 %collective-permute-done.1.refs_11_ = bf16[1552,256]{1,0:T(8,128)(2,1)S(1)} collective-permute-done((bf16[1552,256]{1,0:T(8,128)(2,1)S(1)}, bf16[1552,256]{1,0:T(8,128)(2,1)S(1)}, u32[]{:S(2)}, u32[]{:S(2)}) %collective-permute-start.1) | collective-permute-done | bytes 794656 | tf_op jit(solution)/shard_map/ppermute | solution.py:376
  32.0 5.5 %collective-permute-start.2 = (bf16[1552,256]{1,0:T(8,128)(2,1)S(1)}, bf16[1552,256]{1,0:T(8,128)(2,1)S(1)}, u32[]{:S(2)}, u32[]{:S(2)}) collective-permute-start(bf16[1552,256]{1,0:T(8,128)(2,1)S(1)} %collective-permute-done.1.refs_11_), channel_id=1, source_target_pairs={{14,0},{5,1},{12,2},{7,3},{0,4},{9,5},{2,6},{11,7},{4,8},{13,9},{6... | collective-permute-start | bytes 2383880 | tf_op jit(solution)/shard_map/ppermute | solution.py:376
  37.5 0.8 collective-permute-done.7.refs_1_.refs_15_
  38.2 7.3 %collective-permute-start.8 = (bf16[1552,256]{1,0:T(8,128)(2,1)S(1)}, bf16[1552,256]{1,0:T(8,128)(2,1)S(1)}, u32[]{:S(2)}, u32[]{:S(2)}) collective-permute-start(bf16[1552,256]{1,0:T(8,128)(2,1)S(1)} %collective-permute-done.7.refs_1_.refs_15_), channel_id=1, source_target_pairs={{254,0},{5,1},{252,2},{7,3},{0,4},{9,5},{2,6},{11,7},{4,8},{13,9},... | collective-permute-start | bytes 2383880 | tf_op jit(solution)/shard_map/ppermute | solution.py:376
  45.6 0.0 collective-permute-start.9
  45.6 0.0 copy-start
  45.6 1.1 %copy-done = bf16[1552,256]{1,0:T(8,128)(2,1)S(1)} copy-done((bf16[1552,256]{1,0:T(8,128)(2,1)S(1)}, bf16[1552,256]{1,0:T(8,128)(2,1)}, u32[]{:S(2)}) %copy-start) | copy-done | bytes 794648
  46.7 0.2 shard_map.69
  46.9 0.0 collective-permute-done.2.refs_2_.refs_16_
  47.0 7.1 %collective-permute-start.3 = (bf16[1552,256]{1,0:T(8,128)(2,1)S(1)}, bf16[1552,256]{1,0:T(8,128)(2,1)S(1)}, u32[]{:S(2)}, u32[]{:S(2)}) collective-permute-start(bf16[1552,256]{1,0:T(8,128)(2,1)S(1)} %collective-permute-done.2.refs_2_.refs_16_), channel_id=1, source_target_pairs={{254,0},{5,1},{252,2},{7,3},{0,4},{9,5},{2,6},{11,7},{4,8},{13,9},... | collective-permute-start | bytes 2383880 | tf_op jit(solution)/shard_map/ppermute | solution.py:376
  54.1 0.0 collective-permute-start.4
  54.1 1.2 %collective-permute-done.8.refs_7_.refs_9_ = bf16[1552,256]{1,0:T(8,128)(2,1)S(1)} collective-permute-done((bf16[1552,256]{1,0:T(8,128)(2,1)S(1)}, bf16[1552,256]{1,0:T(8,128)(2,1)S(1)}, u32[]{:S(2)}, u32[]{:S(2)}) %collective-permute-start.8) | collective-permute-done | bytes 794656 | tf_op jit(solution)/shard_map/ppermute | solution.py:376
  55.3 0.0 collective-permute-done.9.refs_5_.refs_11_
  55.3 0.7 collective-permute-start.10
  56.0 2.3 %collective-permute-start.11 = (bf16[1552,256]{1,0:T(8,128)(2,1)S(1)}, bf16[1552,256]{1,0:T(8,128)(2,1)S(1)}, u32[]{:S(2)}, u32[]{:S(2)}) collective-permute-start(bf16[1552,256]{1,0:T(8,128)(2,1)S(1)} %collective-permute-done.8.refs_7_.refs_9_), channel_id=1, source_target_pairs={{0,1},{1,0},{2,3},{3,2},{4,5},{5,4},{6,7},{7,6},{8,9},{9,8},{10,11... | collective-permute-start | bytes 2383880 | tf_op jit(solution)/shard_map/ppermute | solution.py:376
  58.3 5.5 %collective-permute-done.3.refs_8_.refs_10_ = bf16[1552,256]{1,0:T(8,128)(2,1)S(1)} collective-permute-done((bf16[1552,256]{1,0:T(8,128)(2,1)S(1)}, bf16[1552,256]{1,0:T(8,128)(2,1)S(1)}, u32[]{:S(2)}, u32[]{:S(2)}) %collective-permute-start.3) | collective-permute-done | bytes 794656 | tf_op jit(solution)/shard_map/ppermute | solution.py:376
  63.8 0.0 collective-permute-done.4.refs_6_.refs_12_
  63.8 0.7 collective-permute-start.5
  64.5 2.6 %collective-permute-start.12 = (bf16[1552,256]{1,0:T(8,128)(2,1)S(1)}, bf16[1552,256]{1,0:T(8,128)(2,1)S(1)}, u32[]{:S(2)}, u32[]{:S(2)}) collective-permute-start(bf16[1552,256]{1,0:T(8,128)(2,1)S(1)} %collective-permute-done.3.refs_8_.refs_10_), channel_id=1, source_target_pairs={{0,1},{1,0},{2,3},{3,2},{4,5},{5,4},{6,7},{7,6},{8,9},{9,8},{10,11... | collective-permute-start | bytes 2383880 | tf_op jit(solution)/shard_map/ppermute | solution.py:376
  67.1 0.0 collective-permute-done.10.refs_17_.value_ref.refs_4_
  67.1 8.6 %collective-permute-start.13 = (bf16[1552,256]{1,0:T(8,128)(2,1)S(1)}, bf16[1552,256]{1,0:T(8,128)(2,1)S(1)}, u32[]{:S(2)}, u32[]{:S(2)}) collective-permute-start(bf16[1552,256]{1,0:T(8,128)(2,1)S(1)} %collective-permute-done.10.refs_17_.value_ref.refs_4_), channel_id=1, source_target_pairs={{0,1},{1,0},{2,3},{3,2},{4,5},{5,4},{6,7},{7,6},{8,9},{9,8},{10,11... | collective-permute-start | bytes 2383880 | tf_op jit(solution)/shard_map/ppermute | solution.py:376
  75.7 0.0 collective-permute-start.14
  75.7 0.0 collective-permute-done.11.refs_3_.refs_13_
  75.7 0.5 collective-permute-start.15
  76.2 0.0 collective-permute-done.12.refs_4_.refs_14_
  76.2 1.1 %shard_map.70 = (bf16[8,512,256]{2,1,0:T(8,128)(2,1)S(1)}, f32[512,128]{1,0:T(8,128)S(1)}, bf16[16,256]{1,0:T(8,128)(2,1)S(1)}) custom-call(bf16[8,512,256]{2,1,0:T(8,128)(2,1)S(1)} %get-tuple-element.31.refs_0_, bf16[1552,256]{1,0:T(8,128)(2,1)S(1)} %collective-permute-done.7.refs_1_.refs_15_, ...), custom_call_target="tpu_custom_call" | custom-call | flops 1 | bytes 1 | tf_op jit(solution)/shard_map/pallas_call | solution.py:267
  77.3 0.0 collective-permute-done.5.refs_5_
  77.3 0.3 collective-permute-done.13.refs_8_
  77.6 6.8 %collective-permute-start.16 = (bf16[1552,256]{1,0:T(8,128)(2,1)S(1)}, bf16[1552,256]{1,0:T(8,128)(2,1)S(1)}, u32[]{:S(2)}, u32[]{:S(2)}) collective-permute-start(bf16[1552,256]{1,0:T(8,128)(2,1)S(1)} %collective-permute-done.5.refs_5_), channel_id=1, source_target_pairs={{0,1},{1,0},{2,3},{3,2},{4,5},{5,4},{6,7},{7,6},{8,9},{9,8},{10,11... | collective-permute-start | bytes 2383880 | tf_op jit(solution)/shard_map/ppermute | solution.py:376
  84.4 0.0 collective-permute-done.14.refs_6_
  84.5 0.0 collective-permute-done.15.refs_7_
  84.5 1.9 %collective-permute-done.16.refs_9_ = bf16[1552,256]{1,0:T(8,128)(2,1)S(1)} collective-permute-done((bf16[1552,256]{1,0:T(8,128)(2,1)S(1)}, bf16[1552,256]{1,0:T(8,128)(2,1)S(1)}, u32[]{:S(2)}, u32[]{:S(2)}) %collective-permute-start.16) | collective-permute-done | bytes 794656 | tf_op jit(solution)/shard_map/ppermute | solution.py:376
  86.4 1.9 %shard_map.72 = (bf16[1,512,2048]{2,1,0:T(8,128)(2,1)}, bf16[1,512]{1,0:T(2,128)(2,1)}) custom-call(bf16[8,512,256]{2,1,0:T(8,128)(2,1)S(1)} %get-tuple-element.40.refs_0_, f32[512,128]{1,0:T(8,128)S(1)} %get-tuple-element.41.refs_1_, f32[1,512]{1,0:T(1,128)S(1)} %get-tuple-element.42.refs_2_, bf16[16,256]{1,0:T(8,128)(2,1)S(1)} %get-tuple-element.43.refs_3_, ...), custom_call_target="tpu_custom_call" | custom-call | flops 1610612736 | bytes 7340032 | tf_op jit(solution)/shard_map/pallas_call | solution.py:344
  (1 shorter events, 0.0 us)
Async XLA Ops:
  2.9 9.1 %collective-permute-start = (bf16[1552,256]{1,0:T(8,128)(2,1)}, bf16[1552,256]{1,0:T(8,128)(2,1)S(1)}, u32[]{:S(2)}, u32[]{:S(2)}) collective-permute-start(bf16[1552,256]{1,0:T(8,128)(2,1)} %shard_map.68.own_ref), channel_id=1, source_target_pairs={{0,1},{1,0},{2,3},{3,2},{4,5},{5,4},{6,7},{7,6},{8,9},{9,8},{10,11... | collective-permute-start | bytes 2383880 | tf_op jit(solution)/shard_map/ppermute | solution.py:376
  6.3 17.2 %collective-permute-start.6 = (bf16[1552,256]{1,0:T(8,128)(2,1)}, bf16[1552,256]{1,0:T(8,128)(2,1)S(1)}, u32[]{:S(2)}, u32[]{:S(2)}) collective-permute-start(bf16[1552,256]{1,0:T(8,128)(2,1)} %shard_map.68.own_ref), channel_id=1, source_target_pairs={{0,0},{245,1},{2,2},{247,3},{4,4},{249,5},{6,6},{251,7},{8,8},{253... | collective-permute-start | bytes 2383880 | tf_op jit(solution)/shard_map/ppermute | solution.py:376
  12.0 20.0 %collective-permute-start.1 = (bf16[1552,256]{1,0:T(8,128)(2,1)S(1)}, bf16[1552,256]{1,0:T(8,128)(2,1)S(1)}, u32[]{:S(2)}, u32[]{:S(2)}) collective-permute-start(bf16[1552,256]{1,0:T(8,128)(2,1)S(1)} %collective-permute-done), channel_id=1, source_target_pairs={{0,0},{245,1},{2,2},{247,3},{4,4},{249,5},{6,6},{251,7},{8,8},{253... | collective-permute-start | bytes 2383880 | tf_op jit(solution)/shard_map/ppermute | solution.py:376
  23.5 14.7 %collective-permute-start.7 = (bf16[1552,256]{1,0:T(8,128)(2,1)S(1)}, bf16[1552,256]{1,0:T(8,128)(2,1)S(1)}, u32[]{:S(2)}, u32[]{:S(2)}) collective-permute-start(bf16[1552,256]{1,0:T(8,128)(2,1)S(1)} %collective-permute-done.6.refs_18_.refs_10_), channel_id=1, source_target_pairs={{14,0},{5,1},{12,2},{7,3},{0,4},{9,5},{2,6},{11,7},{4,8},{13,9},{6... | collective-permute-start | bytes 2383880 | tf_op jit(solution)/shard_map/ppermute | solution.py:376
  32.0 14.9 %collective-permute-start.2 = (bf16[1552,256]{1,0:T(8,128)(2,1)S(1)}, bf16[1552,256]{1,0:T(8,128)(2,1)S(1)}, u32[]{:S(2)}, u32[]{:S(2)}) collective-permute-start(bf16[1552,256]{1,0:T(8,128)(2,1)S(1)} %collective-permute-done.1.refs_11_), channel_id=1, source_target_pairs={{14,0},{5,1},{12,2},{7,3},{0,4},{9,5},{2,6},{11,7},{4,8},{13,9},{6... | collective-permute-start | bytes 2383880 | tf_op jit(solution)/shard_map/ppermute | solution.py:376
  38.2 17.0 %collective-permute-start.8 = (bf16[1552,256]{1,0:T(8,128)(2,1)S(1)}, bf16[1552,256]{1,0:T(8,128)(2,1)S(1)}, u32[]{:S(2)}, u32[]{:S(2)}) collective-permute-start(bf16[1552,256]{1,0:T(8,128)(2,1)S(1)} %collective-permute-done.7.refs_1_.refs_15_), channel_id=1, source_target_pairs={{254,0},{5,1},{252,2},{7,3},{0,4},{9,5},{2,6},{11,7},{4,8},{13,9},... | collective-permute-start | bytes 2383880 | tf_op jit(solution)/shard_map/ppermute | solution.py:376
  45.6 9.7 %collective-permute-start.9 = (bf16[1552,256]{1,0:T(8,128)(2,1)S(1)}, bf16[1552,256]{1,0:T(8,128)(2,1)S(1)}, u32[]{:S(2)}, u32[]{:S(2)}) collective-permute-start(bf16[1552,256]{1,0:T(8,128)(2,1)S(1)} %collective-permute-done.7.refs_1_.refs_15_), channel_id=1, source_target_pairs={{0,1},{1,0},{2,3},{3,2},{4,5},{5,4},{6,7},{7,6},{8,9},{9,8},{10,11... | collective-permute-start | bytes 2383880 | tf_op jit(solution)/shard_map/ppermute | solution.py:376
  45.6 1.1 %copy-start = (bf16[1552,256]{1,0:T(8,128)(2,1)S(1)}, bf16[1552,256]{1,0:T(8,128)(2,1)}, u32[]{:S(2)}) copy-start(bf16[1552,256]{1,0:T(8,128)(2,1)} %shard_map.68.own_ref) | copy-start | bytes 2383876
  47.0 16.8 %collective-permute-start.3 = (bf16[1552,256]{1,0:T(8,128)(2,1)S(1)}, bf16[1552,256]{1,0:T(8,128)(2,1)S(1)}, u32[]{:S(2)}, u32[]{:S(2)}) collective-permute-start(bf16[1552,256]{1,0:T(8,128)(2,1)S(1)} %collective-permute-done.2.refs_2_.refs_16_), channel_id=1, source_target_pairs={{254,0},{5,1},{252,2},{7,3},{0,4},{9,5},{2,6},{11,7},{4,8},{13,9},... | collective-permute-start | bytes 2383880 | tf_op jit(solution)/shard_map/ppermute | solution.py:376
  54.1 9.7 %collective-permute-start.4 = (bf16[1552,256]{1,0:T(8,128)(2,1)S(1)}, bf16[1552,256]{1,0:T(8,128)(2,1)S(1)}, u32[]{:S(2)}, u32[]{:S(2)}) collective-permute-start(bf16[1552,256]{1,0:T(8,128)(2,1)S(1)} %collective-permute-done.2.refs_2_.refs_16_), channel_id=1, source_target_pairs={{0,1},{1,0},{2,3},{3,2},{4,5},{5,4},{6,7},{7,6},{8,9},{9,8},{10,11... | collective-permute-start | bytes 2383880 | tf_op jit(solution)/shard_map/ppermute | solution.py:376
  55.3 11.8 %collective-permute-start.10 = (bf16[1552,256]{1,0:T(8,128)(2,1)S(1)}, bf16[1552,256]{1,0:T(8,128)(2,1)S(1)}, u32[]{:S(2)}, u32[]{:S(2)}) collective-permute-start(bf16[1552,256]{1,0:T(8,128)(2,1)S(1)} %collective-permute-done.8.refs_7_.refs_9_), channel_id=1, source_target_pairs={{254,0},{1,1},{252,2},{3,3},{0,4},{5,5},{2,6},{7,7},{4,8},{9,9},{6... | collective-permute-start | bytes 2383880 | tf_op jit(solution)/shard_map/ppermute | solution.py:376
  56.0 19.7 %collective-permute-start.11 = (bf16[1552,256]{1,0:T(8,128)(2,1)S(1)}, bf16[1552,256]{1,0:T(8,128)(2,1)S(1)}, u32[]{:S(2)}, u32[]{:S(2)}) collective-permute-start(bf16[1552,256]{1,0:T(8,128)(2,1)S(1)} %collective-permute-done.8.refs_7_.refs_9_), channel_id=1, source_target_pairs={{0,1},{1,0},{2,3},{3,2},{4,5},{5,4},{6,7},{7,6},{8,9},{9,8},{10,11... | collective-permute-start | bytes 2383880 | tf_op jit(solution)/shard_map/ppermute | solution.py:376
  63.8 13.5 %collective-permute-start.5 = (bf16[1552,256]{1,0:T(8,128)(2,1)S(1)}, bf16[1552,256]{1,0:T(8,128)(2,1)S(1)}, u32[]{:S(2)}, u32[]{:S(2)}) collective-permute-start(bf16[1552,256]{1,0:T(8,128)(2,1)S(1)} %collective-permute-done.3.refs_8_.refs_10_), channel_id=1, source_target_pairs={{254,0},{1,1},{252,2},{3,3},{0,4},{5,5},{2,6},{7,7},{4,8},{9,9},{6... | collective-permute-start | bytes 2383880 | tf_op jit(solution)/shard_map/ppermute | solution.py:376
  64.5 11.7 %collective-permute-start.12 = (bf16[1552,256]{1,0:T(8,128)(2,1)S(1)}, bf16[1552,256]{1,0:T(8,128)(2,1)S(1)}, u32[]{:S(2)}, u32[]{:S(2)}) collective-permute-start(bf16[1552,256]{1,0:T(8,128)(2,1)S(1)} %collective-permute-done.3.refs_8_.refs_10_), channel_id=1, source_target_pairs={{0,1},{1,0},{2,3},{3,2},{4,5},{5,4},{6,7},{7,6},{8,9},{9,8},{10,11... | collective-permute-start | bytes 2383880 | tf_op jit(solution)/shard_map/ppermute | solution.py:376
  67.1 10.6 %collective-permute-start.13 = (bf16[1552,256]{1,0:T(8,128)(2,1)S(1)}, bf16[1552,256]{1,0:T(8,128)(2,1)S(1)}, u32[]{:S(2)}, u32[]{:S(2)}) collective-permute-start(bf16[1552,256]{1,0:T(8,128)(2,1)S(1)} %collective-permute-done.10.refs_17_.value_ref.refs_4_), channel_id=1, source_target_pairs={{0,1},{1,0},{2,3},{3,2},{4,5},{5,4},{6,7},{7,6},{8,9},{9,8},{10,11... | collective-permute-start | bytes 2383880 | tf_op jit(solution)/shard_map/ppermute | solution.py:376
  75.7 8.8 %collective-permute-start.14 = (bf16[1552,256]{1,0:T(8,128)(2,1)S(1)}, bf16[1552,256]{1,0:T(8,128)(2,1)S(1)}, u32[]{:S(2)}, u32[]{:S(2)}) collective-permute-start(bf16[1552,256]{1,0:T(8,128)(2,1)S(1)} %collective-permute-done.6.refs_18_.refs_10_), channel_id=1, source_target_pairs={{0,1},{1,0},{2,3},{3,2},{4,5},{5,4},{6,7},{7,6},{8,9},{9,8},{10,11... | collective-permute-start | bytes 2383880 | tf_op jit(solution)/shard_map/ppermute | solution.py:376
  75.7 8.8 %collective-permute-start.15 = (bf16[1552,256]{1,0:T(8,128)(2,1)S(1)}, bf16[1552,256]{1,0:T(8,128)(2,1)S(1)}, u32[]{:S(2)}, u32[]{:S(2)}) collective-permute-start(bf16[1552,256]{1,0:T(8,128)(2,1)S(1)} %collective-permute-done.1.refs_11_), channel_id=1, source_target_pairs={{0,1},{1,0},{2,3},{3,2},{4,5},{5,4},{6,7},{7,6},{8,9},{9,8},{10,11... | collective-permute-start | bytes 2383880 | tf_op jit(solution)/shard_map/ppermute | solution.py:376
  77.6 8.8 %collective-permute-start.16 = (bf16[1552,256]{1,0:T(8,128)(2,1)S(1)}, bf16[1552,256]{1,0:T(8,128)(2,1)S(1)}, u32[]{:S(2)}, u32[]{:S(2)}) collective-permute-start(bf16[1552,256]{1,0:T(8,128)(2,1)S(1)} %collective-permute-done.5.refs_5_), channel_id=1, source_target_pairs={{0,1},{1,0},{2,3},{3,2},{4,5},{5,4},{6,7},{7,6},{8,9},{9,8},{10,11... | collective-permute-start | bytes 2383880 | tf_op jit(solution)/shard_map/ppermute | solution.py:376

commit v6 on v5

--- a/solution.py
+++ b/solution.py
@@ -22,7 +22,10 @@
     for step in range(STEPS):
         for half in range(2):
             for core, source in enumerate((up, down)):
-                from_step, from_half = source(step, half)
+                found = source(step, half)
+                if found is None:
+                    continue
+                from_step, from_half = found
                 pairs.append(
                     ((from_step % STEPS) * 4 + from_half * 2 + core, step * 4 + half * 2 + core)
                 )
@@ -34,7 +37,7 @@
 
 
 def below(t, h):
-    return t - 1, h if t % 4 > 0 else 1 - h
+    return (t - 1, h if t % 4 > 0 else 1 - h) if t > 0 else None
 
 
 HOPS = (
@@ -43,7 +46,7 @@
         lambda t, h: (t - 3, h if t % 4 < 3 else 1 - h),
     ),
     route(lambda t, h: (t - 1, h) if t % 4 > 0 else (t + 3, 1 - h), above),
-    route(below, above),
+    route(lambda t, h: (t - 1, h if t % 4 > 0 else 1 - h), above),
     route(below, lambda t, h: (t, h)),
 )
 SIBLING = [(i, i ^ 1) for i in range(STEPS * 4)]

time: 88.7 us -> 86 us (0.970)
  the two profiles are of different devices: /device:TPU:1 before, /device:TPU:7 now
where the time goes in v6:
time: 86 us; the launch traced here: 85.8 us
  starting transfers between devices  49.4 us (57%)
  waiting for transfers between devices  23.8 us (28%)
  Pallas kernels  10.6 us (12%)
  local copies, waits for them, and re-layouts  1.14 us (1%)
  between operations  0.89 us (1%)
    ppermute x17, starting transfers between devices, move(): x[name] = lax.ppermute(x[source], AXES, hop)  49.4 us
    ppermute x17, waiting for transfers between devices, move(): x[name] = lax.ppermute(x[source], AXES, hop)  23.8 us
    pallas_call x1, Pallas kernels, pair(): pl.pallas_call(pair_kernel, out_shape=[jax.ShapeDtypeStruct((NBLK, LOCAL,...  4.61 us
    pallas_call x1, Pallas kernels, last(): pl.pallas_call(last_kernel, out_shape=[jax.ShapeDtypeStruct((1, LOCAL, NB...  3.44 us
    pallas_call x1, Pallas kernels, prepare(): pl.pallas_call(prepare_kernel, out_shape=jax.ShapeDtypeStruct((TOKEN, BLK...  2.29 us
  transfers between devices with their start and end apart: 17, of which 7 were waited for; matrix products, arithmetic and copies ran while one was open for 0% of the time, Pallas kernels for 6%

profile of v6, /device:TPU:7, one launch (start us, length us, event | category | flops | bytes accessed | tf_op | source)
XLA Modules:
  0.0 85.8 jit_solution(4084489185556081653)
XLA Ops:
  0.6 2.3 %shard_map.68.own_ref = bf16[1552,256]{1,0:T(8,128)(2,1)} custom-call(s32[1,3]{1,0:T(1,128)} %refs_0_.1, bf16[1,3,512,256]{3,2,1,0:T(8,128)(2,1)} %refs_1_.1, s32[1,512]{1,0:T(1,128)} %refs_2_.1, f32[1,512]{1,0:T(1,128)} %refs_3_.1, f32[1,512]{1,0:T(1,128)} %bitcast.1), custom_call_target="tpu_custom_call" | custom-call | tf_op jit(solution)/shard_map/pallas_call | solution.py:91
  2.9 0.8 collective-permute-start
  3.7 7.5 %collective-permute-start.6 = (bf16[1552,256]{1,0:T(8,128)(2,1)}, bf16[1552,256]{1,0:T(8,128)(2,1)S(1)}, u32[]{:S(2)}, u32[]{:S(2)}) collective-permute-start(bf16[1552,256]{1,0:T(8,128)(2,1)} %shard_map.68.own_ref), channel_id=1, source_target_pairs={{0,0},{245,1},{2,2},{247,3},{4,4},{249,5},{6,6},{251,7},{8,8},{253... | collective-permute-start | bytes 2383880 | tf_op jit(solution)/shard_map/ppermute | solution.py:379
  11.2 0.0 collective-permute-done
  11.2 3.6 %collective-permute-start.1 = (bf16[1552,256]{1,0:T(8,128)(2,1)S(1)}, bf16[1552,256]{1,0:T(8,128)(2,1)S(1)}, u32[]{:S(2)}, u32[]{:S(2)}) collective-permute-start(bf16[1552,256]{1,0:T(8,128)(2,1)S(1)} %collective-permute-done), channel_id=1, source_target_pairs={{0,0},{245,1},{2,2},{247,3},{4,4},{249,5},{6,6},{251,7},{8,8},{253... | collective-permute-start | bytes 2383880 | tf_op jit(solution)/shard_map/ppermute | solution.py:379
  14.8 5.6 %collective-permute-done.6.refs_18_.refs_10_ = bf16[1552,256]{1,0:T(8,128)(2,1)S(1)} collective-permute-done((bf16[1552,256]{1,0:T(8,128)(2,1)}, bf16[1552,256]{1,0:T(8,128)(2,1)S(1)}, u32[]{:S(2)}, u32[]{:S(2)}) %collective-permute-start.6) | collective-permute-done | bytes 794656 | tf_op jit(solution)/shard_map/ppermute | solution.py:379
  20.5 5.7 %collective-permute-start.7 = (bf16[1552,256]{1,0:T(8,128)(2,1)S(1)}, bf16[1552,256]{1,0:T(8,128)(2,1)S(1)}, u32[]{:S(2)}, u32[]{:S(2)}) collective-permute-start(bf16[1552,256]{1,0:T(8,128)(2,1)S(1)} %collective-permute-done.6.refs_18_.refs_10_), channel_id=1, source_target_pairs={{14,0},{5,1},{12,2},{7,3},{0,4},{9,5},{2,6},{11,7},{4,8},{13,9},{6... | collective-permute-start | bytes 2383880 | tf_op jit(solution)/shard_map/ppermute | solution.py:379
  26.2 2.7 %collective-permute-done.1.refs_11_ = bf16[1552,256]{1,0:T(8,128)(2,1)S(1)} collective-permute-done((bf16[1552,256]{1,0:T(8,128)(2,1)S(1)}, bf16[1552,256]{1,0:T(8,128)(2,1)S(1)}, u32[]{:S(2)}, u32[]{:S(2)}) %collective-permute-start.1) | collective-permute-done | bytes 794656 | tf_op jit(solution)/shard_map/ppermute | solution.py:379
  28.9 5.8 %collective-permute-start.2 = (bf16[1552,256]{1,0:T(8,128)(2,1)S(1)}, bf16[1552,256]{1,0:T(8,128)(2,1)S(1)}, u32[]{:S(2)}, u32[]{:S(2)}) collective-permute-start(bf16[1552,256]{1,0:T(8,128)(2,1)S(1)} %collective-permute-done.1.refs_11_), channel_id=1, source_target_pairs={{14,0},{5,1},{12,2},{7,3},{0,4},{9,5},{2,6},{11,7},{4,8},{13,9},{6... | collective-permute-start | bytes 2383880 | tf_op jit(solution)/shard_map/ppermute | solution.py:379
  34.7 2.7 %collective-permute-done.7.refs_1_.refs_15_ = bf16[1552,256]{1,0:T(8,128)(2,1)S(1)} collective-permute-done((bf16[1552,256]{1,0:T(8,128)(2,1)S(1)}, bf16[1552,256]{1,0:T(8,128)(2,1)S(1)}, u32[]{:S(2)}, u32[]{:S(2)}) %collective-permute-start.7) | collective-permute-done | bytes 794656 | tf_op jit(solution)/shard_map/ppermute | solution.py:379
  37.4 6.1 %collective-permute-start.8 = (bf16[1552,256]{1,0:T(8,128)(2,1)S(1)}, bf16[1552,256]{1,0:T(8,128)(2,1)S(1)}, u32[]{:S(2)}, u32[]{:S(2)}) collective-permute-start(bf16[1552,256]{1,0:T(8,128)(2,1)S(1)} %collective-permute-done.7.refs_1_.refs_15_), channel_id=1, source_target_pairs={{254,0},{5,1},{252,2},{7,3},{0,4},{9,5},{2,6},{11,7},{4,8},{13,9},... | collective-permute-start | bytes 2383880 | tf_op jit(solution)/shard_map/ppermute | solution.py:379
  43.5 0.0 collective-permute-start.9
  43.5 0.0 copy-start
  43.5 1.1 %copy-done = bf16[1552,256]{1,0:T(8,128)(2,1)S(1)} copy-done((bf16[1552,256]{1,0:T(8,128)(2,1)S(1)}, bf16[1552,256]{1,0:T(8,128)(2,1)}, u32[]{:S(2)}) %copy-start) | copy-done | bytes 794648
  44.7 0.2 shard_map.69
  44.9 1.0 %collective-permute-done.2.refs_2_.refs_16_ = bf16[1552,256]{1,0:T(8,128)(2,1)S(1)} collective-permute-done((bf16[1552,256]{1,0:T(8,128)(2,1)S(1)}, bf16[1552,256]{1,0:T(8,128)(2,1)S(1)}, u32[]{:S(2)}, u32[]{:S(2)}) %collective-permute-start.2) | collective-permute-done | bytes 794656 | tf_op jit(solution)/shard_map/ppermute | solution.py:379
  45.9 6.1 %collective-permute-start.3 = (bf16[1552,256]{1,0:T(8,128)(2,1)S(1)}, bf16[1552,256]{1,0:T(8,128)(2,1)S(1)}, u32[]{:S(2)}, u32[]{:S(2)}) collective-permute-start(bf16[1552,256]{1,0:T(8,128)(2,1)S(1)} %collective-permute-done.2.refs_2_.refs_16_), channel_id=1, source_target_pairs={{254,0},{5,1},{252,2},{7,3},{0,4},{9,5},{2,6},{11,7},{4,8},{13,9},... | collective-permute-start | bytes 2383880 | tf_op jit(solution)/shard_map/ppermute | solution.py:379
  52.0 0.0 collective-permute-start.4
  52.0 2.4 %collective-permute-done.8.refs_7_.refs_9_ = bf16[1552,256]{1,0:T(8,128)(2,1)S(1)} collective-permute-done((bf16[1552,256]{1,0:T(8,128)(2,1)S(1)}, bf16[1552,256]{1,0:T(8,128)(2,1)S(1)}, u32[]{:S(2)}, u32[]{:S(2)}) %collective-permute-start.8) | collective-permute-done | bytes 794656 | tf_op jit(solution)/shard_map/ppermute | solution.py:379
  54.4 0.0 collective-permute-done.9.refs_5_.refs_11_
  54.4 0.7 collective-permute-start.10
  55.1 0.4 collective-permute-start.11
  55.5 7.4 %collective-permute-done.3.refs_8_.refs_10_ = bf16[1552,256]{1,0:T(8,128)(2,1)S(1)} collective-permute-done((bf16[1552,256]{1,0:T(8,128)(2,1)S(1)}, bf16[1552,256]{1,0:T(8,128)(2,1)S(1)}, u32[]{:S(2)}, u32[]{:S(2)}) %collective-permute-start.3) | collective-permute-done | bytes 794656 | tf_op jit(solution)/shard_map/ppermute | solution.py:379
  62.9 0.0 collective-permute-done.4.refs_6_.refs_12_
  63.0 0.7 collective-permute-start.5
  63.7 0.4 collective-permute-start.12
  64.1 0.0 collective-permute-done.10.refs_17_.value_ref.refs_4_
  64.1 7.7 %collective-permute-start.13 = (bf16[1552,256]{1,0:T(8,128)(2,1)S(1)}, bf16[1552,256]{1,0:T(8,128)(2,1)S(1)}, u32[]{:S(2)}, u32[]{:S(2)}) collective-permute-start(bf16[1552,256]{1,0:T(8,128)(2,1)S(1)} %collective-permute-done.10.refs_17_.value_ref.refs_4_), channel_id=1, source_target_pairs={{0,1},{1,0},{2,3},{3,2},{4,5},{5,4},{6,7},{7,6},{8,9},{9,8},{10,11... | collective-permute-start | bytes 2383880 | tf_op jit(solution)/shard_map/ppermute | solution.py:379
  71.7 0.0 collective-permute-start.14
  71.7 0.0 collective-permute-done.11.refs_3_.refs_13_
  71.7 0.5 collective-permute-start.15
  72.2 0.0 collective-permute-done.12.refs_4_.refs_14_
  72.2 4.6 %shard_map.70 = (bf16[8,512,256]{2,1,0:T(8,128)(2,1)S(1)}, f32[512,128]{1,0:T(8,128)S(1)}, bf16[16,256]{1,0:T(8,128)(2,1)S(1)}) custom-call(bf16[8,512,256]{2,1,0:T(8,128)(2,1)S(1)} %get-tuple-element.31.refs_0_, bf16[1552,256]{1,0:T(8,128)(2,1)S(1)} %collective-permute-done.7.refs_1_.refs_15_, ...), custom_call_target="tpu_custom_call" | custom-call | flops 1 | bytes 1 | tf_op jit(solution)/shard_map/pallas_call | solution.py:270
  76.9 0.0 collective-permute-done.5.refs_5_
  76.9 0.0 collective-permute-done.13.refs_8_
  76.9 3.4 %collective-permute-start.16 = (bf16[1552,256]{1,0:T(8,128)(2,1)S(1)}, bf16[1552,256]{1,0:T(8,128)(2,1)S(1)}, u32[]{:S(2)}, u32[]{:S(2)}) collective-permute-start(bf16[1552,256]{1,0:T(8,128)(2,1)S(1)} %collective-permute-done.5.refs_5_), channel_id=1, source_target_pairs={{0,1},{1,0},{2,3},{3,2},{4,5},{5,4},{6,7},{7,6},{8,9},{9,8},{10,11... | collective-permute-start | bytes 2383880 | tf_op jit(solution)/shard_map/ppermute | solution.py:379
  80.2 0.0 collective-permute-done.14.refs_6_
  80.2 0.0 collective-permute-done.15.refs_7_
  80.2 1.9 %collective-permute-done.16.refs_9_ = bf16[1552,256]{1,0:T(8,128)(2,1)S(1)} collective-permute-done((bf16[1552,256]{1,0:T(8,128)(2,1)S(1)}, bf16[1552,256]{1,0:T(8,128)(2,1)S(1)}, u32[]{:S(2)}, u32[]{:S(2)}) %collective-permute-start.16) | collective-permute-done | bytes 794656 | tf_op jit(solution)/shard_map/ppermute | solution.py:379
  82.2 3.4 %shard_map.72 = (bf16[1,512,2048]{2,1,0:T(8,128)(2,1)}, bf16[1,512]{1,0:T(2,128)(2,1)}) custom-call(bf16[8,512,256]{2,1,0:T(8,128)(2,1)S(1)} %get-tuple-element.40.refs_0_, f32[512,128]{1,0:T(8,128)S(1)} %get-tuple-element.41.refs_1_, f32[1,512]{1,0:T(1,128)S(1)} %get-tuple-element.42.refs_2_, bf16[16,256]{1,0:T(8,128)(2,1)S(1)} %get-tuple-element.43.refs_3_, ...), custom_call_target="tpu_custom_call" | custom-call | flops 1610612736 | bytes 7340032 | tf_op jit(solution)/shard_map/pallas_call | solution.py:347
  (1 shorter events, 0.0 us)
Async XLA Ops:
  2.9 8.2 %collective-permute-start = (bf16[1552,256]{1,0:T(8,128)(2,1)}, bf16[1552,256]{1,0:T(8,128)(2,1)S(1)}, u32[]{:S(2)}, u32[]{:S(2)}) collective-permute-start(bf16[1552,256]{1,0:T(8,128)(2,1)} %shard_map.68.own_ref), channel_id=1, source_target_pairs={{0,1},{1,0},{2,3},{3,2},{4,5},{5,4},{6,7},{7,6},{8,9},{9,8},{10,11... | collective-permute-start | bytes 2383880 | tf_op jit(solution)/shard_map/ppermute | solution.py:379
  3.7 16.8 %collective-permute-start.6 = (bf16[1552,256]{1,0:T(8,128)(2,1)}, bf16[1552,256]{1,0:T(8,128)(2,1)S(1)}, u32[]{:S(2)}, u32[]{:S(2)}) collective-permute-start(bf16[1552,256]{1,0:T(8,128)(2,1)} %shard_map.68.own_ref), channel_id=1, source_target_pairs={{0,0},{245,1},{2,2},{247,3},{4,4},{249,5},{6,6},{251,7},{8,8},{253... | collective-permute-start | bytes 2383880 | tf_op jit(solution)/shard_map/ppermute | solution.py:379
  11.2 17.7 %collective-permute-start.1 = (bf16[1552,256]{1,0:T(8,128)(2,1)S(1)}, bf16[1552,256]{1,0:T(8,128)(2,1)S(1)}, u32[]{:S(2)}, u32[]{:S(2)}) collective-permute-start(bf16[1552,256]{1,0:T(8,128)(2,1)S(1)} %collective-permute-done), channel_id=1, source_target_pairs={{0,0},{245,1},{2,2},{247,3},{4,4},{249,5},{6,6},{251,7},{8,8},{253... | collective-permute-start | bytes 2383880 | tf_op jit(solution)/shard_map/ppermute | solution.py:379
  20.5 16.9 %collective-permute-start.7 = (bf16[1552,256]{1,0:T(8,128)(2,1)S(1)}, bf16[1552,256]{1,0:T(8,128)(2,1)S(1)}, u32[]{:S(2)}, u32[]{:S(2)}) collective-permute-start(bf16[1552,256]{1,0:T(8,128)(2,1)S(1)} %collective-permute-done.6.refs_18_.refs_10_), channel_id=1, source_target_pairs={{14,0},{5,1},{12,2},{7,3},{0,4},{9,5},{2,6},{11,7},{4,8},{13,9},{6... | collective-permute-start | bytes 2383880 | tf_op jit(solution)/shard_map/ppermute | solution.py:379
  28.9 17.0 %collective-permute-start.2 = (bf16[1552,256]{1,0:T(8,128)(2,1)S(1)}, bf16[1552,256]{1,0:T(8,128)(2,1)S(1)}, u32[]{:S(2)}, u32[]{:S(2)}) collective-permute-start(bf16[1552,256]{1,0:T(8,128)(2,1)S(1)} %collective-permute-done.1.refs_11_), channel_id=1, source_target_pairs={{14,0},{5,1},{12,2},{7,3},{0,4},{9,5},{2,6},{11,7},{4,8},{13,9},{6... | collective-permute-start | bytes 2383880 | tf_op jit(solution)/shard_map/ppermute | solution.py:379
  37.4 17.0 %collective-permute-start.8 = (bf16[1552,256]{1,0:T(8,128)(2,1)S(1)}, bf16[1552,256]{1,0:T(8,128)(2,1)S(1)}, u32[]{:S(2)}, u32[]{:S(2)}) collective-permute-start(bf16[1552,256]{1,0:T(8,128)(2,1)S(1)} %collective-permute-done.7.refs_1_.refs_15_), channel_id=1, source_target_pairs={{254,0},{5,1},{252,2},{7,3},{0,4},{9,5},{2,6},{11,7},{4,8},{13,9},... | collective-permute-start | bytes 2383880 | tf_op jit(solution)/shard_map/ppermute | solution.py:379
  43.5 10.9 %collective-permute-start.9 = (bf16[1552,256]{1,0:T(8,128)(2,1)S(1)}, bf16[1552,256]{1,0:T(8,128)(2,1)S(1)}, u32[]{:S(2)}, u32[]{:S(2)}) collective-permute-start(bf16[1552,256]{1,0:T(8,128)(2,1)S(1)} %collective-permute-done.7.refs_1_.refs_15_), channel_id=1, source_target_pairs={{0,1},{1,0},{2,3},{3,2},{4,5},{5,4},{6,7},{7,6},{8,9},{9,8},{10,11... | collective-permute-start | bytes 2383880 | tf_op jit(solution)/shard_map/ppermute | solution.py:379
  43.5 1.1 %copy-start = (bf16[1552,256]{1,0:T(8,128)(2,1)S(1)}, bf16[1552,256]{1,0:T(8,128)(2,1)}, u32[]{:S(2)}) copy-start(bf16[1552,256]{1,0:T(8,128)(2,1)} %shard_map.68.own_ref) | copy-start | bytes 2383876
  45.9 17.0 %collective-permute-start.3 = (bf16[1552,256]{1,0:T(8,128)(2,1)S(1)}, bf16[1552,256]{1,0:T(8,128)(2,1)S(1)}, u32[]{:S(2)}, u32[]{:S(2)}) collective-permute-start(bf16[1552,256]{1,0:T(8,128)(2,1)S(1)} %collective-permute-done.2.refs_2_.refs_16_), channel_id=1, source_target_pairs={{254,0},{5,1},{252,2},{7,3},{0,4},{9,5},{2,6},{11,7},{4,8},{13,9},... | collective-permute-start | bytes 2383880 | tf_op jit(solution)/shard_map/ppermute | solution.py:379
  52.0 10.9 %collective-permute-start.4 = (bf16[1552,256]{1,0:T(8,128)(2,1)S(1)}, bf16[1552,256]{1,0:T(8,128)(2,1)S(1)}, u32[]{:S(2)}, u32[]{:S(2)}) collective-permute-start(bf16[1552,256]{1,0:T(8,128)(2,1)S(1)} %collective-permute-done.2.refs_2_.refs_16_), channel_id=1, source_target_pairs={{0,1},{1,0},{2,3},{3,2},{4,5},{5,4},{6,7},{7,6},{8,9},{9,8},{10,11... | collective-permute-start | bytes 2383880 | tf_op jit(solution)/shard_map/ppermute | solution.py:379
  54.4 9.6 %collective-permute-start.10 = (bf16[1552,256]{1,0:T(8,128)(2,1)S(1)}, bf16[1552,256]{1,0:T(8,128)(2,1)S(1)}, u32[]{:S(2)}, u32[]{:S(2)}) collective-permute-start(bf16[1552,256]{1,0:T(8,128)(2,1)S(1)} %collective-permute-done.8.refs_7_.refs_9_), channel_id=1, source_target_pairs={{1,1},{3,3},{0,4},{5,5},{2,6},{7,7},{4,8},{9,9},{6,10},{11,11},{8,... | collective-permute-start | bytes 2383880 | tf_op jit(solution)/shard_map/ppermute | solution.py:379
  55.1 16.6 %collective-permute-start.11 = (bf16[1552,256]{1,0:T(8,128)(2,1)S(1)}, bf16[1552,256]{1,0:T(8,128)(2,1)S(1)}, u32[]{:S(2)}, u32[]{:S(2)}) collective-permute-start(bf16[1552,256]{1,0:T(8,128)(2,1)S(1)} %collective-permute-done.8.refs_7_.refs_9_), channel_id=1, source_target_pairs={{0,1},{1,0},{2,3},{3,2},{4,5},{5,4},{6,7},{7,6},{8,9},{9,8},{10,11... | collective-permute-start | bytes 2383880 | tf_op jit(solution)/shard_map/ppermute | solution.py:379
  63.0 13.9 %collective-permute-start.5 = (bf16[1552,256]{1,0:T(8,128)(2,1)S(1)}, bf16[1552,256]{1,0:T(8,128)(2,1)S(1)}, u32[]{:S(2)}, u32[]{:S(2)}) collective-permute-start(bf16[1552,256]{1,0:T(8,128)(2,1)S(1)} %collective-permute-done.3.refs_8_.refs_10_), channel_id=1, source_target_pairs={{1,1},{3,3},{0,4},{5,5},{2,6},{7,7},{4,8},{9,9},{6,10},{11,11},{8,... | collective-permute-start | bytes 2383880 | tf_op jit(solution)/shard_map/ppermute | solution.py:379
  63.7 8.6 %collective-permute-start.12 = (bf16[1552,256]{1,0:T(8,128)(2,1)S(1)}, bf16[1552,256]{1,0:T(8,128)(2,1)S(1)}, u32[]{:S(2)}, u32[]{:S(2)}) collective-permute-start(bf16[1552,256]{1,0:T(8,128)(2,1)S(1)} %collective-permute-done.3.refs_8_.refs_10_), channel_id=1, source_target_pairs={{0,1},{1,0},{2,3},{3,2},{4,5},{5,4},{6,7},{7,6},{8,9},{9,8},{10,11... | collective-permute-start | bytes 2383880 | tf_op jit(solution)/shard_map/ppermute | solution.py:379
  64.1 12.8 %collective-permute-start.13 = (bf16[1552,256]{1,0:T(8,128)(2,1)S(1)}, bf16[1552,256]{1,0:T(8,128)(2,1)S(1)}, u32[]{:S(2)}, u32[]{:S(2)}) collective-permute-start(bf16[1552,256]{1,0:T(8,128)(2,1)S(1)} %collective-permute-done.10.refs_17_.value_ref.refs_4_), channel_id=1, source_target_pairs={{0,1},{1,0},{2,3},{3,2},{4,5},{5,4},{6,7},{7,6},{8,9},{9,8},{10,11... | collective-permute-start | bytes 2383880 | tf_op jit(solution)/shard_map/ppermute | solution.py:379
  71.7 8.5 %collective-permute-start.14 = (bf16[1552,256]{1,0:T(8,128)(2,1)S(1)}, bf16[1552,256]{1,0:T(8,128)(2,1)S(1)}, u32[]{:S(2)}, u32[]{:S(2)}) collective-permute-start(bf16[1552,256]{1,0:T(8,128)(2,1)S(1)} %collective-permute-done.6.refs_18_.refs_10_), channel_id=1, source_target_pairs={{0,1},{1,0},{2,3},{3,2},{4,5},{5,4},{6,7},{7,6},{8,9},{9,8},{10,11... | collective-permute-start | bytes 2383880 | tf_op jit(solution)/shard_map/ppermute | solution.py:379
  71.7 8.5 %collective-permute-start.15 = (bf16[1552,256]{1,0:T(8,128)(2,1)S(1)}, bf16[1552,256]{1,0:T(8,128)(2,1)S(1)}, u32[]{:S(2)}, u32[]{:S(2)}) collective-permute-start(bf16[1552,256]{1,0:T(8,128)(2,1)S(1)} %collective-permute-done.1.refs_11_), channel_id=1, source_target_pairs={{0,1},{1,0},{2,3},{3,2},{4,5},{5,4},{6,7},{7,6},{8,9},{9,8},{10,11... | collective-permute-start | bytes 2383880 | tf_op jit(solution)/shard_map/ppermute | solution.py:379
  76.9 5.3 %collective-permute-start.16 = (bf16[1552,256]{1,0:T(8,128)(2,1)S(1)}, bf16[1552,256]{1,0:T(8,128)(2,1)S(1)}, u32[]{:S(2)}, u32[]{:S(2)}) collective-permute-start(bf16[1552,256]{1,0:T(8,128)(2,1)S(1)} %collective-permute-done.5.refs_5_), channel_id=1, source_target_pairs={{0,1},{1,0},{2,3},{3,2},{4,5},{5,4},{6,7},{7,6},{8,9},{9,8},{10,11... | collective-permute-start | bytes 2383880 | tf_op jit(solution)/shard_map/ppermute | solution.py:379

commit v7 on v6

--- a/solution.py
+++ b/solution.py
@@ -289,14 +289,93 @@
     )(bare, *first, *second, *third)
 
 
+def most_kernel(*refs):
+    before, total_ref, tile, third = refs[0], refs[1], refs[2], refs[3:9]
+    sum_ref, sum_total_ref = refs[9:11]
+    earlier, sems = refs[11:]
+    step, place = lax.axis_index("tm"), lax.axis_index("rows")
+    side = jnp.where(step % 4 >= 3, place // 2, 1 - place // 2)
+    groups = [2 * side, 2 * (1 - side) + 1, 2 * (1 - side)]
+    pairs = [
+        [
+            pltpu.make_async_copy(third[3 * core + n], earlier.at[groups[n]], sems.at[n])
+            for n in range(3)
+        ]
+        for core in range(2)
+    ]
+    for core in range(2):
+
+        @pl.when(place % 2 == core)
+        def _():
+            for copy in pairs[core]:
+                copy.start()
+
+    earlier[2 * side + 1] = jnp.zeros((TOKEN, BLK), jnp.bfloat16)
+    shifts = shifts_of(tile_of(tile))
+    for copy in pairs[0]:
+        copy.wait()
+
+    @pl.when(step >= 3)
+    def _():
+        tiles = [tile_of(earlier.at[g]) for g in range(4)]
+        sum_total_ref[...] = total_ref[...]
+        for c in range(NBLK):
+            sum_ref[c] = column_of(before, earlier, shifts, c)
+            term = before[c].astype(jnp.float32) * vector_of(tiles, c)
+            sum_total_ref[...] += term[:, :128] + term[:, 128:]
+
+    @pl.when(step < 3)
+    def _():
+        sum_total_ref[...] = total_ref[...]
+        for c in range(NBLK):
+            sum_ref[c] = before[c].astype(jnp.float32)
+
+
+def most(before, total, tile, third):
+    anywhere, vmem = pl.BlockSpec(memory_space=pl.ANY), pl.BlockSpec(memory_space=pltpu.VMEM)
+    return pl.pallas_call(
+        most_kernel,
+        out_shape=[
+            jax.ShapeDtypeStruct((NBLK, LOCAL, BLK), jnp.float32),
+            jax.ShapeDtypeStruct((LOCAL, 128), jnp.float32),
+        ],
+        in_specs=[vmem] * 3 + [anywhere] * 6,
+        out_specs=[vmem, vmem],
+        scratch_shapes=[
+            pltpu.VMEM((4, TOKEN, BLK), jnp.bfloat16),
+            pltpu.SemaphoreType.DMA((3,)),
+        ],
+        compiler_params=pltpu.CompilerParams(vmem_limit_bytes=14 * 1024 * 1024),
+        cost_estimate=pl.CostEstimate(
+            flops=48 * 2 * BLK**3, bytes_accessed=7 * 2**20, transcendentals=0
+        ),
+    )(before, total, tile, *third)
+
+
 def last_kernel(*refs):
-    before, total_ref, own_ref, tile, third = refs[0], refs[1], refs[2], refs[3], refs[4:12]
-    matrix_ref, vector_ref = refs[13:15]
-    earlier, result, vector, sems, out_sems = refs[15:]
-    step = lax.axis_index("tm")
-    start, wait = gather(third, earlier, 3, sems)
-    start()
+    before, sum_ref, total_ref, own_ref, tile, final = *refs[:5], refs[5:7]
+    matrix_ref, vector_ref = refs[8:10]
+    result, vector, out_sems = refs[10:]
+    step, place = lax.axis_index("tm"), lax.axis_index("rows")
+    group = 2 * jnp.where(step % 4 >= 3, place // 2, 1 - place // 2) + 1
     shifts = shifts_of(tile_of(tile))
+    for core, piece in enumerate(final):
+
+        @pl.when((step >= 3) & (place % 2 == core))
+        def _():
+            own_tile = tile_of(piece)
+            total = total_ref[...]
+            for r in range(2):
+                k = 2 * group + r
+                for j in range(NBAND):
+                    at = TILE + (2 * j + r) * BLK
+                    sum_ref[lax.rem(k + shifts[j] + NBLK, NBLK)] += jnp.dot(
+                        before[k], piece[at : at + BLK, :], preferred_element_type=jnp.float32
+                    )
+                term = before[k].astype(jnp.float32) * own_tile[r : r + 1, :]
+                total = total + (term[:, :128] + term[:, 128:])
+            total_ref[...] = total
+
     writes = [
         pltpu.make_async_copy(
             result.at[c], matrix_ref.at[0, :, c * BLK : (c + 1) * BLK], out_sems.at[c]
@@ -304,45 +383,24 @@
         for c in range(NBLK)
     ]
     writes.append(pltpu.make_async_copy(vector, vector_ref, out_sems.at[NBLK]))
-
-    def finish(total):
-        high = total.astype(jnp.bfloat16)
-        low = (total - high.astype(jnp.float32)).astype(jnp.bfloat16)
-        ones = jnp.ones((TILE, 128), jnp.bfloat16)
-        sums = sum(
-            lax.dot_general(
-                ones, part, (((1,), (1,)), ((), ())), preferred_element_type=jnp.float32
-            )
-            for part in (high, low)
-        )
-        vector[...] = (sums[0:1, :] + own_ref[...]).astype(jnp.bfloat16)
-        writes[NBLK].start()
-
-    wait()
-
-    @pl.when(step >= 3)
-    def _():
-        tiles = [tile_of(earlier.at[g]) for g in range(4)]
-        for c in range(NBLK):
-            result[c] = column_of(before, earlier, shifts, c).astype(jnp.bfloat16)
-            term = before[c].astype(jnp.float32) * vector_of(tiles, c)
-            total_ref[...] += term[:, :128] + term[:, 128:]
-            if c == NBLK - 1:
-                finish(total_ref[...])
-            writes[c].start()
-
-    @pl.when(step < 3)
-    def _():
-        for c in range(NBLK):
-            result[c] = before[c]
-            writes[c].start()
-        finish(total_ref[...])
-
+    for c in range(NBLK):
+        result[c] = sum_ref[c].astype(jnp.bfloat16)
+        writes[c].start()
+    total = total_ref[...]
+    high = total.astype(jnp.bfloat16)
+    low = (total - high.astype(jnp.float32)).astype(jnp.bfloat16)
+    ones = jnp.ones((TILE, 128), jnp.bfloat16)
+    sums = sum(
+        lax.dot_general(ones, part, (((1,), (1,)), ((), ())), preferred_element_type=jnp.float32)
+        for part in (high, low)
+    )
+    vector[...] = (sums[0:1, :] + own_ref[...]).astype(jnp.bfloat16)
+    writes[NBLK].start()
     for write in writes:
         write.wait()
 
 
-def last(before, total, own, tile, third, mark):
+def last(before, partial, total, own, tile, final, mark):
     anywhere, vmem = pl.BlockSpec(memory_space=pl.ANY), pl.BlockSpec(memory_space=pltpu.VMEM)
     return pl.pallas_call(
         last_kernel,
@@ -350,20 +408,18 @@
             jax.ShapeDtypeStruct((1, LOCAL, NBLK * BLK), jnp.bfloat16),
             jax.ShapeDtypeStruct((1, LOCAL), jnp.bfloat16),
         ],
-        in_specs=[vmem] * 4 + [anywhere] * 9,
+        in_specs=[vmem] * 7 + [anywhere],
         out_specs=[anywhere, anywhere],
         scratch_shapes=[
-            pltpu.VMEM((4, TOKEN, BLK), jnp.bfloat16),
             pltpu.VMEM((NBLK, LOCAL, BLK), jnp.bfloat16),
             pltpu.VMEM((1, LOCAL), jnp.bfloat16),
-            pltpu.SemaphoreType.DMA((4,)),
             pltpu.SemaphoreType.DMA((NBLK + 1,)),
         ],
         compiler_params=pltpu.CompilerParams(vmem_limit_bytes=14 * 1024 * 1024),
         cost_estimate=pl.CostEstimate(
-            flops=48 * 2 * BLK**3, bytes_accessed=7 * 2**20, transcendentals=0
+            flops=12 * 2 * BLK**3, bytes_accessed=7 * 2**20, transcendentals=0
         ),
-    )(before, total, own, tile, *third, mark)
+    )(before, partial, total, own, tile, *final, mark)
 
 
 def after(arrays, later, earlier):
@@ -411,8 +467,16 @@
     move("s4a", "4a", SIBLING)
     after(x, ["4b"], ["product", "s4a"])
     move("s4b", "4b", SIBLING)
-    third = [x[n] for n in ("4a", "4b", "s1a", "s1b", "s4a", "s4b", "1a", "1b")]
-    return tuple(last(x["product"], x["total"], x["vector"], tile, third, x["mark"]))
+    x["sum"], x["sum_total"] = most(
+        x["product"],
+        x["total"],
+        tile,
+        [x[n] for n in ("4a", "s1a", "s1b", "s4a", "1a", "1b")],
+    )
+    final = [x["4b"], x["s4b"]]
+    return tuple(
+        last(x["product"], x["sum"], x["sum_total"], x["vector"], tile, final, x["mark"])
+    )
 
 
 def solution(mesh):

time: 86 us -> 85.8 us (level)
  waiting for transfers between devices: 23.8 us -> 21.8 us
  Pallas kernels: 10.6 us -> 12.2 us
    pallas_call x0 -> x1, Pallas kernels: none -> 2.65 us  [most(): pl.pallas_call(most_kernel, out_shape=[jax.ShapeDtypeStruct((NBLK, LOCAL,...]
    ppermute x17, waiting for transfers between devices: 23.8 us -> 21.8 us  [move(): x[name] = lax.ppermute(x[source], AXES, hop)]
    pallas_call x1, Pallas kernels: 3.44 us -> 2.46 us  [last(): pl.pallas_call(last_kernel, out_shape=[jax.ShapeDtypeStruct((1, LOCAL, NB...]
  transfers between devices with their start and end apart: 17 -> 17, of which waited for: 7 -> 6; matrix products, arithmetic and copies ran while one was open for 0% -> 0% of each run, Pallas kernels for 6% -> 9%
where the time goes in v7:
time: 85.8 us; the launch traced here: 85.5 us
  starting transfers between devices  49.4 us (58%)
  waiting for transfers between devices  21.8 us (25%)
  Pallas kernels  12.2 us (14%)
  local copies, waits for them, and re-layouts  1.14 us (1%)
  between operations  0.9 us (1%)
    ppermute x17, starting transfers between devices, move(): x[name] = lax.ppermute(x[source], AXES, hop)  49.4 us
    ppermute x17, waiting for transfers between devices, move(): x[name] = lax.ppermute(x[source], AXES, hop)  21.8 us
    pallas_call x1, Pallas kernels, pair(): pl.pallas_call(pair_kernel, out_shape=[jax.ShapeDtypeStruct((NBLK, LOCAL,...  4.61 us
    pallas_call x1, Pallas kernels, most(): pl.pallas_call(most_kernel, out_shape=[jax.ShapeDtypeStruct((NBLK, LOCAL,...  2.65 us
    pallas_call x1, Pallas kernels, last(): pl.pallas_call(last_kernel, out_shape=[jax.ShapeDtypeStruct((1, LOCAL, NB...  2.46 us
    pallas_call x1, Pallas kernels, prepare(): pl.pallas_call(prepare_kernel, out_shape=jax.ShapeDtypeStruct((TOKEN, BLK...  2.29 us
  transfers between devices with their start and end apart: 17, of which 6 were waited for; matrix products, arithmetic and copies ran while one was open for 0% of the time, Pallas kernels for 9%

profile of v7, /device:TPU:7, one launch (start us, length us, event | category | flops | bytes accessed | tf_op | source)
XLA Modules:
  0.0 85.5 jit_solution(15194649175120531585)
XLA Ops:
  0.6 2.3 %shard_map.68.own_ref = bf16[1552,256]{1,0:T(8,128)(2,1)} custom-call(s32[1,3]{1,0:T(1,128)} %refs_0_.1, bf16[1,3,512,256]{3,2,1,0:T(8,128)(2,1)} %refs_1_.1, s32[1,512]{1,0:T(1,128)} %refs_2_.1, f32[1,512]{1,0:T(1,128)} %refs_3_.1, f32[1,512]{1,0:T(1,128)} %bitcast.1), custom_call_target="tpu_custom_call" | custom-call | tf_op jit(solution)/shard_map/pallas_call | solution.py:91
  2.9 0.8 collective-permute-start
  3.7 7.5 %collective-permute-start.6 = (bf16[1552,256]{1,0:T(8,128)(2,1)}, bf16[1552,256]{1,0:T(8,128)(2,1)S(1)}, u32[]{:S(2)}, u32[]{:S(2)}) collective-permute-start(bf16[1552,256]{1,0:T(8,128)(2,1)} %shard_map.68.own_ref), channel_id=1, source_target_pairs={{0,0},{245,1},{2,2},{247,3},{4,4},{249,5},{6,6},{251,7},{8,8},{253... | collective-permute-start | bytes 2383880 | tf_op jit(solution)/shard_map/ppermute | solution.py:435
  11.2 0.0 collective-permute-done
  11.2 3.6 %collective-permute-start.1 = (bf16[1552,256]{1,0:T(8,128)(2,1)S(1)}, bf16[1552,256]{1,0:T(8,128)(2,1)S(1)}, u32[]{:S(2)}, u32[]{:S(2)}) collective-permute-start(bf16[1552,256]{1,0:T(8,128)(2,1)S(1)} %collective-permute-done), channel_id=1, source_target_pairs={{0,0},{245,1},{2,2},{247,3},{4,4},{249,5},{6,6},{251,7},{8,8},{253... | collective-permute-start | bytes 2383880 | tf_op jit(solution)/shard_map/ppermute | solution.py:435
  14.8 5.6 %collective-permute-done.6.refs_18_.refs_7_ = bf16[1552,256]{1,0:T(8,128)(2,1)S(1)} collective-permute-done((bf16[1552,256]{1,0:T(8,128)(2,1)}, bf16[1552,256]{1,0:T(8,128)(2,1)S(1)}, u32[]{:S(2)}, u32[]{:S(2)}) %collective-permute-start.6) | collective-permute-done | bytes 794656 | tf_op jit(solution)/shard_map/ppermute | solution.py:435
  20.5 5.7 %collective-permute-start.7 = (bf16[1552,256]{1,0:T(8,128)(2,1)S(1)}, bf16[1552,256]{1,0:T(8,128)(2,1)S(1)}, u32[]{:S(2)}, u32[]{:S(2)}) collective-permute-start(bf16[1552,256]{1,0:T(8,128)(2,1)S(1)} %collective-permute-done.6.refs_18_.refs_7_), channel_id=1, source_target_pairs={{14,0},{5,1},{12,2},{7,3},{0,4},{9,5},{2,6},{11,7},{4,8},{13,9},{6... | collective-permute-start | bytes 2383880 | tf_op jit(solution)/shard_map/ppermute | solution.py:435
  26.2 2.7 %collective-permute-done.1.refs_8_ = bf16[1552,256]{1,0:T(8,128)(2,1)S(1)} collective-permute-done((bf16[1552,256]{1,0:T(8,128)(2,1)S(1)}, bf16[1552,256]{1,0:T(8,128)(2,1)S(1)}, u32[]{:S(2)}, u32[]{:S(2)}) %collective-permute-start.1) | collective-permute-done | bytes 794656 | tf_op jit(solution)/shard_map/ppermute | solution.py:435
  28.9 5.8 %collective-permute-start.2 = (bf16[1552,256]{1,0:T(8,128)(2,1)S(1)}, bf16[1552,256]{1,0:T(8,128)(2,1)S(1)}, u32[]{:S(2)}, u32[]{:S(2)}) collective-permute-start(bf16[1552,256]{1,0:T(8,128)(2,1)S(1)} %collective-permute-done.1.refs_8_), channel_id=1, source_target_pairs={{14,0},{5,1},{12,2},{7,3},{0,4},{9,5},{2,6},{11,7},{4,8},{13,9},{6... | collective-permute-start | bytes 2383880 | tf_op jit(solution)/shard_map/ppermute | solution.py:435
  34.7 2.7 %collective-permute-done.7.refs_1_.refs_15_ = bf16[1552,256]{1,0:T(8,128)(2,1)S(1)} collective-permute-done((bf16[1552,256]{1,0:T(8,128)(2,1)S(1)}, bf16[1552,256]{1,0:T(8,128)(2,1)S(1)}, u32[]{:S(2)}, u32[]{:S(2)}) %collective-permute-start.7) | collective-permute-done | bytes 794656 | tf_op jit(solution)/shard_map/ppermute | solution.py:435
  37.4 6.1 %collective-permute-start.8 = (bf16[1552,256]{1,0:T(8,128)(2,1)S(1)}, bf16[1552,256]{1,0:T(8,128)(2,1)S(1)}, u32[]{:S(2)}, u32[]{:S(2)}) collective-permute-start(bf16[1552,256]{1,0:T(8,128)(2,1)S(1)} %collective-permute-done.7.refs_1_.refs_15_), channel_id=1, source_target_pairs={{254,0},{5,1},{252,2},{7,3},{0,4},{9,5},{2,6},{11,7},{4,8},{13,9},... | collective-permute-start | bytes 2383880 | tf_op jit(solution)/shard_map/ppermute | solution.py:435
  43.5 0.0 collective-permute-start.9
  43.5 0.0 copy-start
  43.5 1.1 %copy-done = bf16[1552,256]{1,0:T(8,128)(2,1)S(1)} copy-done((bf16[1552,256]{1,0:T(8,128)(2,1)S(1)}, bf16[1552,256]{1,0:T(8,128)(2,1)}, u32[]{:S(2)}) %copy-start) | copy-done | bytes 794648
  44.7 0.2 shard_map.69
  44.9 1.0 %collective-permute-done.2.refs_2_.refs_16_ = bf16[1552,256]{1,0:T(8,128)(2,1)S(1)} collective-permute-done((bf16[1552,256]{1,0:T(8,128)(2,1)S(1)}, bf16[1552,256]{1,0:T(8,128)(2,1)S(1)}, u32[]{:S(2)}, u32[]{:S(2)}) %collective-permute-start.2) | collective-permute-done | bytes 794656 | tf_op jit(solution)/shard_map/ppermute | solution.py:435
  45.9 6.1 %collective-permute-start.3 = (bf16[1552,256]{1,0:T(8,128)(2,1)S(1)}, bf16[1552,256]{1,0:T(8,128)(2,1)S(1)}, u32[]{:S(2)}, u32[]{:S(2)}) collective-permute-start(bf16[1552,256]{1,0:T(8,128)(2,1)S(1)} %collective-permute-done.2.refs_2_.refs_16_), channel_id=1, source_target_pairs={{254,0},{5,1},{252,2},{7,3},{0,4},{9,5},{2,6},{11,7},{4,8},{13,9},... | collective-permute-start | bytes 2383880 | tf_op jit(solution)/shard_map/ppermute | solution.py:435
  52.0 0.0 collective-permute-start.4
  52.0 2.4 %collective-permute-done.8.refs_7_.refs_9_ = bf16[1552,256]{1,0:T(8,128)(2,1)S(1)} collective-permute-done((bf16[1552,256]{1,0:T(8,128)(2,1)S(1)}, bf16[1552,256]{1,0:T(8,128)(2,1)S(1)}, u32[]{:S(2)}, u32[]{:S(2)}) %collective-permute-start.8) | collective-permute-done | bytes 794656 | tf_op jit(solution)/shard_map/ppermute | solution.py:435
  54.4 0.0 collective-permute-done.9.refs_5_.refs_11_
  54.4 0.7 collective-permute-start.10
  55.1 0.4 collective-permute-start.11
  55.5 7.4 %collective-permute-done.3.refs_8_.refs_10_ = bf16[1552,256]{1,0:T(8,128)(2,1)S(1)} collective-permute-done((bf16[1552,256]{1,0:T(8,128)(2,1)S(1)}, bf16[1552,256]{1,0:T(8,128)(2,1)S(1)}, u32[]{:S(2)}, u32[]{:S(2)}) %collective-permute-start.3) | collective-permute-done | bytes 794656 | tf_op jit(solution)/shard_map/ppermute | solution.py:435
  62.9 0.0 collective-permute-done.4.refs_6_.refs_12_
  63.0 0.7 collective-permute-start.5
  63.7 0.4 collective-permute-start.12
  64.1 0.0 collective-permute-done.10.refs_17_.value_ref.refs_3_
  64.1 7.7 %collective-permute-start.13 = (bf16[1552,256]{1,0:T(8,128)(2,1)S(1)}, bf16[1552,256]{1,0:T(8,128)(2,1)S(1)}, u32[]{:S(2)}, u32[]{:S(2)}) collective-permute-start(bf16[1552,256]{1,0:T(8,128)(2,1)S(1)} %collective-permute-done.10.refs_17_.value_ref.refs_3_), channel_id=1, source_target_pairs={{0,1},{1,0},{2,3},{3,2},{4,5},{5,4},{6,7},{7,6},{8,9},{9,8},{10,11... | collective-permute-start | bytes 2383880 | tf_op jit(solution)/shard_map/ppermute | solution.py:435
  71.7 0.0 collective-permute-start.14
  71.7 0.0 collective-permute-done.11.refs_3_.refs_13_
  71.7 0.5 collective-permute-start.15
  72.2 0.0 collective-permute-done.12.refs_4_.refs_14_
  72.2 4.6 %shard_map.70 = (bf16[8,512,256]{2,1,0:T(8,128)(2,1)S(1)}, f32[512,128]{1,0:T(8,128)S(1)}, bf16[16,256]{1,0:T(8,128)(2,1)S(1)}) custom-call(bf16[8,512,256]{2,1,0:T(8,128)(2,1)S(1)} %get-tuple-element.33.refs_0_, bf16[1552,256]{1,0:T(8,128)(2,1)S(1)} %collective-permute-done.7.refs_1_.refs_15_, ...), custom_call_target="tpu_custom_call" | custom-call | flops 1 | bytes 1 | tf_op jit(solution)/shard_map/pallas_call | solution.py:270
  76.9 0.0 collective-permute-done.5.refs_5_
  76.9 0.0 collective-permute-done.13.refs_6_
  76.9 3.4 %collective-permute-start.16 = (bf16[1552,256]{1,0:T(8,128)(2,1)S(1)}, bf16[1552,256]{1,0:T(8,128)(2,1)S(1)}, u32[]{:S(2)}, u32[]{:S(2)}) collective-permute-start(bf16[1552,256]{1,0:T(8,128)(2,1)S(1)} %collective-permute-done.5.refs_5_), channel_id=1, source_target_pairs={{0,1},{1,0},{2,3},{3,2},{4,5},{5,4},{6,7},{7,6},{8,9},{9,8},{10,11... | collective-permute-start | bytes 2383880 | tf_op jit(solution)/shard_map/ppermute | solution.py:435
  80.2 0.0 collective-permute-done.14.refs_4_
  80.2 0.0 collective-permute-done.15.refs_5_
  80.2 2.7 %shard_map.72 = (f32[8,512,256]{2,1,0:T(8,128)S(1)}, f32[512,128]{1,0:T(8,128)S(1)}) custom-call(bf16[8,512,256]{2,1,0:T(8,128)(2,1)S(1)} %get-tuple-element.42.refs_0_, f32[512,128]{1,0:T(8,128)S(1)} %get-tuple-element.43.refs_1_, bf16[16,256]{1,0:T(8,128)(2,1)S(1)} %get-tuple-element.44.refs_2_.refs_4_, ...), custom_call_target="tpu_custom_call" | custom-call | flops 1610612736 | bytes 7340032 | tf_op jit(solution)/shard_map/pallas_call | solution.py:336
  82.9 0.0 collective-permute-done.16.refs_6_
  82.9 2.5 %shard_map.73 = (bf16[1,512,2048]{2,1,0:T(8,128)(2,1)}, bf16[1,512]{1,0:T(2,128)(2,1)}) custom-call(bf16[8,512,256]{2,1,0:T(8,128)(2,1)S(1)} %get-tuple-element.42.refs_0_, f32[8,512,256]{2,1,0:T(8,128)S(1)} %get-tuple-element.47.refs_1_, f32[512,128]{1,0:T(8,128)S(1)} %get-tuple-element.48.refs_2_, f32[1,512]{1,0:T(1,128)S(1)} %get-tuple-element.49.refs_3_, ...), custom_call_target="tpu_custom_call" | custom-call | flops 402653184 | bytes 7340032 | tf_op jit(solution)/shard_map/pallas_call | solution.py:405
  (1 shorter events, 0.0 us)
Async XLA Ops:
  2.9 8.2 %collective-permute-start = (bf16[1552,256]{1,0:T(8,128)(2,1)}, bf16[1552,256]{1,0:T(8,128)(2,1)S(1)}, u32[]{:S(2)}, u32[]{:S(2)}) collective-permute-start(bf16[1552,256]{1,0:T(8,128)(2,1)} %shard_map.68.own_ref), channel_id=1, source_target_pairs={{0,1},{1,0},{2,3},{3,2},{4,5},{5,4},{6,7},{7,6},{8,9},{9,8},{10,11... | collective-permute-start | bytes 2383880 | tf_op jit(solution)/shard_map/ppermute | solution.py:435
  3.7 16.8 %collective-permute-start.6 = (bf16[1552,256]{1,0:T(8,128)(2,1)}, bf16[1552,256]{1,0:T(8,128)(2,1)S(1)}, u32[]{:S(2)}, u32[]{:S(2)}) collective-permute-start(bf16[1552,256]{1,0:T(8,128)(2,1)} %shard_map.68.own_ref), channel_id=1, source_target_pairs={{0,0},{245,1},{2,2},{247,3},{4,4},{249,5},{6,6},{251,7},{8,8},{253... | collective-permute-start | bytes 2383880 | tf_op jit(solution)/shard_map/ppermute | solution.py:435
  11.2 17.7 %collective-permute-start.1 = (bf16[1552,256]{1,0:T(8,128)(2,1)S(1)}, bf16[1552,256]{1,0:T(8,128)(2,1)S(1)}, u32[]{:S(2)}, u32[]{:S(2)}) collective-permute-start(bf16[1552,256]{1,0:T(8,128)(2,1)S(1)} %collective-permute-done), channel_id=1, source_target_pairs={{0,0},{245,1},{2,2},{247,3},{4,4},{249,5},{6,6},{251,7},{8,8},{253... | collective-permute-start | bytes 2383880 | tf_op jit(solution)/shard_map/ppermute | solution.py:435
  20.5 16.9 %collective-permute-start.7 = (bf16[1552,256]{1,0:T(8,128)(2,1)S(1)}, bf16[1552,256]{1,0:T(8,128)(2,1)S(1)}, u32[]{:S(2)}, u32[]{:S(2)}) collective-permute-start(bf16[1552,256]{1,0:T(8,128)(2,1)S(1)} %collective-permute-done.6.refs_18_.refs_7_), channel_id=1, source_target_pairs={{14,0},{5,1},{12,2},{7,3},{0,4},{9,5},{2,6},{11,7},{4,8},{13,9},{6... | collective-permute-start | bytes 2383880 | tf_op jit(solution)/shard_map/ppermute | solution.py:435
  28.9 17.0 %collective-permute-start.2 = (bf16[1552,256]{1,0:T(8,128)(2,1)S(1)}, bf16[1552,256]{1,0:T(8,128)(2,1)S(1)}, u32[]{:S(2)}, u32[]{:S(2)}) collective-permute-start(bf16[1552,256]{1,0:T(8,128)(2,1)S(1)} %collective-permute-done.1.refs_8_), channel_id=1, source_target_pairs={{14,0},{5,1},{12,2},{7,3},{0,4},{9,5},{2,6},{11,7},{4,8},{13,9},{6... | collective-permute-start | bytes 2383880 | tf_op jit(solution)/shard_map/ppermute | solution.py:435
  37.4 17.0 %collective-permute-start.8 = (bf16[1552,256]{1,0:T(8,128)(2,1)S(1)}, bf16[1552,256]{1,0:T(8,128)(2,1)S(1)}, u32[]{:S(2)}, u32[]{:S(2)}) collective-permute-start(bf16[1552,256]{1,0:T(8,128)(2,1)S(1)} %collective-permute-done.7.refs_1_.refs_15_), channel_id=1, source_target_pairs={{254,0},{5,1},{252,2},{7,3},{0,4},{9,5},{2,6},{11,7},{4,8},{13,9},... | collective-permute-start | bytes 2383880 | tf_op jit(solution)/shard_map/ppermute | solution.py:435
  43.5 10.9 %collective-permute-start.9 = (bf16[1552,256]{1,0:T(8,128)(2,1)S(1)}, bf16[1552,256]{1,0:T(8,128)(2,1)S(1)}, u32[]{:S(2)}, u32[]{:S(2)}) collective-permute-start(bf16[1552,256]{1,0:T(8,128)(2,1)S(1)} %collective-permute-done.7.refs_1_.refs_15_), channel_id=1, source_target_pairs={{0,1},{1,0},{2,3},{3,2},{4,5},{5,4},{6,7},{7,6},{8,9},{9,8},{10,11... | collective-permute-start | bytes 2383880 | tf_op jit(solution)/shard_map/ppermute | solution.py:435
  43.5 1.1 %copy-start = (bf16[1552,256]{1,0:T(8,128)(2,1)S(1)}, bf16[1552,256]{1,0:T(8,128)(2,1)}, u32[]{:S(2)}) copy-start(bf16[1552,256]{1,0:T(8,128)(2,1)} %shard_map.68.own_ref) | copy-start | bytes 2383876
  45.9 17.0 %collective-permute-start.3 = (bf16[1552,256]{1,0:T(8,128)(2,1)S(1)}, bf16[1552,256]{1,0:T(8,128)(2,1)S(1)}, u32[]{:S(2)}, u32[]{:S(2)}) collective-permute-start(bf16[1552,256]{1,0:T(8,128)(2,1)S(1)} %collective-permute-done.2.refs_2_.refs_16_), channel_id=1, source_target_pairs={{254,0},{5,1},{252,2},{7,3},{0,4},{9,5},{2,6},{11,7},{4,8},{13,9},... | collective-permute-start | bytes 2383880 | tf_op jit(solution)/shard_map/ppermute | solution.py:435
  52.0 10.9 %collective-permute-start.4 = (bf16[1552,256]{1,0:T(8,128)(2,1)S(1)}, bf16[1552,256]{1,0:T(8,128)(2,1)S(1)}, u32[]{:S(2)}, u32[]{:S(2)}) collective-permute-start(bf16[1552,256]{1,0:T(8,128)(2,1)S(1)} %collective-permute-done.2.refs_2_.refs_16_), channel_id=1, source_target_pairs={{0,1},{1,0},{2,3},{3,2},{4,5},{5,4},{6,7},{7,6},{8,9},{9,8},{10,11... | collective-permute-start | bytes 2383880 | tf_op jit(solution)/shard_map/ppermute | solution.py:435
  54.4 9.6 %collective-permute-start.10 = (bf16[1552,256]{1,0:T(8,128)(2,1)S(1)}, bf16[1552,256]{1,0:T(8,128)(2,1)S(1)}, u32[]{:S(2)}, u32[]{:S(2)}) collective-permute-start(bf16[1552,256]{1,0:T(8,128)(2,1)S(1)} %collective-permute-done.8.refs_7_.refs_9_), channel_id=1, source_target_pairs={{1,1},{3,3},{0,4},{5,5},{2,6},{7,7},{4,8},{9,9},{6,10},{11,11},{8,... | collective-permute-start | bytes 2383880 | tf_op jit(solution)/shard_map/ppermute | solution.py:435
  55.1 16.6 %collective-permute-start.11 = (bf16[1552,256]{1,0:T(8,128)(2,1)S(1)}, bf16[1552,256]{1,0:T(8,128)(2,1)S(1)}, u32[]{:S(2)}, u32[]{:S(2)}) collective-permute-start(bf16[1552,256]{1,0:T(8,128)(2,1)S(1)} %collective-permute-done.8.refs_7_.refs_9_), channel_id=1, source_target_pairs={{0,1},{1,0},{2,3},{3,2},{4,5},{5,4},{6,7},{7,6},{8,9},{9,8},{10,11... | collective-permute-start | bytes 2383880 | tf_op jit(solution)/shard_map/ppermute | solution.py:435
  63.0 13.9 %collective-permute-start.5 = (bf16[1552,256]{1,0:T(8,128)(2,1)S(1)}, bf16[1552,256]{1,0:T(8,128)(2,1)S(1)}, u32[]{:S(2)}, u32[]{:S(2)}) collective-permute-start(bf16[1552,256]{1,0:T(8,128)(2,1)S(1)} %collective-permute-done.3.refs_8_.refs_10_), channel_id=1, source_target_pairs={{1,1},{3,3},{0,4},{5,5},{2,6},{7,7},{4,8},{9,9},{6,10},{11,11},{8,... | collective-permute-start | bytes 2383880 | tf_op jit(solution)/shard_map/ppermute | solution.py:435
  63.7 8.6 %collective-permute-start.12 = (bf16[1552,256]{1,0:T(8,128)(2,1)S(1)}, bf16[1552,256]{1,0:T(8,128)(2,1)S(1)}, u32[]{:S(2)}, u32[]{:S(2)}) collective-permute-start(bf16[1552,256]{1,0:T(8,128)(2,1)S(1)} %collective-permute-done.3.refs_8_.refs_10_), channel_id=1, source_target_pairs={{0,1},{1,0},{2,3},{3,2},{4,5},{5,4},{6,7},{7,6},{8,9},{9,8},{10,11... | collective-permute-start | bytes 2383880 | tf_op jit(solution)/shard_map/ppermute | solution.py:435
  64.1 12.8 %collective-permute-start.13 = (bf16[1552,256]{1,0:T(8,128)(2,1)S(1)}, bf16[1552,256]{1,0:T(8,128)(2,1)S(1)}, u32[]{:S(2)}, u32[]{:S(2)}) collective-permute-start(bf16[1552,256]{1,0:T(8,128)(2,1)S(1)} %collective-permute-done.10.refs_17_.value_ref.refs_3_), channel_id=1, source_target_pairs={{0,1},{1,0},{2,3},{3,2},{4,5},{5,4},{6,7},{7,6},{8,9},{9,8},{10,11... | collective-permute-start | bytes 2383880 | tf_op jit(solution)/shard_map/ppermute | solution.py:435
  71.7 8.5 %collective-permute-start.14 = (bf16[1552,256]{1,0:T(8,128)(2,1)S(1)}, bf16[1552,256]{1,0:T(8,128)(2,1)S(1)}, u32[]{:S(2)}, u32[]{:S(2)}) collective-permute-start(bf16[1552,256]{1,0:T(8,128)(2,1)S(1)} %collective-permute-done.6.refs_18_.refs_7_), channel_id=1, source_target_pairs={{0,1},{1,0},{2,3},{3,2},{4,5},{5,4},{6,7},{7,6},{8,9},{9,8},{10,11... | collective-permute-start | bytes 2383880 | tf_op jit(solution)/shard_map/ppermute | solution.py:435
  71.7 8.5 %collective-permute-start.15 = (bf16[1552,256]{1,0:T(8,128)(2,1)S(1)}, bf16[1552,256]{1,0:T(8,128)(2,1)S(1)}, u32[]{:S(2)}, u32[]{:S(2)}) collective-permute-start(bf16[1552,256]{1,0:T(8,128)(2,1)S(1)} %collective-permute-done.1.refs_8_), channel_id=1, source_target_pairs={{0,1},{1,0},{2,3},{3,2},{4,5},{5,4},{6,7},{7,6},{8,9},{9,8},{10,11... | collective-permute-start | bytes 2383880 | tf_op jit(solution)/shard_map/ppermute | solution.py:435
  76.9 6.0 %collective-permute-start.16 = (bf16[1552,256]{1,0:T(8,128)(2,1)S(1)}, bf16[1552,256]{1,0:T(8,128)(2,1)S(1)}, u32[]{:S(2)}, u32[]{:S(2)}) collective-permute-start(bf16[1552,256]{1,0:T(8,128)(2,1)S(1)} %collective-permute-done.5.refs_5_), channel_id=1, source_target_pairs={{0,1},{1,0},{2,3},{3,2},{4,5},{5,4},{6,7},{7,6},{8,9},{9,8},{10,11... | collective-permute-start | bytes 2383880 | tf_op jit(solution)/shard_map/ppermute | solution.py:435
